TPU v7x, 512 devices: a whole 4x4x16 slice. The times are simulated.
512 devices in a mesh: role: 2 (over y_lo), seq: 32 (over z, y_hi), mp: 8 (over x, core).
Axes of the slice: x: 4, y: 4 (y_hi: 2, y_lo: 2; y = y_hi * 2 + y_lo), z: 16, core: 2. Of those that a mesh axis runs over, the one named last changes fastest.
Arguments:
- gen_hidden: bfloat16 [4096, 3072], P('seq'), may hold values from -6 to 6
- w_gen: bfloat16 [3072, 64], replicated, may hold values from -0.109375 to 0.109375
- noise_latent: bfloat16 [4096, 64], P('seq'), may hold values from -20 to 20, as said below
- level_index: int32 [1], replicated, may hold values from 0 to 999
- w_embed: bfloat16 [2, 64, 3072], P('role'), may hold values from -0.75 to 0.75
- modulation: float32 [2, 3, 3072], P('role'), may hold values from -3 to 3
- w_qkv: bfloat16 [2, 3072, 3, 3072], P('role', 'seq', None, 'mp'), may hold values from -0.109375 to 0.109375
- qk_gain: float32 [2, 2, 128], P('role'), may hold values from 1.6 to 4
- text_kv: bfloat16 [2, 512, 2, 3072], P('role', 'seq', None, 'mp'), may hold values from -305 to 305, as said below
- w_out: bfloat16 [2, 3072, 3072], P('role', 'mp'), may hold values from -0.109375 to 0.109375
- w_final: bfloat16 [2, 3072, 64], P('role'), may hold values from -0.109375 to 0.109375
Outputs:
- grad_x: float32 [4096, 64], P('seq', 'role')
- grad_hidden: bfloat16 [4096, 3072], P('seq', 'role')
- grad_wgen: float32 [3072, 64], P('mp', 'role')
Inputs may be any that keep to these rules, and one draw needn't show every extreme that they name: `text_kv`: keys and values of the text stream, already projected and normalized. `noise_latent`: noise whose spread differs from row to row.
All inputs are finite; a program needn't handle non-finite values. Where the computation divides by a largest or mean magnitude, that divisor is 1e-20 or more.
Results may differ from a plain program's by a relative error of at most 0.027.
Values may be sent and summed in bfloat16 or wider, within the bound.
No kernel may reach another device: no remote copies, remote signals or barrier semaphores. Data moves between devices by JAX's collectives and lax.ppermute only.
A program may use at most 64 MiB of HBM per device.

v0:
```python
import jax
import jax.numpy as jnp
from jax import lax
from jax.sharding import PartitionSpec as P

LEVELS = 1000


def from_partner(array, axis, stride):
    return lax.ppermute(array, axis, [(i, i ^ 1 << stride) for i in range(lax.axis_size(axis))])


def layer_rows(values):
    row_mean = jnp.mean(values, axis=-1, keepdims=True)
    row_var = jnp.mean(jnp.square(values - row_mean), axis=-1, keepdims=True)
    return (values - row_mean) * lax.rsqrt(row_var + 1e-06)


def head_norm(values, gains):
    return values * lax.rsqrt(jnp.mean(values * values, axis=-1, keepdims=True) + 1e-06) * gains


def on_device(
    gen_hidden,
    w_gen,
    noise_latent,
    level_index,
    w_embed,
    modulation,
    w_qkv,
    qk_gain,
    text_kv,
    w_out,
    w_final,
):
    x_gen = jnp.dot(gen_hidden, w_gen, preferred_element_type=jnp.float32)
    time_frac = (level_index[0].astype(jnp.float32) + 1.0) / (LEVELS + 1.0)
    noise_scale = 3.0 * time_frac / (1.0 + 2.0 * time_frac)
    noised = ((1.0 - noise_scale) * x_gen + noise_scale * noise_latent.astype(jnp.float32)).astype(
        jnp.bfloat16
    )
    modulate = modulation[0]
    h_start = jnp.dot(noised, w_embed[0], preferred_element_type=jnp.float32)
    normed = (layer_rows(h_start) * (1.0 + modulate[1]) + modulate[0]).astype(jnp.bfloat16)
    rows_here = normed.shape[0]
    proj_width = w_qkv.shape[2] * w_qkv.shape[3]
    weight_rows = lax.all_gather(w_qkv[0], "seq", axis=0, tiled=True)
    projected = jnp.dot(
        normed,
        weight_rows.reshape(weight_rows.shape[0], proj_width),
        preferred_element_type=jnp.float32,
    )
    head_dim = qk_gain.shape[2]
    heads_here = w_qkv.shape[3] // head_dim
    projected = projected.reshape(rows_here, 3, heads_here, head_dim)
    queries = head_norm(projected[:, 0], qk_gain[0, 0]).astype(jnp.bfloat16)
    own_keys = head_norm(projected[:, 1], qk_gain[0, 1]).astype(jnp.bfloat16)
    own_values = projected[:, 2].astype(jnp.bfloat16)
    text_rows = text_kv.shape[1]
    key_block = jnp.concatenate(
        [text_kv[0, :, 0].reshape(text_rows, heads_here, head_dim), own_keys], axis=0
    )
    value_block = jnp.concatenate(
        [text_kv[0, :, 1].reshape(text_rows, heads_here, head_dim), own_values], axis=0
    )
    score_scale = head_dim ** (-0.5)
    row_max = jnp.full((rows_here, heads_here), -1e30, jnp.float32)
    key_piece = lax.all_gather(key_block, "seq", axis=0, tiled=True)
    value_piece = lax.all_gather(value_block, "seq", axis=0, tiled=True)
    scores = (
        jnp.einsum("qhd,khd->qhk", queries, key_piece, preferred_element_type=jnp.float32)
        * score_scale
    )
    new_max = jnp.maximum(row_max, jnp.max(scores, axis=-1))
    probs = jnp.exp(scores - new_max[..., None])
    row_sums = jnp.sum(probs, axis=-1)
    accum = jnp.einsum(
        "qhk,khd->qhd", probs.astype(jnp.bfloat16), value_piece, preferred_element_type=jnp.float32
    )
    row_max, row_sums, accum = (new_max, row_sums, accum)
    attended = (
        (accum / row_sums[..., None]).astype(jnp.bfloat16).reshape(rows_here, heads_here * head_dim)
    )
    partial_value = jnp.dot(attended, w_out[0], preferred_element_type=jnp.float32)
    gate_row = modulate[2]
    whole_sum = lax.psum(partial_value.astype(jnp.bfloat16), "mp").astype(jnp.float32)
    h_after = h_start + gate_row * whole_sum
    velocity = jnp.dot(
        layer_rows(h_after).astype(jnp.bfloat16), w_final[0], preferred_element_type=jnp.float32
    )
    partner = from_partner(velocity.astype(jnp.bfloat16), "role", 0).astype(velocity.dtype)
    role_here = lax.axis_index("role")
    is_teacher = role_here == 0
    teacher = jnp.where(is_teacher, velocity, partner)
    student = jnp.where(is_teacher, partner, velocity)
    pred_real = noised.astype(jnp.float32) - noise_scale * teacher
    spread_total = lax.psum(jnp.sum(jnp.abs(x_gen - pred_real)), "seq")
    entry_count = x_gen.shape[0] * x_gen.shape[1] * lax.axis_size("seq")
    spread_weight = spread_total / entry_count + 1e-06
    grad_x = noise_scale * (teacher - student) / spread_weight
    grad_b = grad_x.astype(jnp.bfloat16)
    chan_half = grad_x.shape[1] // 2
    chan_start = role_here * chan_half
    grad_x_share = lax.dynamic_slice_in_dim(grad_x, chan_start, chan_half, 1)
    grad_b_share = lax.dynamic_slice_in_dim(grad_b, chan_start, chan_half, 1)
    feat_half = w_gen.shape[0] // 2
    gen_rows = lax.dynamic_slice_in_dim(w_gen, role_here * feat_half, feat_half, 0)
    grad_hidden = lax.dot_general(
        grad_b, gen_rows, (((1,), (1,)), ((), ())), preferred_element_type=jnp.float32
    ).astype(jnp.bfloat16)
    col_width = gen_hidden.shape[1] // lax.axis_size("mp")
    hidden_cols = lax.dynamic_slice_in_dim(
        gen_hidden, lax.axis_index("mp") * col_width, col_width, 1
    )
    partial_grad = lax.dot_general(
        hidden_cols, grad_b_share, (((0,), (0,)), ((), ())), preferred_element_type=jnp.float32
    )
    grad_wgen = lax.psum(partial_grad.astype(jnp.bfloat16), "seq").astype(jnp.float32)
    return (grad_x_share, grad_hidden, grad_wgen)


def solution(mesh):
    placed = (
        P("seq", None),
        P(),
        P("seq", None),
        P(),
        P("role", None, None),
        P("role", None, None),
        P("role", "seq", None, "mp"),
        P("role", None, None),
        P("role", "seq", None, "mp"),
        P("role", "mp", None),
        P("role", None, None),
    )
    return jax.shard_map(
        on_device,
        mesh=mesh,
        in_specs=placed,
        out_specs=(P("seq", "role"), P("seq", "role"), P("mp", "role")),
        check_vma=False,
    )
```

profile of v0, /device:TPU:8, one launch (start us, length us, event | category | flops | bytes accessed | tf_op | source)
XLA Modules:
  0.0 850.2 jit_solution(4951605218128898231)
XLA Ops:
  7.2 0.0 copy-start
  7.2 0.0 all-gather.9.cloned.1.call-start
  7.2 0.7 all-gather.9.cloned.1.call-update
  7.9 0.0 all-gather.7.cloned.1.call-start
  8.7 1.0 slice_reduce_fusion
  9.6 1.6 fusion.47
  11.3 0.0 copy-start.10
  11.3 0.0 copy-start.9
  11.3 1.2 fusion.44
  12.5 1.1 copy-done.2
  13.6 0.3 multiply_reduce_fusion.1
  14.0 184.8 %all-gather.9.cloned.1.call-done = bf16[1,3072,3,384]{3,1,2,0:T(8,128)(2,1)} async-done(((bf16[1,96,3,384]{3,1,2,0:T(8,128)(2,1)}), bf16[1,3072,3,384]{3,1,2,0:T(8,128)(2,1)}) %all-gather.9.cloned.1.call-update) | async-done | bytes 7077904 | tf_op jit(solution)/shard_map/all_gather | solution.py:47
  198.8 10.1 %copy.19 = bf16[1,3072,3,384]{1,3,2,0:T(8,128)(2,1)} copy(bf16[1,3072,3,384]{3,1,2,0:T(8,128)(2,1)} %all-gather.9.cloned.1.call-done) | data formatting | bytes 14155776 | tf_op jit(solution)/shard_map/all_gather | solution.py:47
  208.9 5.9 fusion.17
  214.7 0.2 multiply_reduce_fusion.2
  214.9 0.1 multiply_convert_fusion.3
  215.1 0.7 pad_maximum_fusion.1
  215.7 0.0 all-gather.7.cloned.1.call-update
  215.7 0.0 all-gather.5.cloned.1.call-start
  215.8 0.7 pad_maximum_fusion
  216.5 0.0 all-gather.5.cloned.1.call-update
  216.5 0.0 all-reduce.2.cloned.1.call-start
  216.6 154.1 %all-gather.7.cloned.1.call-done = bf16[4608,3,128]{2,0,1:T(8,128)(2,1)} async-done(((bf16[144,3,128]{2,0,1:T(8,128)(2,1)}), bf16[4608,3,128]{2,0,1:T(8,128)(2,1)}) %all-gather.7.cloned.1.call-update) | async-done | bytes 3538960 | tf_op jit(solution)/shard_map/all_gather | solution.py:68
  370.7 3.2 fusion.45
  373.9 2.9 copy-done.1
  376.7 0.9 fusion.1
  377.7 151.1 %all-gather.5.cloned.1.call-done = bf16[4608,3,128]{2,0,1:T(8,128)(2,1)} async-done(((bf16[144,3,128]{2,0,1:T(8,128)(2,1)}), bf16[4608,3,128]{2,0,1:T(8,128)(2,1)}) %all-gather.5.cloned.1.call-update) | async-done | bytes 3538960 | tf_op jit(solution)/shard_map/all_gather | solution.py:69
  528.8 5.9 fusion.13
  534.7 1.5 convolution_convert_fusion
  536.2 0.0 all-reduce.2.cloned.1.call-update
  536.3 72.9 %all-reduce.2.cloned.1.call-done = bf16[128,3072]{1,0:T(8,128)(2,1)} async-done(((bf16[128,3072]{1,0:T(8,128)(2,1)}), bf16[128,3072]{1,0:T(8,128)(2,1)}) %all-reduce.2.cloned.1.call-update) | async-done | bytes 786448 | tf_op jit(solution)/shard_map/psum | solution.py:86
  609.2 2.0 fusion.26
  611.2 0.0 copy-start.6
  611.2 0.0 copy-done.3
  611.3 0.2 copy-done.4
  611.5 0.4 multiply_reduce_fusion
  611.9 0.0 copy-start.5
  611.9 0.4 copy-done.6
  612.3 0.5 fusion.46
  612.8 2.5 collective-permute-start
  615.3 3.2 collective-permute-done
  618.4 0.6 abs_reduce_fusion
  619.1 78.2 %psum.22 = f32[]{:T(128)} all-reduce(f32[]{:T(128)} %abs_reduce_fusion), channel_id=1, replica_groups=mesh['role'=2,'seq'=32,'mp'=8] {'seq'}, use_global_device_ids=true, to_apply=%region_10.11 | all-reduce | flops 1 | bytes 8 | tf_op jit(solution)/shard_map/psum | solution.py:97
  697.9 1.0 convolution_convert_fusion.1
  699.0 1.0 convolution_convert_fusion.2
  700.0 142.5 %psum.23 = bf16[384,32]{0,1:T(8,128)(2,1)S(1)} all-reduce(bf16[384,32]{0,1:T(8,128)(2,1)S(1)} %convolution_convert_fusion.2), channel_id=1, replica_groups=mesh['role'=2,'seq'=32,'mp'=8] {'seq'}, use_global_device_ids=true, to_apply=%region_11.12 | all-reduce | flops 12288 | bytes 49152 | tf_op jit(solution)/shard_map/psum | solution.py:118
  842.4 0.6 convert_element_type.77
  843.1 0.6 constant_dynamic-slice_fusion
  (25 shorter events, 0.1 us)
Async XLA Ops:
  7.2 527.5 %copy-start = (bf16[1,384,3072]{2,1,0:T(8,128)(2,1)S(1)}, bf16[1,384,3072]{2,1,0:T(8,128)(2,1)}, u32[]{:S(2)}) copy-start(bf16[1,384,3072]{2,1,0:T(8,128)(2,1)} %param.20) | copy-start | bytes 7077892
  7.2 4.1 copy-start.7
  7.2 191.6 %all-gather.9.cloned.1.call-start = ((), (), s32[]{:S(2)}) async-start(), calls=%async_computation.3 | async-start | bytes 7299072 | tf_op jit(solution)/shard_map/all_gather | solution.py:47
  7.9 362.7 %all-gather.7.cloned.1.call-start = ((), (), s32[]{:S(2)}) async-start(), calls=%async_computation.1 | async-start | bytes 3649536 | tf_op jit(solution)/shard_map/all_gather | solution.py:68
  11.3 2.7 copy-start.10
  11.3 2.7 copy-start.9
  12.5 1.1 copy-start.2
  215.7 313.1 %all-gather.5.cloned.1.call-start = ((), (), s32[]{:S(2)}) async-start(), calls=%async_computation | async-start | bytes 3649536 | tf_op jit(solution)/shard_map/all_gather | solution.py:69
  216.5 392.6 %all-reduce.2.cloned.1.call-start = ((), (), s32[]{:S(2)}) async-start(), calls=%async_computation.2 | async-start | bytes 1572864 | tf_op jit(solution)/shard_map/psum | solution.py:86
  373.8 2.9 copy-start.1
  609.2 2.1 copy-start.3
  609.2 2.3 copy-start.4
  611.2 1.1 copy-start.6
  611.9 6.5 copy-start.8
  611.9 86.0 %copy-start.5 = (bf16[3072,64]{0,1:T(8,128)(2,1)S(1)}, bf16[3072,64]{0,1:T(8,128)(2,1)}, u32[]{:S(2)}) copy-start(bf16[3072,64]{0,1:T(8,128)(2,1)} %param.12) | copy-start | bytes 1179652
  612.8 5.6 collective-permute-start
Sparse Core Ops, SparseCore 0:
  11.1 187.6 all-gather.8
  215.9 154.7 all-gather.6
  374.2 154.5 all-gather.4
  536.4 72.7 all-reduce.1
where the time goes:
time: 851 us; the launch traced here: 850 us
  waiting for transfers between devices  567 us (67%)
  blocking collectives  221 us (26%)
  matrix products  21.8 us (3%)
  local copies, waits for them, and re-layouts  16.3 us (2%)
  between operations  15.4 us (2%)
    all_gather x1, waiting for transfers between devices, on_device(): weight_rows = lax.all_gather(w_qkv[0], 'seq', axis=0, tiled=True)  185 us
    all_gather x1, waiting for transfers between devices, on_device(): key_piece = lax.all_gather(key_block, 'seq', axis=0, tiled=True)  154 us
    all_gather x1, waiting for transfers between devices, on_device(): value_piece = lax.all_gather(value_block, 'seq', axis=0, tiled=True)  151 us
    psum x1, blocking collectives, on_device(): lax.psum(partial_grad.astype(jnp.bfloat16), 'seq').astype(jnp.float32)  142 us
    psum x1, blocking collectives, on_device(): spread_total = lax.psum(jnp.sum(jnp.abs(x_gen - pred_real)), 'seq')  78.2 us
    psum x1, waiting for transfers between devices, on_device(): lax.psum(partial_value.astype(jnp.bfloat16), 'mp').astype(jnp.float32)  72.9 us
  transfers between devices with their start and end apart: 5, of which 5 were waited for; matrix products, arithmetic and copies ran while one was open for 1% of the time, Pallas kernels for 0%

commit v1 on v0

v1 whole, which is shorter than its diff:
```python
import jax
import jax.numpy as jnp
from jax import lax
from jax.experimental import pallas as pl
from jax.experimental.pallas import tpu as pltpu
from jax.sharding import PartitionSpec as P

LEVELS = 1000
HD = 128
CHANS = 64
HALF = CHANS // 2
MROWS = 80
PIECE = 80
F32 = jnp.float32
BF16 = jnp.bfloat16
NN = (((1,), (0,)), ((), ()))
NT = (((1,), (1,)), ((), ()))


def dot(a, b, dims=NN):
    return lax.dot_general(a, b, dims, preferred_element_type=F32)


def call(body, out_shape, args, scratch=(), smem=0, limit=24):
    vmem = pl.BlockSpec(memory_space=pltpu.VMEM)
    scalars = pl.BlockSpec(memory_space=pltpu.SMEM)
    return pl.pallas_call(
        body,
        out_shape=out_shape,
        in_specs=[scalars if i < smem else vmem for i in range(len(args))],
        out_specs=jax.tree.map(lambda out: scalars if out.dtype == jnp.int32 else vmem, out_shape),
        scratch_shapes=list(scratch),
        compiler_params=pltpu.CompilerParams(vmem_limit_bytes=limit * 1024 * 1024),
    )(*args)


def noise_scale_of(level, shape):
    time_frac = (jnp.full(shape, level, jnp.int32).astype(F32) + 1.0) / (LEVELS + 1.0)
    return 3.0 * time_frac / (1.0 + 2.0 * time_frac)


def weight_body(idx_ref, embed_ref, mod_ref, qkv_ref, payload_ref, idx_out_ref, term_ref):
    width = embed_ref.shape[1]
    features = qkv_ref.shape[1]
    offset = idx_ref[0] * features
    start = pl.multiple_of(jnp.minimum((offset >> 7) << 7, width - 256), HD)
    mean = jnp.sum(embed_ref[...].astype(F32), axis=1, keepdims=True) / width
    window = embed_ref[:, pl.ds(start, 256)].astype(F32)
    scale = 1.0 + mod_ref[1, :, pl.ds(start, 256)]
    shift = mod_ref[0, :, pl.ds(start, 256)]
    rows = jnp.concatenate(
        [(window - mean) * scale, shift, jnp.zeros((MROWS - CHANS - 1, 256), F32)], axis=0
    )
    select = jnp.where(
        lax.broadcasted_iota(jnp.int32, (256, features), 0)
        == lax.broadcasted_iota(jnp.int32, (256, features), 1) + (offset - start),
        1.0,
        0.0,
    ).astype(BF16)
    high = rows.astype(BF16)
    low = dot((rows - high.astype(F32)).astype(BF16), select).astype(BF16)
    high = dot(high, select).astype(BF16)
    for part in range(3):
        term = dot(high, qkv_ref[part]) + dot(low, qkv_ref[part])
        for head in range(3):
            j = part * 3 + head
            block = term[:, head * HD : (head + 1) * HD]
            term_ref[j * CHANS : (j + 1) * CHANS, :] = block[0:CHANS, :]
            term_ref[9 * CHANS + j : 9 * CHANS + j + 1, :] = block[CHANS : CHANS + 1, :]
    term_ref[9 * CHANS + 9 :, :] = jnp.zeros((term_ref.shape[0] - 9 * CHANS - 9, HD), F32)
    for p in range(payload_ref.shape[0]):
        payload_ref[p] = term_ref[p * PIECE : (p + 1) * PIECE, :].astype(BF16)
    for i in range(idx_out_ref.shape[0]):
        idx_out_ref[i] = idx_ref[i]


def latent_body(
    idx_ref, hidden_ref, gen_t_ref, noise_t_ref, embed_ref, text_in_ref, noised_ref, gap_ref, send_ref
):
    x_t = dot(gen_t_ref[...], hidden_ref[...], NT)
    noise_scale = noise_scale_of(idx_ref[3], x_t.shape)
    noised_t = ((1.0 - noise_scale) * x_t + noise_scale * noise_t_ref[...].astype(F32)).astype(BF16)
    noised = noised_t.astype(F32).T
    noised_ref[...] = noised
    gap_ref[...] = (x_t - noised_t.astype(F32)).T
    h = dot(noised.astype(BF16), embed_ref[...])
    width = h.shape[1]
    row_mean = jnp.sum(h, axis=1, keepdims=True) / width
    row_var = jnp.sum(jnp.square(h - row_mean), axis=1, keepdims=True) / width
    send_ref[0:CHANS, :] = (noised * lax.rsqrt(row_var + 1e-06)).T.astype(BF16)
    for j in range(6):
        send_ref[CHANS + j * 16 : CHANS + (j + 1) * 16, :] = text_in_ref[:, j * HD : (j + 1) * HD]


def total_of(ref, rows):
    total = ref[0, 0:rows, :].astype(F32)
    for i in range(1, ref.shape[0]):
        total = total + ref[i, 0:rows, :].astype(F32)
    return total.astype(BF16)


def far_body(idx_ref, recv_ref, send_ref, out_ref):
    piece = total_of(recv_ref, PIECE)
    channels = send_ref[pl.ds(pl.multiple_of((idx_ref[1] & 1) * HALF, HALF), HALF), :]
    for i in range(out_ref.shape[0]):
        out_ref[i, 0:PIECE, :] = piece
        out_ref[i, PIECE : PIECE + HALF, :] = channels
        out_ref[i, PIECE + HALF :, :] = send_ref[CHANS:, :]


def spread_body(recv_ref, out_ref, text_ref):
    piece = total_of(recv_ref, PIECE)
    text = PIECE + HALF
    for i in range(out_ref.shape[0]):
        out_ref[i, 0:PIECE, :] = piece
        for g in range(recv_ref.shape[0]):
            out_ref[i, PIECE + g * HALF : PIECE + (g + 1) * HALF, :] = recv_ref[g, PIECE:text, :]
            text_ref[i, g * 96 : (g + 1) * 96, :] = recv_ref[g, text:, :]


def image_body(
    idx_ref, send_ref, recv_ref, other_ref, gain_ref, out_ref, lat_ref, s_ref, v_ref, m_ref, own_ref
):
    tokens = lat_ref.shape[1]
    chunk = 512
    n_chunks = tokens // chunk
    ones = jnp.where(lax.broadcasted_iota(jnp.int32, (MROWS - CHANS, HD), 0) == 0, 1.0, 0.0).astype(BF16)
    n_far = (recv_ref.shape[1] - PIECE) // HALF
    for i in range(tokens // HD):
        near, first = i // n_far, (i % n_far) * HALF
        at = slice(i * HD, (i + 1) * HD)
        lat_ref[0:HALF, at] = recv_ref[near, PIECE + first : PIECE + first + HALF, :]
        lat_ref[HALF:CHANS, at] = other_ref[near, first : first + HALF, :]
        lat_ref[CHANS:MROWS, at] = ones
    for i in range(recv_ref.shape[0]):
        m_ref[i * PIECE : (i + 1) * PIECE, :] = recv_ref[i, 0:PIECE, :].astype(F32)
    own_ref[...] = send_ref[0:CHANS, :].astype(F32)

    def reordered(ref, base):
        core = idx_ref[1] & 1
        return jnp.concatenate(
            [ref[pl.ds(pl.multiple_of(k * HALF + base, HALF), HALF), :] for k in (core, 1 - core)], axis=0
        )

    own = jnp.concatenate([reordered(own_ref, 0).astype(BF16), ones], axis=0)
    score_scale = HD ** (-0.5) * 1.4426950408889634
    biases = m_ref[9 * CHANS : 9 * CHANS + 16, :]

    def weight(j):
        block = reordered(m_ref, j * CHANS)
        pad = jnp.zeros((HD - CHANS - 1, HD), F32)
        return jnp.concatenate([block, biases[j : j + 1, :], pad], axis=0).T[:, 0:MROWS].astype(BF16)

    q_image, w_k, w_v = [], [], []
    for head in range(3):
        q_t = dot(weight(head), own)
        q_t = q_t * lax.rsqrt(jnp.mean(q_t * q_t, axis=0, keepdims=True) + 1e-06)
        q = q_t.T * (gain_ref[0:1, :] * score_scale)
        out_ref[head, 3] = q
        q_image.append((q * gain_ref[1:2, :]).astype(BF16))
        w_k.append(weight(3 + head))
        w_v.append(weight(6 + head))
    rows = q_image[0].shape[0]

    def score_step(c, tops):
        at = pl.ds(pl.multiple_of(c * chunk, chunk), chunk)
        lat = lat_ref[:, at]
        out = []
        for head in range(3):
            k_t = dot(w_k[head], lat)
            k_t = k_t * lax.rsqrt(jnp.mean(k_t * k_t, axis=0, keepdims=True) + 1e-06)
            v_ref[head, :, at] = dot(w_v[head], lat).astype(BF16)
            s = dot(q_image[head], k_t.astype(BF16))
            s_ref[head, :, at] = s
            top = tops[head]
            for j in range(chunk // HD):
                top = jnp.maximum(top, s[:, j * HD : (j + 1) * HD])
            out.append(top)
        return tuple(out)

    tops = lax.fori_loop(0, n_chunks, score_step, (jnp.full((rows, HD), -3e38, F32),) * 3)
    for head in range(3):
        out_ref[head, 0] = jnp.zeros((rows, HD), F32)
        out_ref[head, 1] = jnp.zeros((rows, HD), F32)
        out_ref[head, 2] = jnp.broadcast_to(jnp.max(tops[head], axis=1, keepdims=True), (rows, HD))

    def mix_step(c, carry):
        at = pl.ds(pl.multiple_of(c * chunk, chunk), chunk)
        for head in range(3):
            p = jnp.exp2(s_ref[head, :, at] - out_ref[head, 2][:, 0:1])
            total = out_ref[head, 1]
            for j in range(chunk // HD):
                total = total + p[:, j * HD : (j + 1) * HD]
            out_ref[head, 1] = total
            out_ref[head, 0] += dot(p.astype(BF16), v_ref[head, :, at], NT)
        return carry

    lax.fori_loop(0, n_chunks, mix_step, 0)


def text_body(image_ref, text_ref, out_w_ref, y_ref, att_ref):
    def block(first):
        return text_ref[:, first : first + 16, :].reshape(text_ref.shape[0] * 16, HD)

    for head in range(3):
        s = dot(image_ref[head, 3].astype(BF16), block(head * 16), NT)
        image_top = image_ref[head, 2]
        top = jnp.maximum(image_top, jnp.max(s, axis=1, keepdims=True))
        keep = jnp.exp2(image_top - top)
        p = jnp.exp2(s - top[:, 0:1])
        acc = image_ref[head, 0] * keep + dot(p.astype(BF16), block(48 + head * 16))
        total = jnp.sum(image_ref[head, 1] * keep, axis=1, keepdims=True) + jnp.sum(p, axis=1, keepdims=True)
        att_ref[:, head * HD : (head + 1) * HD] = (acc / total).astype(BF16)
    att = att_ref[...]
    step = 512
    for j in range(out_w_ref.shape[1] // step):
        y = dot(att, out_w_ref[:, j * step : (j + 1) * step]).astype(BF16)
        y_ref[:, :, j * step : (j + 1) * step] = y.reshape(y_ref.shape[0], y_ref.shape[1], step)


def velocity_body(idx_ref, parts_ref, noised_ref, embed_ref, mod_ref, final_t_ref, v_ref):
    total = parts_ref[0].astype(F32)
    for i in range(1, parts_ref.shape[0]):
        total = total + parts_ref[i].astype(F32)
    own_rows = total.shape[0]
    own = noised_ref[pl.ds(pl.multiple_of(idx_ref[1] * own_rows, own_rows), own_rows), :].astype(BF16)
    h = dot(own, embed_ref[...]) + mod_ref[2] * total
    width = h.shape[1]
    h = h - jnp.sum(h, axis=1, keepdims=True) / width
    var = jnp.sum(h * h, axis=1, keepdims=True) / width
    v = dot((h * lax.rsqrt(var + 1e-06)).astype(BF16), final_t_ref[...], NT)
    v = jnp.concatenate([v[0:8, :], v[8:16, :]], axis=1)
    for i in range(v_ref.shape[0]):
        v_ref[i] = v


def grad_body(idx_ref, both_ref, gap_ref, hidden_ref, gen_t_ref, piece_ref, share_ref, raw_ref, diff_ref, grad_ref):
    n_mp = both_ref.shape[0] // 2
    chans = gap_ref.shape[1]

    def rows(first):
        blocks = []
        for i in range(first, first + n_mp):
            blocks += [both_ref[i][:, 0:chans], both_ref[i][:, chans : 2 * chans]]
        return jnp.concatenate(blocks, axis=0)

    teacher, student = rows(0), rows(n_mp)
    spread = jnp.abs(gap_ref[...] + noise_scale_of(idx_ref[3], gap_ref.shape) * teacher)
    spread = jnp.sum(jnp.sum(spread, axis=1, keepdims=True), axis=0, keepdims=True)
    diff = teacher - student
    diff_ref[...] = diff.T
    half = chans // 2
    share = diff_ref[pl.ds(pl.multiple_of(idx_ref[2] * half, half), half), :]
    share_ref[...] = share
    cols = grad_ref.shape[1]
    hidden = hidden_ref[:, pl.ds(pl.multiple_of(idx_ref[1] * cols, HD), cols)]
    grad_ref[...] = dot(share.astype(BF16), hidden)
    for p in range(8):
        for g in range(3):
            piece_ref[p, 4 * g : 4 * g + 4, :] = grad_ref[4 * p : 4 * p + 4, g * HD : (g + 1) * HD]
        piece_ref[p, 12:16, :] = jnp.broadcast_to(spread, (4, HD))
    feats = raw_ref.shape[1]
    raw_ref[...] = dot(diff.astype(BF16), gen_t_ref[:, pl.ds(pl.multiple_of(idx_ref[2] * feats, HD), feats)])


def near_body(recv_ref, out_ref):
    total = recv_ref[0]
    for i in range(1, recv_ref.shape[0]):
        total = total + recv_ref[i]
    row = lax.broadcasted_iota(jnp.int32, total.shape, 0)
    high = total.astype(BF16).astype(F32)
    mid = (total - high).astype(BF16).astype(F32)
    low = total - high - mid
    out = jnp.where(row == 13, mid, jnp.where(row == 14, low, high)).astype(BF16)
    for i in range(out_ref.shape[0]):
        out_ref[i] = out


def last_body(idx_ref, recv_ref, share_ref, raw_ref, x_ref, hidden_ref, gen_ref, *, entries):
    totals = []
    for p in range(8):
        total = recv_ref[p].astype(F32)
        for g in range(1, recv_ref.shape[0] // 8):
            total = total + recv_ref[8 * g + p].astype(F32)
        totals.append(total)
    spread = totals[0][12:13, 0:1] + totals[0][13:14, 0:1] + totals[0][14:15, 0:1]
    factor = noise_scale_of(idx_ref[3], (1, 1)) / (spread / entries + 1e-06)
    x_ref[...] = share_ref[...] * factor
    hidden_ref[...] = (raw_ref[...] * factor).astype(BF16)
    for p in range(8):
        scaled = totals[p] * factor
        for g in range(3):
            gen_ref[4 * p : 4 * p + 4, g * HD : (g + 1) * HD] = scaled[4 * g : 4 * g + 4, :]


def exchange(array, axis, groups=None):
    return lax.all_to_all(array, axis, 0, 0, axis_index_groups=groups, tiled=True)


def on_device(
    gen_hidden, w_gen, noise_latent, level_index, w_embed, modulation, w_qkv, qk_gain, text_kv, w_out, w_final
):
    rows_here, width = gen_hidden.shape
    n_seq, n_mp = lax.axis_size("seq"), lax.axis_size("mp")
    chans = w_gen.shape[1]
    tokens = rows_here * n_seq
    sds = jax.ShapeDtypeStruct
    mods = jnp.transpose(modulation, (1, 0, 2))
    embed = w_embed[0]
    gen_t = w_gen.T
    idx = jnp.stack(
        [lax.axis_index("seq"), lax.axis_index("mp"), lax.axis_index("role"), level_index[0]]
    ).astype(jnp.int32)
    near_groups = [[8 * g + i for i in range(8)] for g in range(n_seq // 8)]
    far_groups = [[8 * g + i for g in range(n_seq // 8)] for i in range(8)]

    n_far = n_seq // 8
    payload, idx_late = call(
        weight_body,
        (sds((8, PIECE, HD), BF16), sds(idx.shape, jnp.int32)),
        (idx, embed, mods, jnp.transpose(w_qkv[0], (1, 0, 2))),
        scratch=(pltpu.VMEM((8 * PIECE, HD), F32),),
        smem=1,
        limit=60,
    )
    noised, gap, send = call(
        latent_body,
        (sds((rows_here, chans), F32), sds((rows_here, chans), F32), sds((chans + 96, HD), BF16)),
        (idx_late, gen_hidden, gen_t, noise_latent.T, embed, text_kv[0].reshape(text_kv.shape[1], 6 * HD)),
        smem=1,
        limit=60,
    )
    pieces = exchange(payload, "seq", near_groups)
    pieces = call(far_body, sds((n_far, PIECE + HALF + 96, HD), BF16), (idx, pieces, send), smem=1)
    pieces = exchange(pieces, "seq", far_groups)
    pieces, text = call(
        spread_body,
        (sds((8, PIECE + n_far * HALF, HD), BF16), sds((8, n_far * 96, HD), BF16)),
        (pieces,),
    )
    pieces = exchange(pieces, "seq", near_groups)
    text = exchange(text, "seq", near_groups).reshape(n_seq, 96, HD)
    other = lax.ppermute(pieces[:, PIECE:, :], "mp", [(i, i ^ 1) for i in range(n_mp)])

    image = call(
        image_body,
        sds((3, 4, rows_here, HD), F32),
        (idx, send, pieces, other, qk_gain[0]),
        scratch=(
            pltpu.VMEM((MROWS, tokens), BF16),
            pltpu.VMEM((3, rows_here, tokens), F32),
            pltpu.VMEM((3, HD, tokens), BF16),
            pltpu.VMEM((8 * PIECE, HD), F32),
            pltpu.VMEM((chans, HD), F32),
        ),
        smem=1,
    )
    own_rows = rows_here // n_mp
    y = call(
        text_body,
        sds((n_mp, own_rows, width), BF16),
        (image, text, w_out[0]),
        scratch=(pltpu.VMEM((rows_here, 3 * HD), BF16),),
    )
    parts = exchange(y, "mp")
    velocity = call(
        velocity_body,
        sds((2 * n_mp, 8, 2 * chans), F32),
        (idx, parts, noised, embed, mods, w_final[0].T),
        smem=1,
    )
    both = exchange(velocity, ("role", "mp"))
    half = chans // 2
    grad_piece, share, raw = call(
        grad_body,
        (sds((8, 16, HD), F32), sds((half, rows_here), F32), sds((rows_here, width // 2), F32)),
        (idx, both, gap, gen_hidden, gen_t),
        scratch=(pltpu.VMEM((chans, rows_here), F32), pltpu.VMEM((half, 3 * HD), F32)),
        smem=1,
    )
    near = exchange(grad_piece, "seq", near_groups)
    near = call(near_body, sds((n_seq, 16, HD), BF16), (near,))
    everything = exchange(near, "seq")

    def last(*refs):
        last_body(*refs, entries=tokens * chans)

    grad_x_t, grad_hidden, grad_gen_t = call(
        last,
        (sds((half, rows_here), F32), sds((rows_here, width // 2), BF16), sds((half, 3 * HD), F32)),
        (idx, everything, share, raw),
        smem=1,
    )
    return grad_x_t.T, grad_hidden, grad_gen_t.T


def solution(mesh):
    placed = (
        P("seq", None),
        P(),
        P("seq", None),
        P(),
        P("role", None, None),
        P("role", None, None),
        P("role", "seq", None, "mp"),
        P("role", None, None),
        P("role", "seq", None, "mp"),
        P("role", "mp", None),
        P("role", None, None),
    )
    return jax.shard_map(
        on_device,
        mesh=mesh,
        in_specs=placed,
        out_specs=(P("seq", "role"), P("seq", "role"), P("mp", "role")),
        check_vma=False,
    )
```

time: 851 us -> 160 us (0.19)
  the two profiles are of different devices: /device:TPU:8 before, /device:TPU:2 now
where the time goes in v1:
time: 160 us; the launch traced here: 159 us
  blocking collectives  109 us (68%)
  Pallas kernels  23 us (14%)
  starting transfers between devices  14 us (9%)
  waiting for transfers between devices  7.74 us (5%)
  local copies, waits for them, and re-layouts  3.85 us (2%)
    all_to_all x6, blocking collectives, exchange(): lax.all_to_all(array, axis, 0, 0, axis_index_groups=groups, tiled=True)  109 us
    pallas_call x10, Pallas kernels, call(): pl.pallas_call(body, out_shape=out_shape, in_specs=[scalars if i < smem e...  23 us
    all_to_all x2, starting transfers between devices, exchange(): lax.all_to_all(array, axis, 0, 0, axis_index_groups=groups, tiled=True)  12.1 us
    all_to_all x2, waiting for transfers between devices, exchange(): lax.all_to_all(array, axis, 0, 0, axis_index_groups=groups, tiled=True)  6.24 us
    unnamed x25, local copies, waits for them, and re-layouts  3.83 us
  transfers between devices with their start and end apart: 3, of which 3 were waited for; matrix products, arithmetic and copies ran while one was open for 1% of the time, Pallas kernels for 9%

profile of v1, /device:TPU:2, one launch (start us, length us, event | category | flops | bytes accessed | tf_op | source)
XLA Modules:
  0.0 159.2 jit_solution(9434352368273769761)
XLA Ops:
  1.3 0.7 pad_add_fusion.idx_ref.refs_0_
  1.9 0.0 copy-start.10
  1.9 2.3 %shard_map.130 = (bf16[8,80,128]{2,1,0:T(8,128)(2,1)}, s32[4]{0:T(128)}) custom-call(s32[4]{0:T(128)} %pad_add_fusion.idx_ref.refs_0_, bf16[64,3072]{1,0:T(8,128)(2,1)} %bitcast.21, f32[3,1,3072]{2,1,0:T(1,128)} %bitcast.29, bf16[3,96,384]{2,1,0:T(8,128)(2,1)} %bitcast.32), custom_call_target="tpu_custom_call" | custom-call | tf_op jit(solution)/shard_map/pallas_call | solution.py:27
  4.2 8.5 %all-to-all-start = ((bf16[8,80,128]{2,1,0:T(8,128)(2,1)}), bf16[8,80,128]{2,1,0:T(8,128)(2,1)S(1)}, u32[]{:S(2)}, u32[]{:S(2)}) async-start(bf16[8,80,128]{2,1,0:T(8,128)(2,1)} %get-tuple-element.18), calls=%async_computation | async-start | bytes 327680 | tf_op jit(solution)/shard_map/all_to_all | solution.py:297
  12.8 1.3 copy.14
  14.1 3.5 %shard_map.131 = (f32[128,64]{1,0:T(8,128)}, f32[128,64]{1,0:T(8,128)}, bf16[160,128]{1,0:T(8,128)(2,1)}) custom-call(s32[4]{0:T(128)} %get-tuple-element.16.idx_ref, bf16[128,3072]{1,0:T(8,128)(2,1)} %hidden_ref.3, bf16[64,3072]{1,0:T(8,128)(2,1)} %bitcast.26, bf16[64,128]{1,0:T(8,128)(2,1)} %bitcast.35, bf16[64,3072]{1,0:T(8,128)(2,1)} %bitcast.22, ...), custom_call_target="tpu_custom_call" | custom-call | tf_op jit(solution)/shard_map/pallas_call | solution.py:27
  17.6 0.0 copy-start.11
  17.6 4.2 %all-to-all-done.recv_ref = bf16[8,80,128]{2,1,0:T(8,128)(2,1)S(1)} async-done(((bf16[8,80,128]{2,1,0:T(8,128)(2,1)}), bf16[8,80,128]{2,1,0:T(8,128)(2,1)S(1)}, u32[]{:S(2)}, u32[]{:S(2)}) %all-to-all-start) | async-done | bytes 163872 | tf_op jit(solution)/shard_map/all_to_all | solution.py:297
  21.8 0.0 copy-done.10
  21.8 0.0 copy-start.5
  21.8 0.8 copy-done.5
  22.6 0.0 copy-start.6
  22.6 0.6 shard_map.132
  23.2 28.5 %all_to_all.40.recv_ref = bf16[4,208,128]{2,1,0:T(8,128)(2,1)S(1)} all-to-all(bf16[4,208,128]{2,1,0:T(8,128)(2,1)S(1)} %shard_map.132), channel_id=1, replica_groups={{0,64,128,192},{8,72,136,200},{16,80,144,208},{24,88,152,216},{32,96,16..., dimensions={0} | all-to-all | bytes 425984 | tf_op jit(solution)/shard_map/all_to_all | solution.py:297
  51.7 1.0 shard_map.133
  52.7 16.5 %all_to_all.41.recv_ref = bf16[8,208,128]{2,1,0:T(8,128)(2,1)S(1)} all-to-all(bf16[8,208,128]{2,1,0:T(8,128)(2,1)S(1)} %get-tuple-element.19), channel_id=1, replica_groups={{0,8,16,24,32,40,48,56},{64,72,80,88,96,104,112,120},{128,136,144,152,1..., dimensions={0} | all-to-all | bytes 851968 | tf_op jit(solution)/shard_map/all_to_all | solution.py:297
  69.1 3.5 %all-to-all-start.3 = ((bf16[8,384,128]{2,1,0:T(8,128)(2,1)}), bf16[8,384,128]{2,1,0:T(8,128)(2,1)S(1)}, u32[]{:S(2)}, u32[]{:S(2)}) async-start(bf16[8,384,128]{2,1,0:T(8,128)(2,1)} %get-tuple-element.20), calls=%async_computation.3 | async-start | bytes 1572864 | tf_op jit(solution)/shard_map/all_to_all | solution.py:297
  72.7 1.9 %collective-permute-start = (bf16[8,128,128]{2,1,0:T(8,128)(2,1)S(1)}, bf16[8,128,128]{2,1,0:T(8,128)(2,1)S(1)}, u32[]{:S(2)}, u32[]{:S(2)}) collective-permute-start(bf16[8,128,128]{2,1,0:T(8,128)(2,1)S(1)} %slice.4), channel_id=1, source_target_pairs={{0,1},{1,0},{2,3},{3,2},{4,5},{5,4},{6,7},{7,6},{8,9},{9,8},{10,11... | collective-permute-start | bytes 786440 | tf_op jit(solution)/shard_map/ppermute | solution.py:343
  74.6 1.5 collective-permute-done.other_ref
  76.1 0.0 copy-done.11
  76.2 0.0 copy-done.6
  76.2 10.4 %shard_map.134.image_ref = f32[3,4,128,128]{3,2,1,0:T(8,128)S(1)} custom-call(s32[4]{0:T(128)S(1)} %copy-done.10, bf16[160,128]{1,0:T(8,128)(2,1)S(1)} %copy-done.6, bf16[8,208,128]{2,1,0:T(8,128)(2,1)S(1)} %all_to_all.41.recv_ref, bf16[8,128,128]{2,1,0:T(8,128)(2,1)S(1)} %collective-permute-done.other_ref, f32[2,128]{1,0:T(2,128)S(1)} %bitcast.31), custom_call_target="tpu_custom_call" | custom-call | tf_op jit(solution)/shard_map/pallas_call | solution.py:27
  86.6 2.0 %all-to-all-done.3 = bf16[8,384,128]{2,1,0:T(8,128)(2,1)S(1)} async-done(((bf16[8,384,128]{2,1,0:T(8,128)(2,1)}), bf16[8,384,128]{2,1,0:T(8,128)(2,1)S(1)}, u32[]{:S(2)}, u32[]{:S(2)}) %all-to-all-start.3) | async-done | bytes 786464 | tf_op jit(solution)/shard_map/all_to_all | solution.py:297
  88.6 0.0 copy-start.2
  88.6 1.7 %copy-done.2 = bf16[1,384,3072]{2,1,0:T(8,128)(2,1)S(1)} copy-done((bf16[1,384,3072]{2,1,0:T(8,128)(2,1)S(1)}, bf16[1,384,3072]{2,1,0:T(8,128)(2,1)}, u32[]{:S(2)}) %copy-start.2) | copy-done | bytes 2359320
  90.3 0.0 copy-start
  90.3 0.0 copy-start.4
  90.3 0.0 copy-start.7
  90.3 0.0 copy-start.9
  90.3 1.7 %shard_map.135 = bf16[8,16,3072]{2,1,0:T(8,128)(2,1)S(1)} custom-call(f32[3,4,128,128]{3,2,1,0:T(8,128)S(1)} %shard_map.134.image_ref, bf16[32,96,128]{2,1,0:T(8,128)(2,1)S(1)} %bitcast.24, bf16[384,3072]{1,0:T(8,128)(2,1)S(1)} %bitcast.25), custom_call_target="tpu_custom_call" | custom-call | tf_op jit(solution)/shard_map/pallas_call | solution.py:27
  91.9 0.0 copy-start.1
  92.0 0.0 copy-start.3
  92.0 0.0 copy-start.8
  92.0 16.5 %all_to_all.42.parts_ref = bf16[8,16,3072]{2,1,0:T(8,128)(2,1)S(1)} all-to-all(bf16[8,16,3072]{2,1,0:T(8,128)(2,1)S(1)} %shard_map.135), channel_id=1, replica_groups=mesh['role'=2,'seq'=32,'mp'=8] {'mp'}, dimensions={0} | all-to-all | bytes 1572864 | tf_op jit(solution)/shard_map/all_to_all | solution.py:297
  108.5 0.0 copy-done
  108.5 0.0 copy-done.4
  108.5 0.0 copy-done.7
  108.5 0.0 copy-done.9
  108.5 1.2 shard_map.136
  109.7 13.5 %all_to_all.43.both_ref = f32[16,8,128]{2,1,0:T(8,128)S(1)} all-to-all(f32[16,8,128]{2,1,0:T(8,128)S(1)} %shard_map.136), channel_id=1, replica_groups=mesh['role'=2,'seq'=32,'mp'=8] {'role','mp'}, dimensions={0} | all-to-all | bytes 131072 | tf_op jit(solution)/shard_map/all_to_all | solution.py:297
  123.2 0.0 copy-done.1
  123.2 0.0 copy-done.3
  123.2 0.0 copy-done.8
  123.2 0.9 shard_map.137
  124.2 13.9 %all_to_all.44.recv_ref = f32[8,16,128]{2,1,0:T(8,128)S(1)} all-to-all(f32[8,16,128]{2,1,0:T(8,128)S(1)} %get-tuple-element.23), channel_id=1, replica_groups={{0,8,16,24,32,40,48,56},{64,72,80,88,96,104,112,120},{128,136,144,152,1..., dimensions={0} | all-to-all | bytes 131072 | tf_op jit(solution)/shard_map/all_to_all | solution.py:297
  138.1 19.7 %all_to_all.45.refs_1_ = bf16[32,16,128]{2,1,0:T(8,128)(2,1)S(1)} all-to-all(bf16[32,16,128]{2,1,0:T(8,128)(2,1)S(1)} %shard_map.138), channel_id=1, replica_groups=mesh['role'=2,'seq'=32,'mp'=8] {'seq'}, dimensions={0} | all-to-all | bytes 262144 | tf_op jit(solution)/shard_map/all_to_all | solution.py:297
  157.8 1.4 shard_map.139
  (2 shorter events, 0.0 us)
Async XLA Ops:
  1.9 19.9 %copy-start.10 = (s32[4]{0:T(128)S(1)}, s32[4]{0:T(128)}, u32[]{:S(2)}) copy-start(s32[4]{0:T(128)} %pad_add_fusion.idx_ref.refs_0_) | copy-start | bytes 52
  4.2 17.6 %all-to-all-start = ((bf16[8,80,128]{2,1,0:T(8,128)(2,1)}), bf16[8,80,128]{2,1,0:T(8,128)(2,1)S(1)}, u32[]{:S(2)}, u32[]{:S(2)}) async-start(bf16[8,80,128]{2,1,0:T(8,128)(2,1)} %get-tuple-element.18), calls=%async_computation | async-start | bytes 327680 | tf_op jit(solution)/shard_map/all_to_all | solution.py:297
  17.6 58.6 %copy-start.11 = (f32[1,2,128]{2,1,0:T(2,128)S(1)}, f32[1,2,128]{2,1,0:T(2,128)}, u32[]{:S(2)}) copy-start(f32[1,2,128]{2,1,0:T(2,128)} %param.18) | copy-start | bytes 3076
  21.8 0.8 copy-start.5
  22.6 53.5 %copy-start.6 = (bf16[160,128]{1,0:T(8,128)(2,1)S(1)}, bf16[160,128]{1,0:T(8,128)(2,1)}, u32[]{:S(2)}) copy-start(bf16[160,128]{1,0:T(8,128)(2,1)} %get-tuple-element.17.send_ref) | copy-start | bytes 122884
  69.1 19.5 %all-to-all-start.3 = ((bf16[8,384,128]{2,1,0:T(8,128)(2,1)}), bf16[8,384,128]{2,1,0:T(8,128)(2,1)S(1)}, u32[]{:S(2)}, u32[]{:S(2)}) async-start(bf16[8,384,128]{2,1,0:T(8,128)(2,1)} %get-tuple-element.20), calls=%async_computation.3 | async-start | bytes 1572864 | tf_op jit(solution)/shard_map/all_to_all | solution.py:297
  72.7 3.4 %collective-permute-start = (bf16[8,128,128]{2,1,0:T(8,128)(2,1)S(1)}, bf16[8,128,128]{2,1,0:T(8,128)(2,1)S(1)}, u32[]{:S(2)}, u32[]{:S(2)}) collective-permute-start(bf16[8,128,128]{2,1,0:T(8,128)(2,1)S(1)} %slice.4), channel_id=1, source_target_pairs={{0,1},{1,0},{2,3},{3,2},{4,5},{5,4},{6,7},{7,6},{8,9},{9,8},{10,11... | collective-permute-start | bytes 786440 | tf_op jit(solution)/shard_map/ppermute | solution.py:343
  88.6 1.7 %copy-start.2 = (bf16[1,384,3072]{2,1,0:T(8,128)(2,1)S(1)}, bf16[1,384,3072]{2,1,0:T(8,128)(2,1)}, u32[]{:S(2)}) copy-start(bf16[1,384,3072]{2,1,0:T(8,128)(2,1)} %param.20) | copy-start | bytes 7077892
  90.3 18.3 %copy-start = (bf16[1,64,3072]{2,1,0:T(8,128)(2,1)S(1)}, bf16[1,64,3072]{2,1,0:T(8,128)(2,1)}, u32[]{:S(2)}) copy-start(bf16[1,64,3072]{2,1,0:T(8,128)(2,1)} %param.15) | copy-start | bytes 1179652
  90.3 18.3 %copy-start.4 = (bf16[1,3072,64]{1,2,0:T(8,128)(2,1)S(1)}, bf16[1,3072,64]{1,2,0:T(8,128)(2,1)}, u32[]{:S(2)}) copy-start(bf16[1,3072,64]{1,2,0:T(8,128)(2,1)} %param.21) | copy-start | bytes 1179652
  90.3 18.3 %copy-start.7 = (f32[1,3,3072]{2,0,1:T(1,128)S(1)}, f32[1,3,3072]{2,0,1:T(1,128)}, u32[]{:S(2)}) copy-start(f32[1,3,3072]{2,0,1:T(1,128)} %param.16) | copy-start | bytes 110596
  90.3 18.3 %copy-start.9 = (f32[128,64]{1,0:T(8,128)S(1)}, f32[128,64]{1,0:T(8,128)}, u32[]{:S(2)}) copy-start(f32[128,64]{1,0:T(8,128)} %get-tuple-element.21.noised_ref) | copy-start | bytes 98308
  91.9 31.3 %copy-start.1 = (bf16[128,3072]{1,0:T(8,128)(2,1)S(1)}, bf16[128,3072]{1,0:T(8,128)(2,1)}, u32[]{:S(2)}) copy-start(bf16[128,3072]{1,0:T(8,128)(2,1)} %hidden_ref.3) | copy-start | bytes 2359300
  92.0 31.3 %copy-start.3 = (bf16[3072,64]{0,1:T(8,128)(2,1)S(1)}, bf16[3072,64]{0,1:T(8,128)(2,1)}, u32[]{:S(2)}) copy-start(bf16[3072,64]{0,1:T(8,128)(2,1)} %param.12) | copy-start | bytes 1179652
  92.0 31.3 %copy-start.8 = (f32[128,64]{1,0:T(8,128)S(1)}, f32[128,64]{1,0:T(8,128)}, u32[]{:S(2)}) copy-start(f32[128,64]{1,0:T(8,128)} %get-tuple-element.22.gap_ref) | copy-start | bytes 98308

commit v2 on v1

--- a/solution.py
+++ b/solution.py
@@ -7,6 +7,8 @@
 
 LEVELS = 1000
 HD = 128
+SEQ = ("z_far", "z_near", "y_hi")
+NEAR = ("z_near", "y_hi")
 CHANS = 64
 HALF = CHANS // 2
 MROWS = 80
@@ -88,8 +90,10 @@
     row_mean = jnp.sum(h, axis=1, keepdims=True) / width
     row_var = jnp.sum(jnp.square(h - row_mean), axis=1, keepdims=True) / width
     send_ref[0:CHANS, :] = (noised * lax.rsqrt(row_var + 1e-06)).T.astype(BF16)
+    text = text_in_ref[...].astype(F32)
     for j in range(6):
-        send_ref[CHANS + j * 16 : CHANS + (j + 1) * 16, :] = text_in_ref[:, j * HD : (j + 1) * HD]
+        block = text[:, j // 3, (j % 3) * HD : (j % 3 + 1) * HD]
+        send_ref[CHANS + j * 16 : CHANS + (j + 1) * 16, :] = block.astype(BF16)
 
 
 def total_of(ref, rows):
@@ -122,7 +126,7 @@
     idx_ref, send_ref, recv_ref, other_ref, gain_ref, out_ref, lat_ref, s_ref, v_ref, m_ref, own_ref
 ):
     tokens = lat_ref.shape[1]
-    chunk = 512
+    chunk = 1024
     n_chunks = tokens // chunk
     ones = jnp.where(lax.broadcasted_iota(jnp.int32, (MROWS - CHANS, HD), 0) == 0, 1.0, 0.0).astype(BF16)
     n_far = (recv_ref.shape[1] - PIECE) // HALF
@@ -199,6 +203,8 @@
 
 
 def text_body(image_ref, text_ref, out_w_ref, y_ref, att_ref):
+    step = 512
+
     def block(first):
         return text_ref[:, first : first + 16, :].reshape(text_ref.shape[0] * 16, HD)
 
@@ -212,7 +218,6 @@
         total = jnp.sum(image_ref[head, 1] * keep, axis=1, keepdims=True) + jnp.sum(p, axis=1, keepdims=True)
         att_ref[:, head * HD : (head + 1) * HD] = (acc / total).astype(BF16)
     att = att_ref[...]
-    step = 512
     for j in range(out_w_ref.shape[1] // step):
         y = dot(att, out_w_ref[:, j * step : (j + 1) * step]).astype(BF16)
         y_ref[:, :, j * step : (j + 1) * step] = y.reshape(y_ref.shape[0], y_ref.shape[1], step)
@@ -247,6 +252,7 @@
     teacher, student = rows(0), rows(n_mp)
     spread = jnp.abs(gap_ref[...] + noise_scale_of(idx_ref[3], gap_ref.shape) * teacher)
     spread = jnp.sum(jnp.sum(spread, axis=1, keepdims=True), axis=0, keepdims=True)
+    spread = jnp.broadcast_to(spread, (8, HD))
     diff = teacher - student
     diff_ref[...] = diff.T
     half = chans // 2
@@ -255,53 +261,58 @@
     cols = grad_ref.shape[1]
     hidden = hidden_ref[:, pl.ds(pl.multiple_of(idx_ref[1] * cols, HD), cols)]
     grad_ref[...] = dot(share.astype(BF16), hidden)
-    for p in range(8):
-        for g in range(3):
-            piece_ref[p, 4 * g : 4 * g + 4, :] = grad_ref[4 * p : 4 * p + 4, g * HD : (g + 1) * HD]
-        piece_ref[p, 12:16, :] = jnp.broadcast_to(spread, (4, HD))
+    for p in range(4):
+        terms = [grad_ref[8 * p : 8 * p + 8, g * HD : (g + 1) * HD] for g in range(3)]
+        block = in_parts(jnp.concatenate([*terms, spread], axis=0))
+        for y_hi in range(2):
+            piece_ref[2 * p + y_hi] = block
     feats = raw_ref.shape[1]
     raw_ref[...] = dot(diff.astype(BF16), gen_t_ref[:, pl.ds(pl.multiple_of(idx_ref[2] * feats, HD), feats)])
 
 
+def in_parts(block):
+    row = lax.broadcasted_iota(jnp.int32, block.shape, 0)
+    high = block.astype(BF16).astype(F32)
+    mid = (block - high).astype(BF16).astype(F32)
+    low = block - high - mid
+    return jnp.where(row == 25, mid, jnp.where(row == 26, low, high)).astype(BF16)
+
+
 def near_body(recv_ref, out_ref):
-    total = recv_ref[0]
+    total = recv_ref[0].astype(F32)
     for i in range(1, recv_ref.shape[0]):
-        total = total + recv_ref[i]
-    row = lax.broadcasted_iota(jnp.int32, total.shape, 0)
-    high = total.astype(BF16).astype(F32)
-    mid = (total - high).astype(BF16).astype(F32)
-    low = total - high - mid
-    out = jnp.where(row == 13, mid, jnp.where(row == 14, low, high)).astype(BF16)
+        total = total + recv_ref[i].astype(F32)
+    number = total[24:25, :] + total[25:26, :] + total[26:27, :]
+    out = in_parts(jnp.concatenate([total[0:24, :], jnp.broadcast_to(number, (8, HD))], axis=0))
     for i in range(out_ref.shape[0]):
         out_ref[i] = out
 
 
 def last_body(idx_ref, recv_ref, share_ref, raw_ref, x_ref, hidden_ref, gen_ref, *, entries):
     totals = []
-    for p in range(8):
+    for p in range(4):
         total = recv_ref[p].astype(F32)
-        for g in range(1, recv_ref.shape[0] // 8):
-            total = total + recv_ref[8 * g + p].astype(F32)
+        for g in range(1, recv_ref.shape[0] // 4):
+            total = total + recv_ref[4 * g + p].astype(F32)
         totals.append(total)
-    spread = totals[0][12:13, 0:1] + totals[0][13:14, 0:1] + totals[0][14:15, 0:1]
+    spread = totals[0][24:25, 0:1] + totals[0][25:26, 0:1] + totals[0][26:27, 0:1]
     factor = noise_scale_of(idx_ref[3], (1, 1)) / (spread / entries + 1e-06)
     x_ref[...] = share_ref[...] * factor
     hidden_ref[...] = (raw_ref[...] * factor).astype(BF16)
-    for p in range(8):
-        scaled = totals[p] * factor
+    for p in range(4):
         for g in range(3):
-            gen_ref[4 * p : 4 * p + 4, g * HD : (g + 1) * HD] = scaled[4 * g : 4 * g + 4, :]
-
-
-def exchange(array, axis, groups=None):
-    return lax.all_to_all(array, axis, 0, 0, axis_index_groups=groups, tiled=True)
+            gen_ref[8 * p : 8 * p + 8, g * HD : (g + 1) * HD] = totals[p][8 * g : 8 * g + 8, :] * factor
+
+
+def exchange(array, axis):
+    return lax.all_to_all(array, axis, 0, 0, tiled=True)
 
 
 def on_device(
     gen_hidden, w_gen, noise_latent, level_index, w_embed, modulation, w_qkv, qk_gain, text_kv, w_out, w_final
 ):
     rows_here, width = gen_hidden.shape
-    n_seq, n_mp = lax.axis_size("seq"), lax.axis_size("mp")
+    n_seq, n_far, n_mp = lax.axis_size(SEQ), lax.axis_size("z_far"), lax.axis_size("mp")
     chans = w_gen.shape[1]
     tokens = rows_here * n_seq
     sds = jax.ShapeDtypeStruct
@@ -309,7 +320,7 @@
     embed = w_embed[0]
     gen_t = w_gen.T
     idx = jnp.stack(
-        [lax.axis_index("seq"), lax.axis_index("mp"), lax.axis_index("role"), level_index[0]]
+        [lax.axis_index(SEQ), lax.axis_index("mp"), lax.axis_index("role"), level_index[0]]
     ).astype(jnp.int32)
     near_groups = [[8 * g + i for i in range(8)] for g in range(n_seq // 8)]
     far_groups = [[8 * g + i for g in range(n_seq // 8)] for i in range(8)]
@@ -325,21 +336,25 @@
     )
     noised, gap, send = call(
         latent_body,
-        (sds((rows_here, chans), F32), sds((rows_here, chans), F32), sds((chans + 96, HD), BF16)),
-        (idx_late, gen_hidden, gen_t, noise_latent.T, embed, text_kv[0].reshape(text_kv.shape[1], 6 * HD)),
+        (
+            sds((rows_here, chans), F32),
+            sds((rows_here, chans), F32),
+            sds((chans + 96, HD), BF16),
+        ),
+        (idx_late, gen_hidden, gen_t, noise_latent.T, embed, text_kv[0]),
         smem=1,
         limit=60,
     )
-    pieces = exchange(payload, "seq", near_groups)
+    pieces = exchange(payload, NEAR)
     pieces = call(far_body, sds((n_far, PIECE + HALF + 96, HD), BF16), (idx, pieces, send), smem=1)
-    pieces = exchange(pieces, "seq", far_groups)
+    pieces = exchange(pieces, "z_far")
     pieces, text = call(
         spread_body,
         (sds((8, PIECE + n_far * HALF, HD), BF16), sds((8, n_far * 96, HD), BF16)),
         (pieces,),
     )
-    pieces = exchange(pieces, "seq", near_groups)
-    text = exchange(text, "seq", near_groups).reshape(n_seq, 96, HD)
+    pieces = exchange(pieces, NEAR)
+    text = exchange(text, NEAR).reshape(n_seq, 96, HD)
     other = lax.ppermute(pieces[:, PIECE:, :], "mp", [(i, i ^ 1) for i in range(n_mp)])
 
     image = call(
@@ -373,14 +388,14 @@
     half = chans // 2
     grad_piece, share, raw = call(
         grad_body,
-        (sds((8, 16, HD), F32), sds((half, rows_here), F32), sds((rows_here, width // 2), F32)),
+        (sds((8, 32, HD), BF16), sds((half, rows_here), F32), sds((rows_here, width // 2), F32)),
         (idx, both, gap, gen_hidden, gen_t),
         scratch=(pltpu.VMEM((chans, rows_here), F32), pltpu.VMEM((half, 3 * HD), F32)),
         smem=1,
     )
-    near = exchange(grad_piece, "seq", near_groups)
-    near = call(near_body, sds((n_seq, 16, HD), BF16), (near,))
-    everything = exchange(near, "seq")
+    near = exchange(grad_piece, NEAR)
+    near = call(near_body, sds((n_seq // 2, 32, HD), BF16), (near,))
+    everything = exchange(near, ("z_far", "z_near"))
 
     def last(*refs):
         last_body(*refs, entries=tokens * chans)
@@ -395,16 +410,19 @@
 
 
 def solution(mesh):
+    n_role, n_seq, n_mp = (mesh.shape[name] for name in ("role", "seq", "mp"))
+    names = ("role", *SEQ, "mp")
+    mesh = jax.sharding.Mesh(mesh.devices.reshape(n_role, n_seq // 8, 4, 2, n_mp), names)
     placed = (
-        P("seq", None),
+        P(SEQ, None),
         P(),
-        P("seq", None),
+        P(SEQ, None),
         P(),
         P("role", None, None),
         P("role", None, None),
-        P("role", "seq", None, "mp"),
+        P("role", SEQ, None, "mp"),
         P("role", None, None),
-        P("role", "seq", None, "mp"),
+        P("role", SEQ, None, "mp"),
         P("role", "mp", None),
         P("role", None, None),
     )
@@ -412,6 +430,6 @@
         on_device,
         mesh=mesh,
         in_specs=placed,
-        out_specs=(P("seq", "role"), P("seq", "role"), P("mp", "role")),
+        out_specs=(P(SEQ, "role"), P(SEQ, "role"), P("mp", "role")),
         check_vma=False,
     )

time: 160 us -> 158 us (0.988)
  waiting for transfers between devices: 7.74 us -> 12.2 us
  Pallas kernels: 23 us -> 19.7 us
  blocking collectives: 109 us -> 107 us
    all_to_all x2, waiting for transfers between devices: 6.24 us -> 10.7 us  [exchange(): return lax.all_to_all(array, axis, 0, 0, tiled=True)]
    pallas_call x10, Pallas kernels: 23 us -> 19.7 us  [call(): pl.pallas_call(body, out_shape=out_shape, in_specs=[scalars if i < smem e...]
    all_to_all x6, blocking collectives: 109 us -> 107 us  [exchange(): return lax.all_to_all(array, axis, 0, 0, tiled=True)]
    unnamed x25 -> x24, local copies, waits for them, and re-layouts: 3.83 us -> 2.49 us
  transfers between devices with their start and end apart: 3 -> 3, of which waited for: 3 -> 3; matrix products, arithmetic and copies ran while one was open for 1% -> 0% of each run, Pallas kernels for 9% -> 7%
where the time goes in v2:
time: 158 us; the launch traced here: 157 us
  blocking collectives  107 us (68%)
  Pallas kernels  19.7 us (12%)
  starting transfers between devices  14 us (9%)
  waiting for transfers between devices  12.2 us (8%)
  local copies, waits for them, and re-layouts  2.51 us (2%)
    all_to_all x6, blocking collectives, exchange(): return lax.all_to_all(array, axis, 0, 0, tiled=True)  107 us
    pallas_call x10, Pallas kernels, call(): pl.pallas_call(body, out_shape=out_shape, in_specs=[scalars if i < smem e...  19.7 us
    all_to_all x2, starting transfers between devices, exchange(): return lax.all_to_all(array, axis, 0, 0, tiled=True)  12.1 us
    all_to_all x2, waiting for transfers between devices, exchange(): return lax.all_to_all(array, axis, 0, 0, tiled=True)  10.7 us
  transfers between devices with their start and end apart: 3, of which 3 were waited for; matrix products, arithmetic and copies ran while one was open for 0% of the time, Pallas kernels for 7%

profile of v2, /device:TPU:2, one launch (start us, length us, event | category | flops | bytes accessed | tf_op | source)
XLA Modules:
  0.0 157.2 jit_solution(11875120380350620763)
XLA Ops:
  1.3 0.6 pad_add_fusion.idx_ref.refs_0_
  1.9 0.0 copy-start.10
  1.9 2.3 %shard_map.130 = (bf16[8,80,128]{2,1,0:T(8,128)(2,1)}, s32[4]{0:T(128)}) custom-call(s32[4]{0:T(128)} %pad_add_fusion.idx_ref.refs_0_, bf16[64,3072]{1,0:T(8,128)(2,1)} %bitcast.19, f32[3,1,3072]{2,1,0:T(1,128)} %bitcast.27, bf16[3,96,384]{2,1,0:T(8,128)(2,1)} %bitcast.30), custom_call_target="tpu_custom_call" | custom-call | tf_op jit(solution)/shard_map/pallas_call | solution.py:29
  4.2 8.5 %all-to-all-start = ((bf16[8,80,128]{2,1,0:T(8,128)(2,1)}), bf16[8,80,128]{2,1,0:T(8,128)(2,1)S(1)}, u32[]{:S(2)}, u32[]{:S(2)}) async-start(bf16[8,80,128]{2,1,0:T(8,128)(2,1)} %get-tuple-element.18), calls=%async_computation | async-start | bytes 327680 | tf_op jit(solution)/shard_map/all_to_all | solution.py:308
  12.7 3.5 %shard_map.131 = (f32[128,64]{1,0:T(8,128)}, f32[128,64]{1,0:T(8,128)}, bf16[160,128]{1,0:T(8,128)(2,1)}) custom-call(s32[4]{0:T(128)} %get-tuple-element.16.idx_ref, bf16[128,3072]{1,0:T(8,128)(2,1)} %hidden_ref.3, bf16[64,3072]{1,0:T(8,128)(2,1)} %bitcast.24, bf16[64,128]{1,0:T(8,128)(2,1)} %bitcast.32, bf16[64,3072]{1,0:T(8,128)(2,1)} %bitcast.20, ...), custom_call_target="tpu_custom_call" | custom-call | tf_op jit(solution)/shard_map/pallas_call | solution.py:29
  16.2 0.0 copy-start.11
  16.2 5.6 %all-to-all-done.recv_ref = bf16[8,80,128]{2,1,0:T(8,128)(2,1)S(1)} async-done(((bf16[8,80,128]{2,1,0:T(8,128)(2,1)}), bf16[8,80,128]{2,1,0:T(8,128)(2,1)S(1)}, u32[]{:S(2)}, u32[]{:S(2)}) %all-to-all-start) | async-done | bytes 163872 | tf_op jit(solution)/shard_map/all_to_all | solution.py:308
  21.8 0.0 copy-done.10
  21.8 0.0 copy-start.5
  21.8 0.8 copy-done.5
  22.6 0.0 copy-start.6
  22.6 0.6 shard_map.132
  23.2 28.4 %all_to_all.40.recv_ref = bf16[4,208,128]{2,1,0:T(8,128)(2,1)S(1)} all-to-all(bf16[4,208,128]{2,1,0:T(8,128)(2,1)S(1)} %shard_map.132), channel_id=1, replica_groups=mesh['role'=2,'z_far'=4,'z_near'=4,'y_hi'=2,'mp'=8] {'z_far'}, dimensions={0} | all-to-all | bytes 425984 | tf_op jit(solution)/shard_map/all_to_all | solution.py:308
  51.6 1.0 shard_map.133
  52.6 14.6 %all_to_all.41.recv_ref = bf16[8,208,128]{2,1,0:T(8,128)(2,1)S(1)} all-to-all(bf16[8,208,128]{2,1,0:T(8,128)(2,1)S(1)} %get-tuple-element.19), channel_id=1, replica_groups=mesh['role'=2,'z_far'=4,'z_near'=4,'y_hi'=2,'mp'=8] {'z_near','y_hi'}, dimensions={0} | all-to-all | bytes 851968 | tf_op jit(solution)/shard_map/all_to_all | solution.py:308
  67.2 3.5 %all-to-all-start.3 = ((bf16[8,384,128]{2,1,0:T(8,128)(2,1)}), bf16[8,384,128]{2,1,0:T(8,128)(2,1)S(1)}, u32[]{:S(2)}, u32[]{:S(2)}) async-start(bf16[8,384,128]{2,1,0:T(8,128)(2,1)} %get-tuple-element.20), calls=%async_computation.3 | async-start | bytes 1572864 | tf_op jit(solution)/shard_map/all_to_all | solution.py:308
  70.8 1.9 %collective-permute-start = (bf16[8,128,128]{2,1,0:T(8,128)(2,1)S(1)}, bf16[8,128,128]{2,1,0:T(8,128)(2,1)S(1)}, u32[]{:S(2)}, u32[]{:S(2)}) collective-permute-start(bf16[8,128,128]{2,1,0:T(8,128)(2,1)S(1)} %slice.4), channel_id=1, source_target_pairs={{0,1},{1,0},{2,3},{3,2},{4,5},{5,4},{6,7},{7,6},{8,9},{9,8},{10,11... | collective-permute-start | bytes 786440 | tf_op jit(solution)/shard_map/ppermute | solution.py:358
  72.7 1.5 collective-permute-done.other_ref
  74.2 0.0 copy-done.11
  74.2 0.0 copy-done.6
  74.2 7.1 %shard_map.134.image_ref = f32[3,4,128,128]{3,2,1,0:T(8,128)S(1)} custom-call(s32[4]{0:T(128)S(1)} %copy-done.10, bf16[160,128]{1,0:T(8,128)(2,1)S(1)} %copy-done.6, bf16[8,208,128]{2,1,0:T(8,128)(2,1)S(1)} %all_to_all.41.recv_ref, bf16[8,128,128]{2,1,0:T(8,128)(2,1)S(1)} %collective-permute-done.other_ref, f32[2,128]{1,0:T(2,128)S(1)} %bitcast.29), custom_call_target="tpu_custom_call" | custom-call | tf_op jit(solution)/shard_map/pallas_call | solution.py:29
  81.3 5.1 %all-to-all-done.3 = bf16[8,384,128]{2,1,0:T(8,128)(2,1)S(1)} async-done(((bf16[8,384,128]{2,1,0:T(8,128)(2,1)}), bf16[8,384,128]{2,1,0:T(8,128)(2,1)S(1)}, u32[]{:S(2)}, u32[]{:S(2)}) %all-to-all-start.3) | async-done | bytes 786464 | tf_op jit(solution)/shard_map/all_to_all | solution.py:308
  86.4 0.0 copy-start.2
  86.4 1.7 %copy-done.2 = bf16[1,384,3072]{2,1,0:T(8,128)(2,1)S(1)} copy-done((bf16[1,384,3072]{2,1,0:T(8,128)(2,1)S(1)}, bf16[1,384,3072]{2,1,0:T(8,128)(2,1)}, u32[]{:S(2)}) %copy-start.2) | copy-done | bytes 2359320
  88.1 0.0 copy-start
  88.1 0.0 copy-start.4
  88.1 0.0 copy-start.7
  88.1 0.0 copy-start.9
  88.1 1.7 %shard_map.135 = bf16[8,16,3072]{2,1,0:T(8,128)(2,1)S(1)} custom-call(f32[3,4,128,128]{3,2,1,0:T(8,128)S(1)} %shard_map.134.image_ref, bf16[32,96,128]{2,1,0:T(8,128)(2,1)S(1)} %bitcast.22, bf16[384,3072]{1,0:T(8,128)(2,1)S(1)} %bitcast.23), custom_call_target="tpu_custom_call" | custom-call | tf_op jit(solution)/shard_map/pallas_call | solution.py:29
  89.8 0.0 copy-start.1
  89.8 0.0 copy-start.3
  89.8 0.0 copy-start.8
  89.8 16.5 %all_to_all.42.parts_ref = bf16[8,16,3072]{2,1,0:T(8,128)(2,1)S(1)} all-to-all(bf16[8,16,3072]{2,1,0:T(8,128)(2,1)S(1)} %shard_map.135), channel_id=1, replica_groups=mesh['role'=2,'z_far'=4,'z_near'=4,'y_hi'=2,'mp'=8] {'mp'}, dimensions={0} | all-to-all | bytes 1572864 | tf_op jit(solution)/shard_map/all_to_all | solution.py:308
  106.3 0.0 copy-done
  106.3 0.0 copy-done.4
  106.3 0.0 copy-done.7
  106.3 0.0 copy-done.9
  106.4 1.2 shard_map.136
  107.5 9.1 %all_to_all.43.both_ref = f32[16,8,128]{2,1,0:T(8,128)S(1)} all-to-all(f32[16,8,128]{2,1,0:T(8,128)S(1)} %shard_map.136), channel_id=1, replica_groups=mesh['role'=2,'z_far'=4,'z_near'=4,'y_hi'=2,'mp'=8] {'role','mp'}, dimensions={0} | all-to-all | bytes 131072 | tf_op jit(solution)/shard_map/all_to_all | solution.py:308
  116.6 0.0 copy-done.1
  116.6 0.0 copy-done.3
  116.6 0.0 copy-done.8
  116.6 0.9 shard_map.137
  117.5 13.8 %all_to_all.44.recv_ref = bf16[8,32,128]{2,1,0:T(8,128)(2,1)S(1)} all-to-all(bf16[8,32,128]{2,1,0:T(8,128)(2,1)S(1)} %get-tuple-element.23), channel_id=1, replica_groups=mesh['role'=2,'z_far'=4,'z_near'=4,'y_hi'=2,'mp'=8] {'z_near','y_hi'}, dimensions={0} | all-to-all | bytes 131072 | tf_op jit(solution)/shard_map/all_to_all | solution.py:308
  131.4 24.4 %all_to_all.45.refs_1_ = bf16[16,32,128]{2,1,0:T(8,128)(2,1)S(1)} all-to-all(bf16[16,32,128]{2,1,0:T(8,128)(2,1)S(1)} %shard_map.138), channel_id=1, replica_groups=mesh['role'=2,'z_far'=4,'z_near'=4,'y_hi'=2,'mp'=8] {'z_far','z_near'}, dimensions={0} | all-to-all | bytes 262144 | tf_op jit(solution)/shard_map/all_to_all | solution.py:308
  155.8 1.4 shard_map.139
  (2 shorter events, 0.0 us)
Async XLA Ops:
  1.9 19.9 %copy-start.10 = (s32[4]{0:T(128)S(1)}, s32[4]{0:T(128)}, u32[]{:S(2)}) copy-start(s32[4]{0:T(128)} %pad_add_fusion.idx_ref.refs_0_) | copy-start | bytes 52
  4.2 17.6 %all-to-all-start = ((bf16[8,80,128]{2,1,0:T(8,128)(2,1)}), bf16[8,80,128]{2,1,0:T(8,128)(2,1)S(1)}, u32[]{:S(2)}, u32[]{:S(2)}) async-start(bf16[8,80,128]{2,1,0:T(8,128)(2,1)} %get-tuple-element.18), calls=%async_computation | async-start | bytes 327680 | tf_op jit(solution)/shard_map/all_to_all | solution.py:308
  16.2 58.0 %copy-start.11 = (f32[1,2,128]{2,1,0:T(2,128)S(1)}, f32[1,2,128]{2,1,0:T(2,128)}, u32[]{:S(2)}) copy-start(f32[1,2,128]{2,1,0:T(2,128)} %param.18) | copy-start | bytes 3076
  21.8 0.8 copy-start.5
  22.6 51.6 %copy-start.6 = (bf16[160,128]{1,0:T(8,128)(2,1)S(1)}, bf16[160,128]{1,0:T(8,128)(2,1)}, u32[]{:S(2)}) copy-start(bf16[160,128]{1,0:T(8,128)(2,1)} %get-tuple-element.17.send_ref) | copy-start | bytes 122884
  67.2 19.2 %all-to-all-start.3 = ((bf16[8,384,128]{2,1,0:T(8,128)(2,1)}), bf16[8,384,128]{2,1,0:T(8,128)(2,1)S(1)}, u32[]{:S(2)}, u32[]{:S(2)}) async-start(bf16[8,384,128]{2,1,0:T(8,128)(2,1)} %get-tuple-element.20), calls=%async_computation.3 | async-start | bytes 1572864 | tf_op jit(solution)/shard_map/all_to_all | solution.py:308
  70.8 3.4 %collective-permute-start = (bf16[8,128,128]{2,1,0:T(8,128)(2,1)S(1)}, bf16[8,128,128]{2,1,0:T(8,128)(2,1)S(1)}, u32[]{:S(2)}, u32[]{:S(2)}) collective-permute-start(bf16[8,128,128]{2,1,0:T(8,128)(2,1)S(1)} %slice.4), channel_id=1, source_target_pairs={{0,1},{1,0},{2,3},{3,2},{4,5},{5,4},{6,7},{7,6},{8,9},{9,8},{10,11... | collective-permute-start | bytes 786440 | tf_op jit(solution)/shard_map/ppermute | solution.py:358
  86.4 1.7 %copy-start.2 = (bf16[1,384,3072]{2,1,0:T(8,128)(2,1)S(1)}, bf16[1,384,3072]{2,1,0:T(8,128)(2,1)}, u32[]{:S(2)}) copy-start(bf16[1,384,3072]{2,1,0:T(8,128)(2,1)} %param.20) | copy-start | bytes 7077892
  88.1 18.3 %copy-start = (bf16[1,64,3072]{2,1,0:T(8,128)(2,1)S(1)}, bf16[1,64,3072]{2,1,0:T(8,128)(2,1)}, u32[]{:S(2)}) copy-start(bf16[1,64,3072]{2,1,0:T(8,128)(2,1)} %param.15) | copy-start | bytes 1179652
  88.1 18.3 %copy-start.4 = (bf16[1,3072,64]{1,2,0:T(8,128)(2,1)S(1)}, bf16[1,3072,64]{1,2,0:T(8,128)(2,1)}, u32[]{:S(2)}) copy-start(bf16[1,3072,64]{1,2,0:T(8,128)(2,1)} %param.21) | copy-start | bytes 1179652
  88.1 18.3 %copy-start.7 = (f32[1,3,3072]{2,0,1:T(1,128)S(1)}, f32[1,3,3072]{2,0,1:T(1,128)}, u32[]{:S(2)}) copy-start(f32[1,3,3072]{2,0,1:T(1,128)} %param.16) | copy-start | bytes 110596
  88.1 18.3 %copy-start.9 = (f32[128,64]{1,0:T(8,128)S(1)}, f32[128,64]{1,0:T(8,128)}, u32[]{:S(2)}) copy-start(f32[128,64]{1,0:T(8,128)} %get-tuple-element.21.noised_ref) | copy-start | bytes 98308
  89.8 26.8 %copy-start.1 = (bf16[128,3072]{1,0:T(8,128)(2,1)S(1)}, bf16[128,3072]{1,0:T(8,128)(2,1)}, u32[]{:S(2)}) copy-start(bf16[128,3072]{1,0:T(8,128)(2,1)} %hidden_ref.3) | copy-start | bytes 2359300
  89.8 26.8 %copy-start.3 = (bf16[3072,64]{0,1:T(8,128)(2,1)S(1)}, bf16[3072,64]{0,1:T(8,128)(2,1)}, u32[]{:S(2)}) copy-start(bf16[3072,64]{0,1:T(8,128)(2,1)} %param.12) | copy-start | bytes 1179652
  89.8 26.8 %copy-start.8 = (f32[128,64]{1,0:T(8,128)S(1)}, f32[128,64]{1,0:T(8,128)}, u32[]{:S(2)}) copy-start(f32[128,64]{1,0:T(8,128)} %get-tuple-element.22.gap_ref) | copy-start | bytes 98308

commit v3 on v2

--- a/solution.py
+++ b/solution.py
@@ -36,15 +36,19 @@
     )(*args)
 
 
+def seq_here():
+    return (lax.axis_index("z_far") * 4 + lax.axis_index("z_near")) * 2 + lax.axis_index("y_hi")
+
+
 def noise_scale_of(level, shape):
     time_frac = (jnp.full(shape, level, jnp.int32).astype(F32) + 1.0) / (LEVELS + 1.0)
     return 3.0 * time_frac / (1.0 + 2.0 * time_frac)
 
 
-def weight_body(idx_ref, embed_ref, mod_ref, qkv_ref, payload_ref, idx_out_ref, term_ref):
+def weight_body(level_ref, embed_ref, mod_ref, qkv_ref, payload_ref, level_out_ref, term_ref):
     width = embed_ref.shape[1]
     features = qkv_ref.shape[1]
-    offset = idx_ref[0] * features
+    offset = seq_here() * features
     start = pl.multiple_of(jnp.minimum((offset >> 7) << 7, width - 256), HD)
     mean = jnp.sum(embed_ref[...].astype(F32), axis=1, keepdims=True) / width
     window = embed_ref[:, pl.ds(start, 256)].astype(F32)
@@ -72,15 +76,14 @@
     term_ref[9 * CHANS + 9 :, :] = jnp.zeros((term_ref.shape[0] - 9 * CHANS - 9, HD), F32)
     for p in range(payload_ref.shape[0]):
         payload_ref[p] = term_ref[p * PIECE : (p + 1) * PIECE, :].astype(BF16)
-    for i in range(idx_out_ref.shape[0]):
-        idx_out_ref[i] = idx_ref[i]
+    level_out_ref[0] = level_ref[0]
 
 
 def latent_body(
-    idx_ref, hidden_ref, gen_t_ref, noise_t_ref, embed_ref, text_in_ref, noised_ref, gap_ref, send_ref
+    level_ref, hidden_ref, gen_t_ref, noise_t_ref, embed_ref, text_in_ref, noised_ref, gap_ref, send_ref
 ):
     x_t = dot(gen_t_ref[...], hidden_ref[...], NT)
-    noise_scale = noise_scale_of(idx_ref[3], x_t.shape)
+    noise_scale = noise_scale_of(level_ref[0], x_t.shape)
     noised_t = ((1.0 - noise_scale) * x_t + noise_scale * noise_t_ref[...].astype(F32)).astype(BF16)
     noised = noised_t.astype(F32).T
     noised_ref[...] = noised
@@ -103,9 +106,9 @@
     return total.astype(BF16)
 
 
-def far_body(idx_ref, recv_ref, send_ref, out_ref):
+def far_body(recv_ref, send_ref, out_ref):
     piece = total_of(recv_ref, PIECE)
-    channels = send_ref[pl.ds(pl.multiple_of((idx_ref[1] & 1) * HALF, HALF), HALF), :]
+    channels = send_ref[pl.ds(pl.multiple_of((lax.axis_index("mp") & 1) * HALF, HALF), HALF), :]
     for i in range(out_ref.shape[0]):
         out_ref[i, 0:PIECE, :] = piece
         out_ref[i, PIECE : PIECE + HALF, :] = channels
@@ -123,7 +126,7 @@
 
 
 def image_body(
-    idx_ref, send_ref, recv_ref, other_ref, gain_ref, out_ref, lat_ref, s_ref, v_ref, m_ref, own_ref
+    send_ref, recv_ref, other_ref, gain_ref, out_ref, lat_ref, s_ref, v_ref, m_ref, own_ref
 ):
     tokens = lat_ref.shape[1]
     chunk = 1024
@@ -141,7 +144,7 @@
     own_ref[...] = send_ref[0:CHANS, :].astype(F32)
 
     def reordered(ref, base):
-        core = idx_ref[1] & 1
+        core = lax.axis_index("mp") & 1
         return jnp.concatenate(
             [ref[pl.ds(pl.multiple_of(k * HALF + base, HALF), HALF), :] for k in (core, 1 - core)], axis=0
         )
@@ -202,9 +205,7 @@
     lax.fori_loop(0, n_chunks, mix_step, 0)
 
 
-def text_body(image_ref, text_ref, out_w_ref, y_ref, att_ref):
-    step = 512
-
+def text_body(image_ref, text_ref, att_ref):
     def block(first):
         return text_ref[:, first : first + 16, :].reshape(text_ref.shape[0] * 16, HD)
 
@@ -217,18 +218,14 @@
         acc = image_ref[head, 0] * keep + dot(p.astype(BF16), block(48 + head * 16))
         total = jnp.sum(image_ref[head, 1] * keep, axis=1, keepdims=True) + jnp.sum(p, axis=1, keepdims=True)
         att_ref[:, head * HD : (head + 1) * HD] = (acc / total).astype(BF16)
-    att = att_ref[...]
-    for j in range(out_w_ref.shape[1] // step):
-        y = dot(att, out_w_ref[:, j * step : (j + 1) * step]).astype(BF16)
-        y_ref[:, :, j * step : (j + 1) * step] = y.reshape(y_ref.shape[0], y_ref.shape[1], step)
-
-
-def velocity_body(idx_ref, parts_ref, noised_ref, embed_ref, mod_ref, final_t_ref, v_ref):
+
+
+def velocity_body(parts_ref, noised_ref, embed_ref, mod_ref, final_t_ref, v_ref):
     total = parts_ref[0].astype(F32)
     for i in range(1, parts_ref.shape[0]):
         total = total + parts_ref[i].astype(F32)
     own_rows = total.shape[0]
-    own = noised_ref[pl.ds(pl.multiple_of(idx_ref[1] * own_rows, own_rows), own_rows), :].astype(BF16)
+    own = noised_ref[pl.ds(pl.multiple_of(lax.axis_index("mp") * own_rows, own_rows), own_rows), :].astype(BF16)
     h = dot(own, embed_ref[...]) + mod_ref[2] * total
     width = h.shape[1]
     h = h - jnp.sum(h, axis=1, keepdims=True) / width
@@ -239,7 +236,7 @@
         v_ref[i] = v
 
 
-def grad_body(idx_ref, both_ref, gap_ref, hidden_ref, gen_t_ref, piece_ref, share_ref, raw_ref, diff_ref, grad_ref):
+def grad_body(level_ref, both_ref, gap_ref, hidden_ref, gen_t_ref, piece_ref, share_ref, raw_ref, diff_ref, grad_ref):
     n_mp = both_ref.shape[0] // 2
     chans = gap_ref.shape[1]
 
@@ -250,16 +247,16 @@
         return jnp.concatenate(blocks, axis=0)
 
     teacher, student = rows(0), rows(n_mp)
-    spread = jnp.abs(gap_ref[...] + noise_scale_of(idx_ref[3], gap_ref.shape) * teacher)
+    spread = jnp.abs(gap_ref[...] + noise_scale_of(level_ref[0], gap_ref.shape) * teacher)
     spread = jnp.sum(jnp.sum(spread, axis=1, keepdims=True), axis=0, keepdims=True)
     spread = jnp.broadcast_to(spread, (8, HD))
     diff = teacher - student
     diff_ref[...] = diff.T
     half = chans // 2
-    share = diff_ref[pl.ds(pl.multiple_of(idx_ref[2] * half, half), half), :]
+    share = diff_ref[pl.ds(pl.multiple_of(lax.axis_index("role") * half, half), half), :]
     share_ref[...] = share
     cols = grad_ref.shape[1]
-    hidden = hidden_ref[:, pl.ds(pl.multiple_of(idx_ref[1] * cols, HD), cols)]
+    hidden = hidden_ref[:, pl.ds(pl.multiple_of(lax.axis_index("mp") * cols, HD), cols)]
     grad_ref[...] = dot(share.astype(BF16), hidden)
     for p in range(4):
         terms = [grad_ref[8 * p : 8 * p + 8, g * HD : (g + 1) * HD] for g in range(3)]
@@ -267,7 +264,7 @@
         for y_hi in range(2):
             piece_ref[2 * p + y_hi] = block
     feats = raw_ref.shape[1]
-    raw_ref[...] = dot(diff.astype(BF16), gen_t_ref[:, pl.ds(pl.multiple_of(idx_ref[2] * feats, HD), feats)])
+    raw_ref[...] = dot(diff.astype(BF16), gen_t_ref[:, pl.ds(pl.multiple_of(lax.axis_index("role") * feats, HD), feats)])
 
 
 def in_parts(block):
@@ -288,7 +285,7 @@
         out_ref[i] = out
 
 
-def last_body(idx_ref, recv_ref, share_ref, raw_ref, x_ref, hidden_ref, gen_ref, *, entries):
+def last_body(level_ref, recv_ref, share_ref, raw_ref, x_ref, hidden_ref, gen_ref, *, entries):
     totals = []
     for p in range(4):
         total = recv_ref[p].astype(F32)
@@ -296,7 +293,7 @@
             total = total + recv_ref[4 * g + p].astype(F32)
         totals.append(total)
     spread = totals[0][24:25, 0:1] + totals[0][25:26, 0:1] + totals[0][26:27, 0:1]
-    factor = noise_scale_of(idx_ref[3], (1, 1)) / (spread / entries + 1e-06)
+    factor = noise_scale_of(level_ref[0], (1, 1)) / (spread / entries + 1e-06)
     x_ref[...] = share_ref[...] * factor
     hidden_ref[...] = (raw_ref[...] * factor).astype(BF16)
     for p in range(4):
@@ -319,17 +316,10 @@
     mods = jnp.transpose(modulation, (1, 0, 2))
     embed = w_embed[0]
     gen_t = w_gen.T
-    idx = jnp.stack(
-        [lax.axis_index(SEQ), lax.axis_index("mp"), lax.axis_index("role"), level_index[0]]
-    ).astype(jnp.int32)
-    near_groups = [[8 * g + i for i in range(8)] for g in range(n_seq // 8)]
-    far_groups = [[8 * g + i for g in range(n_seq // 8)] for i in range(8)]
-
-    n_far = n_seq // 8
-    payload, idx_late = call(
+    payload, level_late = call(
         weight_body,
-        (sds((8, PIECE, HD), BF16), sds(idx.shape, jnp.int32)),
-        (idx, embed, mods, jnp.transpose(w_qkv[0], (1, 0, 2))),
+        (sds((8, PIECE, HD), BF16), sds((1,), jnp.int32)),
+        (level_index, embed, mods, jnp.transpose(w_qkv[0], (1, 0, 2))),
         scratch=(pltpu.VMEM((8 * PIECE, HD), F32),),
         smem=1,
         limit=60,
@@ -341,12 +331,12 @@
             sds((rows_here, chans), F32),
             sds((chans + 96, HD), BF16),
         ),
-        (idx_late, gen_hidden, gen_t, noise_latent.T, embed, text_kv[0]),
+        (level_late, gen_hidden, gen_t, noise_latent.T, embed, text_kv[0]),
         smem=1,
         limit=60,
     )
     pieces = exchange(payload, NEAR)
-    pieces = call(far_body, sds((n_far, PIECE + HALF + 96, HD), BF16), (idx, pieces, send), smem=1)
+    pieces = call(far_body, sds((n_far, PIECE + HALF + 96, HD), BF16), (pieces, send), limit=60)
     pieces = exchange(pieces, "z_far")
     pieces, text = call(
         spread_body,
@@ -360,7 +350,7 @@
     image = call(
         image_body,
         sds((3, 4, rows_here, HD), F32),
-        (idx, send, pieces, other, qk_gain[0]),
+        (send, pieces, other, qk_gain[0]),
         scratch=(
             pltpu.VMEM((MROWS, tokens), BF16),
             pltpu.VMEM((3, rows_here, tokens), F32),
@@ -368,28 +358,22 @@
             pltpu.VMEM((8 * PIECE, HD), F32),
             pltpu.VMEM((chans, HD), F32),
         ),
-        smem=1,
     )
     own_rows = rows_here // n_mp
-    y = call(
-        text_body,
-        sds((n_mp, own_rows, width), BF16),
-        (image, text, w_out[0]),
-        scratch=(pltpu.VMEM((rows_here, 3 * HD), BF16),),
-    )
+    attended = call(text_body, sds((rows_here, 3 * HD), BF16), (image, text))
+    y = dot(attended, w_out[0]).astype(BF16).reshape(n_mp, own_rows, width)
     parts = exchange(y, "mp")
     velocity = call(
         velocity_body,
         sds((2 * n_mp, 8, 2 * chans), F32),
-        (idx, parts, noised, embed, mods, w_final[0].T),
-        smem=1,
+        (parts, noised, embed, mods, w_final[0].T),
     )
     both = exchange(velocity, ("role", "mp"))
     half = chans // 2
     grad_piece, share, raw = call(
         grad_body,
         (sds((8, 32, HD), BF16), sds((half, rows_here), F32), sds((rows_here, width // 2), F32)),
-        (idx, both, gap, gen_hidden, gen_t),
+        (level_index, both, gap, gen_hidden, gen_t),
         scratch=(pltpu.VMEM((chans, rows_here), F32), pltpu.VMEM((half, 3 * HD), F32)),
         smem=1,
     )
@@ -403,7 +387,7 @@
     grad_x_t, grad_hidden, grad_gen_t = call(
         last,
         (sds((half, rows_here), F32), sds((rows_here, width // 2), BF16), sds((half, 3 * HD), F32)),
-        (idx, everything, share, raw),
+        (level_index, everything, share, raw),
         smem=1,
     )
     return grad_x_t.T, grad_hidden, grad_gen_t.T

time: 158 us -> 155 us (0.981)
  waiting for transfers between devices: 12.2 us -> 9.47 us
  local copies, waits for them, and re-layouts: 2.51 us -> 4.75 us
  Pallas kernels: 19.7 us -> 17.7 us
    all_to_all x2, waiting for transfers between devices: 10.7 us -> 7.97 us  [exchange(): return lax.all_to_all(array, axis, 0, 0, tiled=True)]
    pallas_call x10, Pallas kernels: 19.7 us -> 17.7 us  [call(): pl.pallas_call(body, out_shape=out_shape, in_specs=[scalars if i < smem e...]
    unnamed x24 -> x30, local copies, waits for them, and re-layouts: 2.49 us -> 3.77 us
  transfers between devices with their start and end apart: 3 -> 3, of which waited for: 3 -> 3; matrix products, arithmetic and copies ran while one was open for 0% -> 1% of each run, Pallas kernels for 7% -> 7%
where the time goes in v3:
time: 155 us; the launch traced here: 154 us
  blocking collectives  106 us (68%)
  Pallas kernels  17.7 us (11%)
  starting transfers between devices  14 us (9%)
  waiting for transfers between devices  9.47 us (6%)
  local copies, waits for them, and re-layouts  4.75 us (3%)
  between operations  1.6 us (1%)
    all_to_all x6, blocking collectives, exchange(): return lax.all_to_all(array, axis, 0, 0, tiled=True)  106 us
    pallas_call x10, Pallas kernels, call(): pl.pallas_call(body, out_shape=out_shape, in_specs=[scalars if i < smem e...  17.7 us
    all_to_all x2, starting transfers between devices, exchange(): return lax.all_to_all(array, axis, 0, 0, tiled=True)  12.1 us
    all_to_all x2, waiting for transfers between devices, exchange(): return lax.all_to_all(array, axis, 0, 0, tiled=True)  7.97 us
    unnamed x30, local copies, waits for them, and re-layouts  3.77 us
  transfers between devices with their start and end apart: 3, of which 3 were waited for; matrix products, arithmetic and copies ran while one was open for 1% of the time, Pallas kernels for 7%

profile of v3, /device:TPU:2, one launch (start us, length us, event | category | flops | bytes accessed | tf_op | source)
XLA Modules:
  0.0 154.0 jit_solution(6642116370640489455)
XLA Ops:
  0.6 0.0 copy-start
  1.4 2.3 %shard_map.130 = (bf16[8,80,128]{2,1,0:T(8,128)(2,1)}, s32[1]{0:T(128)}) custom-call(s32[1]{0:T(128)S(6)} %copy.14.level_ref.refs_0_, bf16[64,3072]{1,0:T(8,128)(2,1)} %bitcast.20, f32[3,1,3072]{2,1,0:T(1,128)} %bitcast.27, bf16[3,96,384]{2,1,0:T(8,128)(2,1)} %bitcast.31), custom_call_target="tpu_custom_call" | custom-call | tf_op jit(solution)/shard_map/pallas_call | solution.py:29
  3.7 8.6 %all-to-all-start = ((bf16[8,80,128]{2,1,0:T(8,128)(2,1)}), bf16[8,80,128]{2,1,0:T(8,128)(2,1)S(1)}, u32[]{:S(2)}, u32[]{:S(2)}) async-start(bf16[8,80,128]{2,1,0:T(8,128)(2,1)} %get-tuple-element.18), calls=%async_computation | async-start | bytes 327680 | tf_op jit(solution)/shard_map/all_to_all | solution.py:305
  12.3 4.1 %shard_map.131 = (f32[128,64]{1,0:T(8,128)}, f32[128,64]{1,0:T(8,128)}, bf16[160,128]{1,0:T(8,128)(2,1)}) custom-call(s32[1]{0:T(128)} %get-tuple-element.16.level_ref, bf16[128,3072]{1,0:T(8,128)(2,1)} %hidden_ref.3, bf16[64,3072]{1,0:T(8,128)(2,1)} %bitcast.24, bf16[64,128]{1,0:T(8,128)(2,1)} %bitcast.33, bf16[64,3072]{1,0:T(8,128)(2,1)} %bitcast.21, ...), custom_call_target="tpu_custom_call" | custom-call | tf_op jit(solution)/shard_map/pallas_call | solution.py:29
  16.4 4.9 %all-to-all-done.recv_ref = bf16[8,80,128]{2,1,0:T(8,128)(2,1)S(1)} async-done(((bf16[8,80,128]{2,1,0:T(8,128)(2,1)}), bf16[8,80,128]{2,1,0:T(8,128)(2,1)S(1)}, u32[]{:S(2)}, u32[]{:S(2)}) %all-to-all-start) | async-done | bytes 163872 | tf_op jit(solution)/shard_map/all_to_all | solution.py:305
  21.4 0.7 copy-done.14
  22.0 1.6 %shard_map.132 = bf16[4,208,128]{2,1,0:T(8,128)(2,1)} custom-call(bf16[8,80,128]{2,1,0:T(8,128)(2,1)} %copy-done.14, bf16[160,128]{1,0:T(8,128)(2,1)} %get-tuple-element.17.send_ref), custom_call_target="tpu_custom_call" | custom-call | tf_op jit(solution)/shard_map/pallas_call | solution.py:29
  23.7 28.6 %all_to_all.40.recv_ref = bf16[4,208,128]{2,1,0:T(8,128)(2,1)S(1)} all-to-all(bf16[4,208,128]{2,1,0:T(8,128)(2,1)} %shard_map.132), channel_id=1, replica_groups=mesh['role'=2,'z_far'=4,'z_near'=4,'y_hi'=2,'mp'=8] {'z_far'}, dimensions={0} | all-to-all | bytes 425984 | tf_op jit(solution)/shard_map/all_to_all | solution.py:305
  52.3 0.1 shard_map.133
  52.4 0.0 copy-start.7
  52.4 15.8 %all_to_all.41.recv_ref = bf16[8,208,128]{2,1,0:T(8,128)(2,1)} all-to-all(bf16[8,208,128]{2,1,0:T(8,128)(2,1)S(1)} %get-tuple-element.19), channel_id=1, replica_groups=mesh['role'=2,'z_far'=4,'z_near'=4,'y_hi'=2,'mp'=8] {'z_near','y_hi'}, dimensions={0} | all-to-all | bytes 851968 | tf_op jit(solution)/shard_map/all_to_all | solution.py:305
  68.3 0.0 copy-done.7
  68.3 3.5 %all-to-all-start.3 = ((bf16[8,384,128]{2,1,0:T(8,128)(2,1)}), bf16[8,384,128]{2,1,0:T(8,128)(2,1)S(1)}, u32[]{:S(2)}, u32[]{:S(2)}) async-start(bf16[8,384,128]{2,1,0:T(8,128)(2,1)} %copy-done.7), calls=%async_computation.3 | async-start | bytes 1572864 | tf_op jit(solution)/shard_map/all_to_all | solution.py:305
  71.8 1.0 slice.4
  72.8 1.9 %collective-permute-start = (bf16[8,128,128]{2,1,0:T(8,128)(2,1)S(1)}, bf16[8,128,128]{2,1,0:T(8,128)(2,1)S(1)}, u32[]{:S(2)}, u32[]{:S(2)}) collective-permute-start(bf16[8,128,128]{2,1,0:T(8,128)(2,1)S(1)} %slice.4), channel_id=1, source_target_pairs={{0,1},{1,0},{2,3},{3,2},{4,5},{5,4},{6,7},{7,6},{8,9},{9,8},{10,11... | collective-permute-start | bytes 786440 | tf_op jit(solution)/shard_map/ppermute | solution.py:348
  74.7 1.5 collective-permute-done.other_ref
  76.2 0.0 copy-done.9
  76.2 0.0 copy-done.13
  76.2 1.0 copy-done.5
  77.2 6.4 %shard_map.134.image_ref = f32[3,4,128,128]{3,2,1,0:T(8,128)S(1)} custom-call(bf16[160,128]{1,0:T(8,128)(2,1)S(1)} %copy-done.9, bf16[8,208,128]{2,1,0:T(8,128)(2,1)S(1)} %copy-done.5, bf16[8,128,128]{2,1,0:T(8,128)(2,1)S(1)} %collective-permute-done.other_ref, f32[2,128]{1,0:T(2,128)S(1)} %bitcast.29), custom_call_target="tpu_custom_call" | custom-call | tf_op jit(solution)/shard_map/pallas_call | solution.py:29
  83.7 0.0 copy-start.3
  83.7 0.9 copy-done.3
  84.6 3.0 %all-to-all-done.3 = bf16[8,384,128]{2,1,0:T(8,128)(2,1)S(1)} async-done(((bf16[8,384,128]{2,1,0:T(8,128)(2,1)}), bf16[8,384,128]{2,1,0:T(8,128)(2,1)S(1)}, u32[]{:S(2)}, u32[]{:S(2)}) %all-to-all-start.3) | async-done | bytes 786464 | tf_op jit(solution)/shard_map/all_to_all | solution.py:305
  87.6 1.1 copy-done.4
  88.7 1.2 shard_map.135
  89.9 0.0 copy-done
  89.9 0.0 copy-start.1
  89.9 0.0 copy-start.8
  89.9 0.0 copy-start.10
  89.9 0.0 copy-start.12
  90.0 0.6 convolution_convert_fusion
  90.5 0.0 copy-start.2
  90.5 0.0 copy-start.6
  90.6 0.0 copy-start.11
  90.6 16.6 %all_to_all.42.parts_ref = bf16[8,16,3072]{2,1,0:T(8,128)(2,1)S(1)} all-to-all(bf16[8,16,3072]{2,1,0:T(8,128)(2,1)S(1)} %bitcast.30), channel_id=1, replica_groups=mesh['role'=2,'z_far'=4,'z_near'=4,'y_hi'=2,'mp'=8] {'mp'}, dimensions={0} | all-to-all | bytes 1572864 | tf_op jit(solution)/shard_map/all_to_all | solution.py:305
  107.1 0.0 copy-done.1
  107.1 0.0 copy-done.8
  107.1 0.0 copy-done.10
  107.1 0.0 copy-done.12
  107.1 0.6 shard_map.136
  107.8 9.4 %all_to_all.43.both_ref = f32[16,8,128]{2,1,0:T(8,128)S(1)} all-to-all(f32[16,8,128]{2,1,0:T(8,128)S(1)} %shard_map.136), channel_id=1, replica_groups=mesh['role'=2,'z_far'=4,'z_near'=4,'y_hi'=2,'mp'=8] {'role','mp'}, dimensions={0} | all-to-all | bytes 131072 | tf_op jit(solution)/shard_map/all_to_all | solution.py:305
  117.2 0.0 copy-done.2
  117.2 0.0 copy-done.6
  117.2 0.0 copy-done.11
  117.2 0.4 shard_map.137
  117.6 13.8 %all_to_all.44.recv_ref = bf16[8,32,128]{2,1,0:T(8,128)(2,1)S(1)} all-to-all(bf16[8,32,128]{2,1,0:T(8,128)(2,1)S(1)} %get-tuple-element.23), channel_id=1, replica_groups=mesh['role'=2,'z_far'=4,'z_near'=4,'y_hi'=2,'mp'=8] {'z_near','y_hi'}, dimensions={0} | all-to-all | bytes 131072 | tf_op jit(solution)/shard_map/all_to_all | solution.py:305
  131.4 21.7 %all_to_all.45.refs_1_ = bf16[16,32,128]{2,1,0:T(8,128)(2,1)S(1)} all-to-all(bf16[16,32,128]{2,1,0:T(8,128)(2,1)S(1)} %shard_map.138), channel_id=1, replica_groups=mesh['role'=2,'z_far'=4,'z_near'=4,'y_hi'=2,'mp'=8] {'z_far','z_near'}, dimensions={0} | all-to-all | bytes 262144 | tf_op jit(solution)/shard_map/all_to_all | solution.py:305
  153.1 0.9 shard_map.139
  (6 shorter events, 0.0 us)
Async XLA Ops:
  0.6 89.3 %copy-start = (bf16[1,384,3072]{2,1,0:T(8,128)(2,1)S(1)}, bf16[1,384,3072]{2,1,0:T(8,128)(2,1)}, u32[]{:S(2)}) copy-start(bf16[1,384,3072]{2,1,0:T(8,128)(2,1)} %param.20) | copy-start | bytes 7077892
  3.7 17.6 %all-to-all-start = ((bf16[8,80,128]{2,1,0:T(8,128)(2,1)}), bf16[8,80,128]{2,1,0:T(8,128)(2,1)S(1)}, u32[]{:S(2)}, u32[]{:S(2)}) async-start(bf16[8,80,128]{2,1,0:T(8,128)(2,1)} %get-tuple-element.18), calls=%async_computation | async-start | bytes 327680 | tf_op jit(solution)/shard_map/all_to_all | solution.py:305
  16.4 59.8 %copy-start.9 = (bf16[160,128]{1,0:T(8,128)(2,1)S(1)}, bf16[160,128]{1,0:T(8,128)(2,1)}, u32[]{:S(2)}) copy-start(bf16[160,128]{1,0:T(8,128)(2,1)} %get-tuple-element.17.send_ref) | copy-start | bytes 122884
  16.4 59.8 %copy-start.13 = (f32[1,2,128]{2,1,0:T(2,128)S(1)}, f32[1,2,128]{2,1,0:T(2,128)}, u32[]{:S(2)}) copy-start(f32[1,2,128]{2,1,0:T(2,128)} %param.18) | copy-start | bytes 3076
  21.4 0.7 copy-start.14
  52.4 15.8 %copy-start.7 = (bf16[8,384,128]{2,1,0:T(8,128)(2,1)}, bf16[8,384,128]{2,1,0:T(8,128)(2,1)S(1)}, u32[]{:S(2)}) copy-start(bf16[8,384,128]{2,1,0:T(8,128)(2,1)S(1)} %get-tuple-element.20) | copy-start | bytes 2359300
  68.3 19.3 %all-to-all-start.3 = ((bf16[8,384,128]{2,1,0:T(8,128)(2,1)}), bf16[8,384,128]{2,1,0:T(8,128)(2,1)S(1)}, u32[]{:S(2)}, u32[]{:S(2)}) async-start(bf16[8,384,128]{2,1,0:T(8,128)(2,1)} %copy-done.7), calls=%async_computation.3 | async-start | bytes 1572864 | tf_op jit(solution)/shard_map/all_to_all | solution.py:305
  72.8 3.4 %collective-permute-start = (bf16[8,128,128]{2,1,0:T(8,128)(2,1)S(1)}, bf16[8,128,128]{2,1,0:T(8,128)(2,1)S(1)}, u32[]{:S(2)}, u32[]{:S(2)}) collective-permute-start(bf16[8,128,128]{2,1,0:T(8,128)(2,1)S(1)} %slice.4), channel_id=1, source_target_pairs={{0,1},{1,0},{2,3},{3,2},{4,5},{5,4},{6,7},{7,6},{8,9},{9,8},{10,11... | collective-permute-start | bytes 786440 | tf_op jit(solution)/shard_map/ppermute | solution.py:348
  76.2 1.0 copy-start.5
  83.7 0.9 copy-start.3
  87.6 1.1 copy-start.4
  89.9 17.2 %copy-start.1 = (bf16[1,64,3072]{2,1,0:T(8,128)(2,1)S(1)}, bf16[1,64,3072]{2,1,0:T(8,128)(2,1)}, u32[]{:S(2)}) copy-start(bf16[1,64,3072]{2,1,0:T(8,128)(2,1)} %param.15) | copy-start | bytes 1179652
  89.9 17.2 %copy-start.8 = (bf16[1,3072,64]{1,2,0:T(8,128)(2,1)S(1)}, bf16[1,3072,64]{1,2,0:T(8,128)(2,1)}, u32[]{:S(2)}) copy-start(bf16[1,3072,64]{1,2,0:T(8,128)(2,1)} %param.21) | copy-start | bytes 1179652
  89.9 17.2 %copy-start.10 = (f32[1,3,3072]{2,0,1:T(1,128)S(1)}, f32[1,3,3072]{2,0,1:T(1,128)}, u32[]{:S(2)}) copy-start(f32[1,3,3072]{2,0,1:T(1,128)} %param.16) | copy-start | bytes 110596
  89.9 17.2 %copy-start.12 = (f32[128,64]{1,0:T(8,128)S(1)}, f32[128,64]{1,0:T(8,128)}, u32[]{:S(2)}) copy-start(f32[128,64]{1,0:T(8,128)} %get-tuple-element.21.noised_ref) | copy-start | bytes 98308
  90.5 26.6 %copy-start.2 = (bf16[128,3072]{1,0:T(8,128)(2,1)S(1)}, bf16[128,3072]{1,0:T(8,128)(2,1)}, u32[]{:S(2)}) copy-start(bf16[128,3072]{1,0:T(8,128)(2,1)} %hidden_ref.3) | copy-start | bytes 2359300
  90.5 26.6 %copy-start.6 = (bf16[3072,64]{0,1:T(8,128)(2,1)S(1)}, bf16[3072,64]{0,1:T(8,128)(2,1)}, u32[]{:S(2)}) copy-start(bf16[3072,64]{0,1:T(8,128)(2,1)} %param.12) | copy-start | bytes 1179652
  90.6 26.6 %copy-start.11 = (f32[128,64]{1,0:T(8,128)S(1)}, f32[128,64]{1,0:T(8,128)}, u32[]{:S(2)}) copy-start(f32[128,64]{1,0:T(8,128)} %get-tuple-element.22.gap_ref) | copy-start | bytes 98308

commit v4 on v3

--- a/solution.py
+++ b/solution.py
@@ -126,7 +126,7 @@
 
 
 def image_body(
-    send_ref, recv_ref, other_ref, gain_ref, out_ref, lat_ref, s_ref, v_ref, m_ref, own_ref
+    send_ref, recv_ref, other_ref, gain_ref, out_ref, lat_ref, s_ref, v_ref, m_ref, own_ref, sum_ref
 ):
     tokens = lat_ref.shape[1]
     chunk = 1024
@@ -163,7 +163,7 @@
         q_t = dot(weight(head), own)
         q_t = q_t * lax.rsqrt(jnp.mean(q_t * q_t, axis=0, keepdims=True) + 1e-06)
         q = q_t.T * (gain_ref[0:1, :] * score_scale)
-        out_ref[head, 3] = q
+        out_ref[3 + head] = q
         q_image.append((q * gain_ref[1:2, :]).astype(BF16))
         w_k.append(weight(3 + head))
         w_v.append(weight(6 + head))
@@ -186,23 +186,29 @@
         return tuple(out)
 
     tops = lax.fori_loop(0, n_chunks, score_step, (jnp.full((rows, HD), -3e38, F32),) * 3)
+    tops = [jnp.max(top, axis=1, keepdims=True) for top in tops]
     for head in range(3):
-        out_ref[head, 0] = jnp.zeros((rows, HD), F32)
-        out_ref[head, 1] = jnp.zeros((rows, HD), F32)
-        out_ref[head, 2] = jnp.broadcast_to(jnp.max(tops[head], axis=1, keepdims=True), (rows, HD))
+        out_ref[head] = jnp.zeros((rows, HD), F32)
+        sum_ref[head] = jnp.zeros((rows, HD), F32)
 
     def mix_step(c, carry):
         at = pl.ds(pl.multiple_of(c * chunk, chunk), chunk)
         for head in range(3):
-            p = jnp.exp2(s_ref[head, :, at] - out_ref[head, 2][:, 0:1])
-            total = out_ref[head, 1]
+            p = jnp.exp2(s_ref[head, :, at] - tops[head])
+            total = sum_ref[head]
             for j in range(chunk // HD):
                 total = total + p[:, j * HD : (j + 1) * HD]
-            out_ref[head, 1] = total
-            out_ref[head, 0] += dot(p.astype(BF16), v_ref[head, :, at], NT)
+            sum_ref[head] = total
+            out_ref[head] += dot(p.astype(BF16), v_ref[head, :, at], NT)
         return carry
 
     lax.fori_loop(0, n_chunks, mix_step, 0)
+    lane = lax.broadcasted_iota(jnp.int32, (rows, HD), 1)
+    numbers = jnp.zeros((rows, HD), F32)
+    for head in range(3):
+        numbers = jnp.where(lane == head, tops[head], numbers)
+        numbers = jnp.where(lane == 3 + head, jnp.sum(sum_ref[head], axis=1, keepdims=True), numbers)
+    out_ref[6] = numbers
 
 
 def text_body(image_ref, text_ref, att_ref):
@@ -210,13 +216,13 @@
         return text_ref[:, first : first + 16, :].reshape(text_ref.shape[0] * 16, HD)
 
     for head in range(3):
-        s = dot(image_ref[head, 3].astype(BF16), block(head * 16), NT)
-        image_top = image_ref[head, 2]
+        s = dot(image_ref[3 + head].astype(BF16), block(head * 16), NT)
+        image_top = image_ref[6][:, head : head + 1]
         top = jnp.maximum(image_top, jnp.max(s, axis=1, keepdims=True))
         keep = jnp.exp2(image_top - top)
-        p = jnp.exp2(s - top[:, 0:1])
-        acc = image_ref[head, 0] * keep + dot(p.astype(BF16), block(48 + head * 16))
-        total = jnp.sum(image_ref[head, 1] * keep, axis=1, keepdims=True) + jnp.sum(p, axis=1, keepdims=True)
+        p = jnp.exp2(s - top)
+        acc = image_ref[head] * keep + dot(p.astype(BF16), block(48 + head * 16))
+        total = image_ref[6][:, 3 + head : 4 + head] * keep + jnp.sum(p, axis=1, keepdims=True)
         att_ref[:, head * HD : (head + 1) * HD] = (acc / total).astype(BF16)
 
 
@@ -258,47 +264,46 @@
     cols = grad_ref.shape[1]
     hidden = hidden_ref[:, pl.ds(pl.multiple_of(lax.axis_index("mp") * cols, HD), cols)]
     grad_ref[...] = dot(share.astype(BF16), hidden)
-    for p in range(4):
-        terms = [grad_ref[8 * p : 8 * p + 8, g * HD : (g + 1) * HD] for g in range(3)]
-        block = in_parts(jnp.concatenate([*terms, spread], axis=0))
-        for y_hi in range(2):
-            piece_ref[2 * p + y_hi] = block
+    terms = [grad_ref[:, g * HD : (g + 1) * HD] for g in range(3)]
+    block = in_parts(jnp.concatenate([*terms, spread], axis=0))
+    for i in range(piece_ref.shape[0]):
+        piece_ref[i] = block
     feats = raw_ref.shape[1]
     raw_ref[...] = dot(diff.astype(BF16), gen_t_ref[:, pl.ds(pl.multiple_of(lax.axis_index("role") * feats, HD), feats)])
 
 
 def in_parts(block):
-    row = lax.broadcasted_iota(jnp.int32, block.shape, 0)
+    row = lax.broadcasted_iota(jnp.int32, block.shape, 0) - (block.shape[0] - 8)
     high = block.astype(BF16).astype(F32)
     mid = (block - high).astype(BF16).astype(F32)
     low = block - high - mid
-    return jnp.where(row == 25, mid, jnp.where(row == 26, low, high)).astype(BF16)
+    return jnp.where(row == 1, mid, jnp.where(row == 2, low, high)).astype(BF16)
+
+
+def whole_total(ref):
+    total = ref[0].astype(F32)
+    for i in range(1, ref.shape[0]):
+        total = total + ref[i].astype(F32)
+    last = total.shape[0] - 8
+    number = total[last : last + 1, :] + total[last + 1 : last + 2, :] + total[last + 2 : last + 3, :]
+    return total[0:last, :], number
 
 
 def near_body(recv_ref, out_ref):
-    total = recv_ref[0].astype(F32)
-    for i in range(1, recv_ref.shape[0]):
-        total = total + recv_ref[i].astype(F32)
-    number = total[24:25, :] + total[25:26, :] + total[26:27, :]
-    out = in_parts(jnp.concatenate([total[0:24, :], jnp.broadcast_to(number, (8, HD))], axis=0))
+    total, number = whole_total(recv_ref)
+    out = in_parts(jnp.concatenate([total, jnp.broadcast_to(number, (8, HD))], axis=0))
     for i in range(out_ref.shape[0]):
         out_ref[i] = out
 
 
 def last_body(level_ref, recv_ref, share_ref, raw_ref, x_ref, hidden_ref, gen_ref, *, entries):
-    totals = []
-    for p in range(4):
-        total = recv_ref[p].astype(F32)
-        for g in range(1, recv_ref.shape[0] // 4):
-            total = total + recv_ref[4 * g + p].astype(F32)
-        totals.append(total)
-    spread = totals[0][24:25, 0:1] + totals[0][25:26, 0:1] + totals[0][26:27, 0:1]
-    factor = noise_scale_of(level_ref[0], (1, 1)) / (spread / entries + 1e-06)
+    total, number = whole_total(recv_ref)
+    factor = noise_scale_of(level_ref[0], (1, 1)) / (number[:, 0:1] / entries + 1e-06)
     x_ref[...] = share_ref[...] * factor
     hidden_ref[...] = (raw_ref[...] * factor).astype(BF16)
-    for p in range(4):
-        for g in range(3):
-            gen_ref[8 * p : 8 * p + 8, g * HD : (g + 1) * HD] = totals[p][8 * g : 8 * g + 8, :] * factor
+    half = gen_ref.shape[0]
+    for g in range(3):
+        gen_ref[:, g * HD : (g + 1) * HD] = total[g * half : (g + 1) * half, :] * factor
 
 
 def exchange(array, axis):
@@ -336,7 +341,7 @@
         limit=60,
     )
     pieces = exchange(payload, NEAR)
-    pieces = call(far_body, sds((n_far, PIECE + HALF + 96, HD), BF16), (pieces, send), limit=60)
+    pieces = call(far_body, sds((n_far, PIECE + HALF + 96, HD), BF16), (pieces, send))
     pieces = exchange(pieces, "z_far")
     pieces, text = call(
         spread_body,
@@ -349,7 +354,7 @@
 
     image = call(
         image_body,
-        sds((3, 4, rows_here, HD), F32),
+        sds((7, rows_here, HD), F32),
         (send, pieces, other, qk_gain[0]),
         scratch=(
             pltpu.VMEM((MROWS, tokens), BF16),
@@ -357,6 +362,7 @@
             pltpu.VMEM((3, HD, tokens), BF16),
             pltpu.VMEM((8 * PIECE, HD), F32),
             pltpu.VMEM((chans, HD), F32),
+            pltpu.VMEM((3, rows_here, HD), F32),
         ),
     )
     own_rows = rows_here // n_mp
@@ -372,14 +378,14 @@
     half = chans // 2
     grad_piece, share, raw = call(
         grad_body,
-        (sds((8, 32, HD), BF16), sds((half, rows_here), F32), sds((rows_here, width // 2), F32)),
+        (sds((8, 3 * half + 8, HD), BF16), sds((half, rows_here), F32), sds((rows_here, width // 2), F32)),
         (level_index, both, gap, gen_hidden, gen_t),
         scratch=(pltpu.VMEM((chans, rows_here), F32), pltpu.VMEM((half, 3 * HD), F32)),
         smem=1,
     )
     near = exchange(grad_piece, NEAR)
-    near = call(near_body, sds((n_seq // 2, 32, HD), BF16), (near,))
-    everything = exchange(near, ("z_far", "z_near"))
+    near = call(near_body, sds((n_far, 3 * half + 8, HD), BF16), (near,))
+    everything = exchange(near, "z_far")
 
     def last(*refs):
         last_body(*refs, entries=tokens * chans)

time: 155 us -> 154 us (level)
  the two profiles are of different devices: /device:TPU:2 before, /device:TPU:64 now
where the time goes in v4:
time: 154 us; the launch traced here: 153 us
  blocking collectives  108 us (70%)
  Pallas kernels  16.1 us (10%)
  starting transfers between devices  15.9 us (10%)
  waiting for transfers between devices  6.31 us (4%)
  local copies, waits for them, and re-layouts  4.62 us (3%)
  between operations  1.58 us (1%)
    all_to_all x6, blocking collectives, exchange(): return lax.all_to_all(array, axis, 0, 0, tiled=True)  108 us
    pallas_call x10, Pallas kernels, call(): pl.pallas_call(body, out_shape=out_shape, in_specs=[scalars if i < smem e...  16.1 us
    all_to_all x2, starting transfers between devices, exchange(): return lax.all_to_all(array, axis, 0, 0, tiled=True)  13.9 us
    all_to_all x2, waiting for transfers between devices, exchange(): return lax.all_to_all(array, axis, 0, 0, tiled=True)  4.81 us
    unnamed x30, local copies, waits for them, and re-layouts  3.65 us
  transfers between devices with their start and end apart: 3, of which 3 were waited for; matrix products, arithmetic and copies ran while one was open for 1% of the time, Pallas kernels for 7%

profile of v4, /device:TPU:64, one launch (start us, length us, event | category | flops | bytes accessed | tf_op | source)
XLA Modules:
  0.0 153.1 jit_solution(1574569264036617141)
XLA Ops:
  0.6 0.0 copy-start
  1.4 2.3 %shard_map.130 = (bf16[8,80,128]{2,1,0:T(8,128)(2,1)}, s32[1]{0:T(128)}) custom-call(s32[1]{0:T(128)S(6)} %copy.14.level_ref.refs_0_, bf16[64,3072]{1,0:T(8,128)(2,1)} %bitcast.20, f32[3,1,3072]{2,1,0:T(1,128)} %bitcast.27, bf16[3,96,384]{2,1,0:T(8,128)(2,1)} %bitcast.31), custom_call_target="tpu_custom_call" | custom-call | tf_op jit(solution)/shard_map/pallas_call | solution.py:29
  3.7 8.4 %all-to-all-start = ((bf16[8,80,128]{2,1,0:T(8,128)(2,1)}), bf16[8,80,128]{2,1,0:T(8,128)(2,1)S(1)}, u32[]{:S(2)}, u32[]{:S(2)}) async-start(bf16[8,80,128]{2,1,0:T(8,128)(2,1)} %get-tuple-element.18), calls=%async_computation | async-start | bytes 327680 | tf_op jit(solution)/shard_map/all_to_all | solution.py:310
  12.1 4.1 %shard_map.131 = (f32[128,64]{1,0:T(8,128)}, f32[128,64]{1,0:T(8,128)}, bf16[160,128]{1,0:T(8,128)(2,1)}) custom-call(s32[1]{0:T(128)} %get-tuple-element.16.level_ref, bf16[128,3072]{1,0:T(8,128)(2,1)} %hidden_ref.3, bf16[64,3072]{1,0:T(8,128)(2,1)} %bitcast.24, bf16[64,128]{1,0:T(8,128)(2,1)} %bitcast.33, bf16[64,3072]{1,0:T(8,128)(2,1)} %bitcast.21, ...), custom_call_target="tpu_custom_call" | custom-call | tf_op jit(solution)/shard_map/pallas_call | solution.py:29
  16.2 0.0 copy-start.14
  16.2 2.5 %all-to-all-done.recv_ref = bf16[8,80,128]{2,1,0:T(8,128)(2,1)S(1)} async-done(((bf16[8,80,128]{2,1,0:T(8,128)(2,1)}), bf16[8,80,128]{2,1,0:T(8,128)(2,1)S(1)}, u32[]{:S(2)}, u32[]{:S(2)}) %all-to-all-start) | async-done | bytes 163872 | tf_op jit(solution)/shard_map/all_to_all | solution.py:310
  18.7 0.8 copy-done.9
  19.5 28.1 %all_to_all.40.recv_ref = bf16[4,208,128]{2,1,0:T(8,128)(2,1)S(1)} all-to-all(bf16[4,208,128]{2,1,0:T(8,128)(2,1)S(1)} %shard_map.132), channel_id=1, replica_groups=mesh['role'=2,'z_far'=4,'z_near'=4,'y_hi'=2,'mp'=8] {'z_far'}, dimensions={0} | all-to-all | bytes 425984 | tf_op jit(solution)/shard_map/all_to_all | solution.py:310
  47.7 0.1 shard_map.133
  47.8 0.0 copy-start.7
  47.8 16.3 %all_to_all.41.recv_ref = bf16[8,208,128]{2,1,0:T(8,128)(2,1)} all-to-all(bf16[8,208,128]{2,1,0:T(8,128)(2,1)S(1)} %get-tuple-element.19), channel_id=1, replica_groups=mesh['role'=2,'z_far'=4,'z_near'=4,'y_hi'=2,'mp'=8] {'z_near','y_hi'}, dimensions={0} | all-to-all | bytes 851968 | tf_op jit(solution)/shard_map/all_to_all | solution.py:310
  64.1 0.0 copy-done.7
  64.1 5.6 %all-to-all-start.3 = ((bf16[8,384,128]{2,1,0:T(8,128)(2,1)}), bf16[8,384,128]{2,1,0:T(8,128)(2,1)S(1)}, u32[]{:S(2)}, u32[]{:S(2)}) async-start(bf16[8,384,128]{2,1,0:T(8,128)(2,1)} %copy-done.7), calls=%async_computation.3 | async-start | bytes 1572864 | tf_op jit(solution)/shard_map/all_to_all | solution.py:310
  69.7 1.0 slice.4
  70.7 1.9 %collective-permute-start = (bf16[8,128,128]{2,1,0:T(8,128)(2,1)S(1)}, bf16[8,128,128]{2,1,0:T(8,128)(2,1)S(1)}, u32[]{:S(2)}, u32[]{:S(2)}) collective-permute-start(bf16[8,128,128]{2,1,0:T(8,128)(2,1)S(1)} %slice.4), channel_id=1, source_target_pairs={{0,1},{1,0},{2,3},{3,2},{4,5},{5,4},{6,7},{7,6},{8,9},{9,8},{10,11... | collective-permute-start | bytes 786440 | tf_op jit(solution)/shard_map/ppermute | solution.py:353
  72.6 1.5 collective-permute-done.other_ref
  74.1 0.0 copy-done.14
  74.1 0.0 copy-done.10
  74.1 1.0 copy-done.3
  75.1 6.2 %shard_map.134.image_ref = f32[7,128,128]{2,1,0:T(8,128)S(1)} custom-call(bf16[160,128]{1,0:T(8,128)(2,1)S(1)} %copy-done.10, bf16[8,208,128]{2,1,0:T(8,128)(2,1)S(1)} %copy-done.3, bf16[8,128,128]{2,1,0:T(8,128)(2,1)S(1)} %collective-permute-done.other_ref, f32[2,128]{1,0:T(2,128)S(1)} %bitcast.29), custom_call_target="tpu_custom_call" | custom-call | tf_op jit(solution)/shard_map/pallas_call | solution.py:29
  81.4 0.0 copy-start.4
  81.4 0.8 copy-done.4
  82.2 2.3 %all-to-all-done.3 = bf16[8,384,128]{2,1,0:T(8,128)(2,1)S(1)} async-done(((bf16[8,384,128]{2,1,0:T(8,128)(2,1)}), bf16[8,384,128]{2,1,0:T(8,128)(2,1)S(1)}, u32[]{:S(2)}, u32[]{:S(2)}) %all-to-all-start.3) | async-done | bytes 786464 | tf_op jit(solution)/shard_map/all_to_all | solution.py:310
  84.5 1.0 copy-done.5
  85.5 1.3 shard_map.135
  86.8 0.0 copy-done
  86.8 0.0 copy-start.1
  86.8 0.0 copy-start.8
  86.8 0.0 copy-start.11
  86.8 0.0 copy-start.13
  86.8 0.6 convolution_convert_fusion
  87.4 0.0 copy-start.2
  87.4 0.0 copy-start.6
  87.4 0.0 copy-start.12
  87.4 17.5 %all_to_all.42.parts_ref = bf16[8,16,3072]{2,1,0:T(8,128)(2,1)S(1)} all-to-all(bf16[8,16,3072]{2,1,0:T(8,128)(2,1)S(1)} %bitcast.30), channel_id=1, replica_groups=mesh['role'=2,'z_far'=4,'z_near'=4,'y_hi'=2,'mp'=8] {'mp'}, dimensions={0} | all-to-all | bytes 1572864 | tf_op jit(solution)/shard_map/all_to_all | solution.py:310
  104.9 0.0 copy-done.1
  104.9 0.0 copy-done.8
  104.9 0.0 copy-done.11
  104.9 0.0 copy-done.13
  104.9 0.6 shard_map.136
  105.6 9.4 %all_to_all.43.both_ref = f32[16,8,128]{2,1,0:T(8,128)S(1)} all-to-all(f32[16,8,128]{2,1,0:T(8,128)S(1)} %shard_map.136), channel_id=1, replica_groups=mesh['role'=2,'z_far'=4,'z_near'=4,'y_hi'=2,'mp'=8] {'role','mp'}, dimensions={0} | all-to-all | bytes 131072 | tf_op jit(solution)/shard_map/all_to_all | solution.py:310
  114.9 0.0 copy-done.2
  114.9 0.0 copy-done.6
  114.9 0.0 copy-done.12
  114.9 0.4 shard_map.137
  115.3 14.4 %all_to_all.44.recv_ref = bf16[8,104,128]{2,1,0:T(8,128)(2,1)S(1)} all-to-all(bf16[8,104,128]{2,1,0:T(8,128)(2,1)S(1)} %get-tuple-element.23), channel_id=1, replica_groups=mesh['role'=2,'z_far'=4,'z_near'=4,'y_hi'=2,'mp'=8] {'z_near','y_hi'}, dimensions={0} | all-to-all | bytes 425984 | tf_op jit(solution)/shard_map/all_to_all | solution.py:310
  129.8 22.5 %all_to_all.45.refs_1_ = bf16[4,104,128]{2,1,0:T(8,128)(2,1)S(1)} all-to-all(bf16[4,104,128]{2,1,0:T(8,128)(2,1)S(1)} %shard_map.138), channel_id=1, replica_groups=mesh['role'=2,'z_far'=4,'z_near'=4,'y_hi'=2,'mp'=8] {'z_far'}, dimensions={0} | all-to-all | bytes 212992 | tf_op jit(solution)/shard_map/all_to_all | solution.py:310
  152.3 0.9 shard_map.139
  (6 shorter events, 0.1 us)
Async XLA Ops:
  0.6 86.1 %copy-start = (bf16[1,384,3072]{2,1,0:T(8,128)(2,1)S(1)}, bf16[1,384,3072]{2,1,0:T(8,128)(2,1)}, u32[]{:S(2)}) copy-start(bf16[1,384,3072]{2,1,0:T(8,128)(2,1)} %param.20) | copy-start | bytes 7077892
  3.7 15.0 %all-to-all-start = ((bf16[8,80,128]{2,1,0:T(8,128)(2,1)}), bf16[8,80,128]{2,1,0:T(8,128)(2,1)S(1)}, u32[]{:S(2)}, u32[]{:S(2)}) async-start(bf16[8,80,128]{2,1,0:T(8,128)(2,1)} %get-tuple-element.18), calls=%async_computation | async-start | bytes 327680 | tf_op jit(solution)/shard_map/all_to_all | solution.py:310
  16.2 57.9 %copy-start.14 = (f32[1,2,128]{2,1,0:T(2,128)S(1)}, f32[1,2,128]{2,1,0:T(2,128)}, u32[]{:S(2)}) copy-start(f32[1,2,128]{2,1,0:T(2,128)} %param.18) | copy-start | bytes 3076
  18.7 0.8 copy-start.9
  19.5 54.6 %copy-start.10 = (bf16[160,128]{1,0:T(8,128)(2,1)S(1)}, bf16[160,128]{1,0:T(8,128)(2,1)}, u32[]{:S(2)}) copy-start(bf16[160,128]{1,0:T(8,128)(2,1)} %get-tuple-element.17.send_ref) | copy-start | bytes 122884
  47.8 16.3 %copy-start.7 = (bf16[8,384,128]{2,1,0:T(8,128)(2,1)}, bf16[8,384,128]{2,1,0:T(8,128)(2,1)S(1)}, u32[]{:S(2)}) copy-start(bf16[8,384,128]{2,1,0:T(8,128)(2,1)S(1)} %get-tuple-element.20) | copy-start | bytes 2359300
  64.1 20.3 %all-to-all-start.3 = ((bf16[8,384,128]{2,1,0:T(8,128)(2,1)}), bf16[8,384,128]{2,1,0:T(8,128)(2,1)S(1)}, u32[]{:S(2)}, u32[]{:S(2)}) async-start(bf16[8,384,128]{2,1,0:T(8,128)(2,1)} %copy-done.7), calls=%async_computation.3 | async-start | bytes 1572864 | tf_op jit(solution)/shard_map/all_to_all | solution.py:310
  70.7 3.4 %collective-permute-start = (bf16[8,128,128]{2,1,0:T(8,128)(2,1)S(1)}, bf16[8,128,128]{2,1,0:T(8,128)(2,1)S(1)}, u32[]{:S(2)}, u32[]{:S(2)}) collective-permute-start(bf16[8,128,128]{2,1,0:T(8,128)(2,1)S(1)} %slice.4), channel_id=1, source_target_pairs={{0,1},{1,0},{2,3},{3,2},{4,5},{5,4},{6,7},{7,6},{8,9},{9,8},{10,11... | collective-permute-start | bytes 786440 | tf_op jit(solution)/shard_map/ppermute | solution.py:353
  74.1 1.0 copy-start.3
  81.4 0.8 copy-start.4
  84.5 1.0 copy-start.5
  86.8 18.1 %copy-start.1 = (bf16[1,64,3072]{2,1,0:T(8,128)(2,1)S(1)}, bf16[1,64,3072]{2,1,0:T(8,128)(2,1)}, u32[]{:S(2)}) copy-start(bf16[1,64,3072]{2,1,0:T(8,128)(2,1)} %param.15) | copy-start | bytes 1179652
  86.8 18.1 %copy-start.8 = (bf16[1,3072,64]{1,2,0:T(8,128)(2,1)S(1)}, bf16[1,3072,64]{1,2,0:T(8,128)(2,1)}, u32[]{:S(2)}) copy-start(bf16[1,3072,64]{1,2,0:T(8,128)(2,1)} %param.21) | copy-start | bytes 1179652
  86.8 18.1 %copy-start.11 = (f32[1,3,3072]{2,0,1:T(1,128)S(1)}, f32[1,3,3072]{2,0,1:T(1,128)}, u32[]{:S(2)}) copy-start(f32[1,3,3072]{2,0,1:T(1,128)} %param.16) | copy-start | bytes 110596
  86.8 18.1 %copy-start.13 = (f32[128,64]{1,0:T(8,128)S(1)}, f32[128,64]{1,0:T(8,128)}, u32[]{:S(2)}) copy-start(f32[128,64]{1,0:T(8,128)} %get-tuple-element.21.noised_ref) | copy-start | bytes 98308
  87.4 27.5 %copy-start.2 = (bf16[128,3072]{1,0:T(8,128)(2,1)S(1)}, bf16[128,3072]{1,0:T(8,128)(2,1)}, u32[]{:S(2)}) copy-start(bf16[128,3072]{1,0:T(8,128)(2,1)} %hidden_ref.3) | copy-start | bytes 2359300
  87.4 27.5 %copy-start.6 = (bf16[3072,64]{0,1:T(8,128)(2,1)S(1)}, bf16[3072,64]{0,1:T(8,128)(2,1)}, u32[]{:S(2)}) copy-start(bf16[3072,64]{0,1:T(8,128)(2,1)} %param.12) | copy-start | bytes 1179652
  87.4 27.5 %copy-start.12 = (f32[128,64]{1,0:T(8,128)S(1)}, f32[128,64]{1,0:T(8,128)}, u32[]{:S(2)}) copy-start(f32[128,64]{1,0:T(8,128)} %get-tuple-element.22.gap_ref) | copy-start | bytes 98308

commit v5 on v4

--- a/solution.py
+++ b/solution.py
@@ -45,7 +45,7 @@
     return 3.0 * time_frac / (1.0 + 2.0 * time_frac)
 
 
-def weight_body(level_ref, embed_ref, mod_ref, qkv_ref, payload_ref, level_out_ref, term_ref):
+def weight_body(embed_ref, mod_ref, qkv_ref, payload_ref, order_ref, term_ref):
     width = embed_ref.shape[1]
     features = qkv_ref.shape[1]
     offset = seq_here() * features
@@ -76,11 +76,11 @@
     term_ref[9 * CHANS + 9 :, :] = jnp.zeros((term_ref.shape[0] - 9 * CHANS - 9, HD), F32)
     for p in range(payload_ref.shape[0]):
         payload_ref[p] = term_ref[p * PIECE : (p + 1) * PIECE, :].astype(BF16)
-    level_out_ref[0] = level_ref[0]
+    order_ref[0] = 0
 
 
 def latent_body(
-    level_ref, hidden_ref, gen_t_ref, noise_t_ref, embed_ref, text_in_ref, noised_ref, gap_ref, send_ref
+    level_ref, _, hidden_ref, gen_t_ref, noise_t_ref, embed_ref, text_in_ref, noised_ref, gap_ref, send_ref
 ):
     x_t = dot(gen_t_ref[...], hidden_ref[...], NT)
     noise_scale = noise_scale_of(level_ref[0], x_t.shape)
@@ -88,10 +88,21 @@
     noised = noised_t.astype(F32).T
     noised_ref[...] = noised
     gap_ref[...] = (x_t - noised_t.astype(F32)).T
-    h = dot(noised.astype(BF16), embed_ref[...])
-    width = h.shape[1]
-    row_mean = jnp.sum(h, axis=1, keepdims=True) / width
-    row_var = jnp.sum(jnp.square(h - row_mean), axis=1, keepdims=True) / width
+    width = embed_ref.shape[1]
+    step = 512
+    embed_mean = jnp.zeros((embed_ref.shape[0], HD), F32)
+    for j in range(width // HD):
+        embed_mean = embed_mean + embed_ref[:, j * HD : (j + 1) * HD].astype(F32)
+    embed_mean = jnp.sum(embed_mean, axis=1, keepdims=True) / width
+    row_mean = jnp.sum(noised_t.astype(F32) * embed_mean, axis=0, keepdims=True)
+    row_mean = jnp.broadcast_to(row_mean, (HD, noised.shape[0])).T
+    row_var = jnp.zeros(row_mean.shape, F32)
+    noised_b = noised.astype(BF16)
+    for j in range(width // step):
+        h = dot(noised_b, embed_ref[:, j * step : (j + 1) * step])
+        for k in range(step // HD):
+            row_var = row_var + jnp.square(h[:, k * HD : (k + 1) * HD] - row_mean)
+    row_var = jnp.sum(row_var, axis=1, keepdims=True) / width
     send_ref[0:CHANS, :] = (noised * lax.rsqrt(row_var + 1e-06)).T.astype(BF16)
     text = text_in_ref[...].astype(F32)
     for j in range(6):
@@ -321,12 +332,11 @@
     mods = jnp.transpose(modulation, (1, 0, 2))
     embed = w_embed[0]
     gen_t = w_gen.T
-    payload, level_late = call(
+    payload, order = call(
         weight_body,
         (sds((8, PIECE, HD), BF16), sds((1,), jnp.int32)),
-        (level_index, embed, mods, jnp.transpose(w_qkv[0], (1, 0, 2))),
+        (embed, mods, jnp.transpose(w_qkv[0], (1, 0, 2))),
         scratch=(pltpu.VMEM((8 * PIECE, HD), F32),),
-        smem=1,
         limit=60,
     )
     noised, gap, send = call(
@@ -336,8 +346,8 @@
             sds((rows_here, chans), F32),
             sds((chans + 96, HD), BF16),
         ),
-        (level_late, gen_hidden, gen_t, noise_latent.T, embed, text_kv[0]),
-        smem=1,
+        (level_index, order, gen_hidden, gen_t, noise_latent.T, embed, text_kv[0]),
+        smem=2,
         limit=60,
     )
     pieces = exchange(payload, NEAR)

time: 154 us -> 153 us (level)
  waiting for transfers between devices: 6.31 us -> 8.5 us
  blocking collectives: 108 us -> 106 us
    all_to_all x6, blocking collectives: 108 us -> 106 us  [exchange(): return lax.all_to_all(array, axis, 0, 0, tiled=True)]
    all_to_all x2, waiting for transfers between devices: 4.81 us -> 7 us  [exchange(): return lax.all_to_all(array, axis, 0, 0, tiled=True)]
where the time goes in v5:
time: 153 us
  blocking collectives  106 us (69%)
  Pallas kernels  16 us (10%)
  starting transfers between devices  15.7 us (10%)
  waiting for transfers between devices  8.5 us (6%)
  local copies, waits for them, and re-layouts  4.62 us (3%)
    all_to_all x6, blocking collectives, exchange(): return lax.all_to_all(array, axis, 0, 0, tiled=True)  106 us
    pallas_call x10, Pallas kernels, call(): pl.pallas_call(body, out_shape=out_shape, in_specs=[scalars if i < smem e...  16 us
    all_to_all x2, starting transfers between devices, exchange(): return lax.all_to_all(array, axis, 0, 0, tiled=True)  13.7 us
    all_to_all x2, waiting for transfers between devices, exchange(): return lax.all_to_all(array, axis, 0, 0, tiled=True)  7 us
    unnamed x30, local copies, waits for them, and re-layouts  3.65 us
  transfers between devices with their start and end apart: 3, of which 3 were waited for; matrix products, arithmetic and copies ran while one was open for 1% of the time, Pallas kernels for 7%

profile of v5, /device:TPU:64, one launch (start us, length us, event | category | flops | bytes accessed | tf_op | source)
XLA Modules:
  0.0 152.7 jit_solution(13970030371225050688)
XLA Ops:
  0.6 0.0 copy-start
  0.6 2.4 %shard_map.130 = (bf16[8,80,128]{2,1,0:T(8,128)(2,1)}, s32[1]{0:T(128)}) custom-call(bf16[64,3072]{1,0:T(8,128)(2,1)} %bitcast.20, f32[3,1,3072]{2,1,0:T(1,128)} %bitcast.27, bf16[3,96,384]{2,1,0:T(8,128)(2,1)} %bitcast.31), custom_call_target="tpu_custom_call" | custom-call | tf_op jit(solution)/shard_map/pallas_call | solution.py:29
  3.1 8.4 %all-to-all-start = ((bf16[8,80,128]{2,1,0:T(8,128)(2,1)}), bf16[8,80,128]{2,1,0:T(8,128)(2,1)S(1)}, u32[]{:S(2)}, u32[]{:S(2)}) async-start(bf16[8,80,128]{2,1,0:T(8,128)(2,1)} %get-tuple-element.18), calls=%async_computation | async-start | bytes 327680 | tf_op jit(solution)/shard_map/all_to_all | solution.py:321
  12.1 3.9 %shard_map.131 = (f32[128,64]{1,0:T(8,128)}, f32[128,64]{1,0:T(8,128)}, bf16[160,128]{1,0:T(8,128)(2,1)}) custom-call(s32[1]{0:T(128)S(6)} %copy.14.level_ref.refs_0_, s32[1]{0:T(128)} %get-tuple-element.16._, bf16[128,3072]{1,0:T(8,128)(2,1)} %hidden_ref.3, bf16[64,3072]{1,0:T(8,128)(2,1)} %bitcast.24, bf16[64,128]{1,0:T(8,128)(2,1)} %bitcast.33, ...), custom_call_target="tpu_custom_call" | custom-call | tf_op jit(solution)/shard_map/pallas_call | solution.py:29
  16.0 0.0 copy-start.14
  16.0 2.1 %all-to-all-done.recv_ref = bf16[8,80,128]{2,1,0:T(8,128)(2,1)S(1)} async-done(((bf16[8,80,128]{2,1,0:T(8,128)(2,1)}), bf16[8,80,128]{2,1,0:T(8,128)(2,1)S(1)}, u32[]{:S(2)}, u32[]{:S(2)}) %all-to-all-start) | async-done | bytes 163872 | tf_op jit(solution)/shard_map/all_to_all | solution.py:321
  18.1 0.8 copy-done.9
  18.9 28.2 %all_to_all.40.recv_ref = bf16[4,208,128]{2,1,0:T(8,128)(2,1)S(1)} all-to-all(bf16[4,208,128]{2,1,0:T(8,128)(2,1)S(1)} %shard_map.132), channel_id=1, replica_groups=mesh['role'=2,'z_far'=4,'z_near'=4,'y_hi'=2,'mp'=8] {'z_far'}, dimensions={0} | all-to-all | bytes 425984 | tf_op jit(solution)/shard_map/all_to_all | solution.py:321
  47.0 0.1 shard_map.133
  47.2 0.0 copy-start.7
  47.2 18.4 %all_to_all.41.recv_ref = bf16[8,208,128]{2,1,0:T(8,128)(2,1)} all-to-all(bf16[8,208,128]{2,1,0:T(8,128)(2,1)S(1)} %get-tuple-element.19), channel_id=1, replica_groups=mesh['role'=2,'z_far'=4,'z_near'=4,'y_hi'=2,'mp'=8] {'z_near','y_hi'}, dimensions={0} | all-to-all | bytes 851968 | tf_op jit(solution)/shard_map/all_to_all | solution.py:321
  65.6 0.0 copy-done.7
  65.6 5.4 %all-to-all-start.3 = ((bf16[8,384,128]{2,1,0:T(8,128)(2,1)}), bf16[8,384,128]{2,1,0:T(8,128)(2,1)S(1)}, u32[]{:S(2)}, u32[]{:S(2)}) async-start(bf16[8,384,128]{2,1,0:T(8,128)(2,1)} %copy-done.7), calls=%async_computation.3 | async-start | bytes 1572864 | tf_op jit(solution)/shard_map/all_to_all | solution.py:321
  71.0 1.0 slice.4
  72.0 1.9 %collective-permute-start = (bf16[8,128,128]{2,1,0:T(8,128)(2,1)S(1)}, bf16[8,128,128]{2,1,0:T(8,128)(2,1)S(1)}, u32[]{:S(2)}, u32[]{:S(2)}) collective-permute-start(bf16[8,128,128]{2,1,0:T(8,128)(2,1)S(1)} %slice.4), channel_id=1, source_target_pairs={{0,1},{1,0},{2,3},{3,2},{4,5},{5,4},{6,7},{7,6},{8,9},{9,8},{10,11... | collective-permute-start | bytes 786440 | tf_op jit(solution)/shard_map/ppermute | solution.py:363
  73.9 1.5 collective-permute-done.other_ref
  75.4 0.0 copy-done.14
  75.4 0.0 copy-done.10
  75.4 1.0 copy-done.3
  76.4 6.2 %shard_map.134.image_ref = f32[7,128,128]{2,1,0:T(8,128)S(1)} custom-call(bf16[160,128]{1,0:T(8,128)(2,1)S(1)} %copy-done.10, bf16[8,208,128]{2,1,0:T(8,128)(2,1)S(1)} %copy-done.3, bf16[8,128,128]{2,1,0:T(8,128)(2,1)S(1)} %collective-permute-done.other_ref, f32[2,128]{1,0:T(2,128)S(1)} %bitcast.29), custom_call_target="tpu_custom_call" | custom-call | tf_op jit(solution)/shard_map/pallas_call | solution.py:29
  82.7 0.0 copy-start.4
  82.7 0.8 copy-done.4
  83.5 4.9 %all-to-all-done.3 = bf16[8,384,128]{2,1,0:T(8,128)(2,1)S(1)} async-done(((bf16[8,384,128]{2,1,0:T(8,128)(2,1)}), bf16[8,384,128]{2,1,0:T(8,128)(2,1)S(1)}, u32[]{:S(2)}, u32[]{:S(2)}) %all-to-all-start.3) | async-done | bytes 786464 | tf_op jit(solution)/shard_map/all_to_all | solution.py:321
  88.4 1.0 copy-done.5
  89.4 1.3 shard_map.135
  90.7 0.0 copy-done
  90.7 0.0 copy-start.1
  90.8 0.0 copy-start.8
  90.8 0.0 copy-start.11
  90.8 0.0 copy-start.13
  90.8 0.6 convolution_convert_fusion
  91.4 0.0 copy-start.2
  91.4 0.0 copy-start.6
  91.4 0.0 copy-start.12
  91.4 15.8 %all_to_all.42.parts_ref = bf16[8,16,3072]{2,1,0:T(8,128)(2,1)S(1)} all-to-all(bf16[8,16,3072]{2,1,0:T(8,128)(2,1)S(1)} %bitcast.30), channel_id=1, replica_groups=mesh['role'=2,'z_far'=4,'z_near'=4,'y_hi'=2,'mp'=8] {'mp'}, dimensions={0} | all-to-all | bytes 1572864 | tf_op jit(solution)/shard_map/all_to_all | solution.py:321
  107.2 0.0 copy-done.1
  107.2 0.0 copy-done.8
  107.2 0.0 copy-done.11
  107.2 0.0 copy-done.13
  107.2 0.6 shard_map.136
  107.9 8.7 %all_to_all.43.both_ref = f32[16,8,128]{2,1,0:T(8,128)S(1)} all-to-all(f32[16,8,128]{2,1,0:T(8,128)S(1)} %shard_map.136), channel_id=1, replica_groups=mesh['role'=2,'z_far'=4,'z_near'=4,'y_hi'=2,'mp'=8] {'role','mp'}, dimensions={0} | all-to-all | bytes 131072 | tf_op jit(solution)/shard_map/all_to_all | solution.py:321
  116.5 0.0 copy-done.2
  116.5 0.0 copy-done.6
  116.6 0.0 copy-done.12
  116.6 0.4 shard_map.137
  117.0 15.2 %all_to_all.44.recv_ref = bf16[8,104,128]{2,1,0:T(8,128)(2,1)S(1)} all-to-all(bf16[8,104,128]{2,1,0:T(8,128)(2,1)S(1)} %get-tuple-element.23), channel_id=1, replica_groups=mesh['role'=2,'z_far'=4,'z_near'=4,'y_hi'=2,'mp'=8] {'z_near','y_hi'}, dimensions={0} | all-to-all | bytes 425984 | tf_op jit(solution)/shard_map/all_to_all | solution.py:321
  132.2 19.6 %all_to_all.45.refs_1_ = bf16[4,104,128]{2,1,0:T(8,128)(2,1)S(1)} all-to-all(bf16[4,104,128]{2,1,0:T(8,128)(2,1)S(1)} %shard_map.138), channel_id=1, replica_groups=mesh['role'=2,'z_far'=4,'z_near'=4,'y_hi'=2,'mp'=8] {'z_far'}, dimensions={0} | all-to-all | bytes 212992 | tf_op jit(solution)/shard_map/all_to_all | solution.py:321
  151.8 0.9 shard_map.139
  (6 shorter events, 0.1 us)
Async XLA Ops:
  0.6 90.1 %copy-start = (bf16[1,384,3072]{2,1,0:T(8,128)(2,1)S(1)}, bf16[1,384,3072]{2,1,0:T(8,128)(2,1)}, u32[]{:S(2)}) copy-start(bf16[1,384,3072]{2,1,0:T(8,128)(2,1)} %param.20) | copy-start | bytes 7077892
  3.1 15.0 %all-to-all-start = ((bf16[8,80,128]{2,1,0:T(8,128)(2,1)}), bf16[8,80,128]{2,1,0:T(8,128)(2,1)S(1)}, u32[]{:S(2)}, u32[]{:S(2)}) async-start(bf16[8,80,128]{2,1,0:T(8,128)(2,1)} %get-tuple-element.18), calls=%async_computation | async-start | bytes 327680 | tf_op jit(solution)/shard_map/all_to_all | solution.py:321
  16.0 59.4 %copy-start.14 = (f32[1,2,128]{2,1,0:T(2,128)S(1)}, f32[1,2,128]{2,1,0:T(2,128)}, u32[]{:S(2)}) copy-start(f32[1,2,128]{2,1,0:T(2,128)} %param.18) | copy-start | bytes 3076
  18.1 0.8 copy-start.9
  18.9 56.6 %copy-start.10 = (bf16[160,128]{1,0:T(8,128)(2,1)S(1)}, bf16[160,128]{1,0:T(8,128)(2,1)}, u32[]{:S(2)}) copy-start(bf16[160,128]{1,0:T(8,128)(2,1)} %get-tuple-element.17.send_ref) | copy-start | bytes 122884
  47.2 18.4 %copy-start.7 = (bf16[8,384,128]{2,1,0:T(8,128)(2,1)}, bf16[8,384,128]{2,1,0:T(8,128)(2,1)S(1)}, u32[]{:S(2)}) copy-start(bf16[8,384,128]{2,1,0:T(8,128)(2,1)S(1)} %get-tuple-element.20) | copy-start | bytes 2359300
  65.6 22.8 %all-to-all-start.3 = ((bf16[8,384,128]{2,1,0:T(8,128)(2,1)}), bf16[8,384,128]{2,1,0:T(8,128)(2,1)S(1)}, u32[]{:S(2)}, u32[]{:S(2)}) async-start(bf16[8,384,128]{2,1,0:T(8,128)(2,1)} %copy-done.7), calls=%async_computation.3 | async-start | bytes 1572864 | tf_op jit(solution)/shard_map/all_to_all | solution.py:321
  72.0 3.4 %collective-permute-start = (bf16[8,128,128]{2,1,0:T(8,128)(2,1)S(1)}, bf16[8,128,128]{2,1,0:T(8,128)(2,1)S(1)}, u32[]{:S(2)}, u32[]{:S(2)}) collective-permute-start(bf16[8,128,128]{2,1,0:T(8,128)(2,1)S(1)} %slice.4), channel_id=1, source_target_pairs={{0,1},{1,0},{2,3},{3,2},{4,5},{5,4},{6,7},{7,6},{8,9},{9,8},{10,11... | collective-permute-start | bytes 786440 | tf_op jit(solution)/shard_map/ppermute | solution.py:363
  75.4 1.0 copy-start.3
  82.7 0.8 copy-start.4
  88.4 1.0 copy-start.5
  90.7 16.5 %copy-start.1 = (bf16[1,64,3072]{2,1,0:T(8,128)(2,1)S(1)}, bf16[1,64,3072]{2,1,0:T(8,128)(2,1)}, u32[]{:S(2)}) copy-start(bf16[1,64,3072]{2,1,0:T(8,128)(2,1)} %param.15) | copy-start | bytes 1179652
  90.8 16.5 %copy-start.8 = (bf16[1,3072,64]{1,2,0:T(8,128)(2,1)S(1)}, bf16[1,3072,64]{1,2,0:T(8,128)(2,1)}, u32[]{:S(2)}) copy-start(bf16[1,3072,64]{1,2,0:T(8,128)(2,1)} %param.21) | copy-start | bytes 1179652
  90.8 16.4 %copy-start.11 = (f32[1,3,3072]{2,0,1:T(1,128)S(1)}, f32[1,3,3072]{2,0,1:T(1,128)}, u32[]{:S(2)}) copy-start(f32[1,3,3072]{2,0,1:T(1,128)} %param.16) | copy-start | bytes 110596
  90.8 16.4 %copy-start.13 = (f32[128,64]{1,0:T(8,128)S(1)}, f32[128,64]{1,0:T(8,128)}, u32[]{:S(2)}) copy-start(f32[128,64]{1,0:T(8,128)} %get-tuple-element.21.noised_ref) | copy-start | bytes 98308
  91.4 25.2 %copy-start.2 = (bf16[128,3072]{1,0:T(8,128)(2,1)S(1)}, bf16[128,3072]{1,0:T(8,128)(2,1)}, u32[]{:S(2)}) copy-start(bf16[128,3072]{1,0:T(8,128)(2,1)} %hidden_ref.3) | copy-start | bytes 2359300
  91.4 25.2 %copy-start.6 = (bf16[3072,64]{0,1:T(8,128)(2,1)S(1)}, bf16[3072,64]{0,1:T(8,128)(2,1)}, u32[]{:S(2)}) copy-start(bf16[3072,64]{0,1:T(8,128)(2,1)} %param.12) | copy-start | bytes 1179652
  91.4 25.2 %copy-start.12 = (f32[128,64]{1,0:T(8,128)S(1)}, f32[128,64]{1,0:T(8,128)}, u32[]{:S(2)}) copy-start(f32[128,64]{1,0:T(8,128)} %get-tuple-element.22.gap_ref) | copy-start | bytes 98308

commit v6 on v5

--- a/solution.py
+++ b/solution.py
@@ -10,7 +10,7 @@
 SEQ = ("z_far", "z_near", "y_hi")
 NEAR = ("z_near", "y_hi")
 CHANS = 64
-HALF = CHANS // 2
+PART = CHANS // 4
 MROWS = 80
 PIECE = 80
 F32 = jnp.float32
@@ -119,46 +119,47 @@
 
 def far_body(recv_ref, send_ref, out_ref):
     piece = total_of(recv_ref, PIECE)
-    channels = send_ref[pl.ds(pl.multiple_of((lax.axis_index("mp") & 1) * HALF, HALF), HALF), :]
+    channels = send_ref[pl.ds(pl.multiple_of((lax.axis_index("mp") & 3) * PART, PART), PART), :]
     for i in range(out_ref.shape[0]):
         out_ref[i, 0:PIECE, :] = piece
-        out_ref[i, PIECE : PIECE + HALF, :] = channels
-        out_ref[i, PIECE + HALF :, :] = send_ref[CHANS:, :]
+        out_ref[i, PIECE : PIECE + PART, :] = channels
+        out_ref[i, PIECE + PART :, :] = send_ref[CHANS:, :]
 
 
 def spread_body(recv_ref, out_ref, text_ref):
     piece = total_of(recv_ref, PIECE)
-    text = PIECE + HALF
+    text = PIECE + PART
     for i in range(out_ref.shape[0]):
         out_ref[i, 0:PIECE, :] = piece
         for g in range(recv_ref.shape[0]):
-            out_ref[i, PIECE + g * HALF : PIECE + (g + 1) * HALF, :] = recv_ref[g, PIECE:text, :]
+            out_ref[i, PIECE + g * PART : PIECE + (g + 1) * PART, :] = recv_ref[g, PIECE:text, :]
             text_ref[i, g * 96 : (g + 1) * 96, :] = recv_ref[g, text:, :]
 
 
 def image_body(
-    send_ref, recv_ref, other_ref, gain_ref, out_ref, lat_ref, s_ref, v_ref, m_ref, own_ref, sum_ref
+    send_ref, recv_ref, other1_ref, other2_ref, other3_ref, gain_ref, out_ref, lat_ref, s_ref, v_ref, m_ref, own_ref, sum_ref
 ):
     tokens = lat_ref.shape[1]
     chunk = 1024
     n_chunks = tokens // chunk
     ones = jnp.where(lax.broadcasted_iota(jnp.int32, (MROWS - CHANS, HD), 0) == 0, 1.0, 0.0).astype(BF16)
-    n_far = (recv_ref.shape[1] - PIECE) // HALF
+    other_refs = (other1_ref, other2_ref, other3_ref)
+    n_far = (recv_ref.shape[1] - PIECE) // PART
     for i in range(tokens // HD):
-        near, first = i // n_far, (i % n_far) * HALF
+        near, first = i // n_far, (i % n_far) * PART
         at = slice(i * HD, (i + 1) * HD)
-        lat_ref[0:HALF, at] = recv_ref[near, PIECE + first : PIECE + first + HALF, :]
-        lat_ref[HALF:CHANS, at] = other_ref[near, first : first + HALF, :]
+        lat_ref[0:PART, at] = recv_ref[near, PIECE + first : PIECE + first + PART, :]
+        for k, ref in enumerate(other_refs):
+            lat_ref[(k + 1) * PART : (k + 2) * PART, at] = ref[near, first : first + PART, :]
         lat_ref[CHANS:MROWS, at] = ones
     for i in range(recv_ref.shape[0]):
         m_ref[i * PIECE : (i + 1) * PIECE, :] = recv_ref[i, 0:PIECE, :].astype(F32)
     own_ref[...] = send_ref[0:CHANS, :].astype(F32)
 
     def reordered(ref, base):
-        core = lax.axis_index("mp") & 1
-        return jnp.concatenate(
-            [ref[pl.ds(pl.multiple_of(k * HALF + base, HALF), HALF), :] for k in (core, 1 - core)], axis=0
-        )
+        here = lax.axis_index("mp") & 3
+        starts = [pl.multiple_of((here ^ k) * PART + base, PART) for k in range(4)]
+        return jnp.concatenate([ref[pl.ds(start, PART), :] for start in starts], axis=0)
 
     own = jnp.concatenate([reordered(own_ref, 0).astype(BF16), ones], axis=0)
     score_scale = HD ** (-0.5) * 1.4426950408889634
@@ -351,21 +352,22 @@
         limit=60,
     )
     pieces = exchange(payload, NEAR)
-    pieces = call(far_body, sds((n_far, PIECE + HALF + 96, HD), BF16), (pieces, send))
+    pieces = call(far_body, sds((n_far, PIECE + PART + 96, HD), BF16), (pieces, send))
     pieces = exchange(pieces, "z_far")
     pieces, text = call(
         spread_body,
-        (sds((8, PIECE + n_far * HALF, HD), BF16), sds((8, n_far * 96, HD), BF16)),
+        (sds((8, PIECE + n_far * PART, HD), BF16), sds((8, n_far * 96, HD), BF16)),
         (pieces,),
     )
     pieces = exchange(pieces, NEAR)
     text = exchange(text, NEAR).reshape(n_seq, 96, HD)
-    other = lax.ppermute(pieces[:, PIECE:, :], "mp", [(i, i ^ 1) for i in range(n_mp)])
+    channels = pieces[:, PIECE:, :]
+    others = [lax.ppermute(channels, "mp", [(i, i ^ k) for i in range(n_mp)]) for k in (1, 2, 3)]
 
     image = call(
         image_body,
         sds((7, rows_here, HD), F32),
-        (send, pieces, other, qk_gain[0]),
+        (send, pieces, *others, qk_gain[0]),
         scratch=(
             pltpu.VMEM((MROWS, tokens), BF16),
             pltpu.VMEM((3, rows_here, tokens), F32),

time: 153 us -> 152 us (level)
  starting transfers between devices: 15.7 us -> 21.8 us
  waiting for transfers between devices: 8.5 us -> 4.56 us
  blocking collectives: 106 us -> 103 us
    ppermute x1 -> x3, starting transfers between devices: 1.92 us -> 7.59 us  [on_device(): lax.ppermute(channels, 'mp', [(i, i ^ k) for i in range(n_mp)])]
    all_to_all x2, waiting for transfers between devices: 7 us -> 2.05 us  [exchange(): return lax.all_to_all(array, axis, 0, 0, tiled=True)]
    all_to_all x6, blocking collectives: 106 us -> 103 us  [exchange(): return lax.all_to_all(array, axis, 0, 0, tiled=True)]
    unnamed x30 -> x28, local copies, waits for them, and re-layouts: 3.65 us -> 3.5 us
  transfers between devices with their start and end apart: 3 -> 5, of which waited for: 3 -> 2; matrix products, arithmetic and copies ran while one was open for 1% -> 0% of each run, Pallas kernels for 7% -> 7%
where the time goes in v6:
time: 152 us; the launch traced here: 151 us
  blocking collectives  103 us (68%)
  starting transfers between devices  21.8 us (14%)
  Pallas kernels  16 us (11%)
  waiting for transfers between devices  4.56 us (3%)
  local copies, waits for them, and re-layouts  3.51 us (2%)
    all_to_all x6, blocking collectives, exchange(): return lax.all_to_all(array, axis, 0, 0, tiled=True)  103 us
    pallas_call x10, Pallas kernels, call(): pl.pallas_call(body, out_shape=out_shape, in_specs=[scalars if i < smem e...  16 us
    all_to_all x2, starting transfers between devices, exchange(): return lax.all_to_all(array, axis, 0, 0, tiled=True)  14.2 us
    ppermute x3, starting transfers between devices, on_device(): lax.ppermute(channels, 'mp', [(i, i ^ k) for i in range(n_mp)])  7.59 us
    unnamed x28, local copies, waits for them, and re-layouts  3.5 us
  transfers between devices with their start and end apart: 5, of which 2 were waited for; matrix products, arithmetic and copies ran while one was open for 0% of the time, Pallas kernels for 7%

profile of v6, /device:TPU:64, one launch (start us, length us, event | category | flops | bytes accessed | tf_op | source)
XLA Modules:
  0.0 150.8 jit_solution(12536044966272598266)
XLA Ops:
  0.6 0.0 copy-start
  0.6 2.4 %shard_map.130 = (bf16[8,80,128]{2,1,0:T(8,128)(2,1)}, s32[1]{0:T(128)}) custom-call(bf16[64,3072]{1,0:T(8,128)(2,1)} %bitcast.20, f32[3,1,3072]{2,1,0:T(1,128)} %bitcast.27, bf16[3,96,384]{2,1,0:T(8,128)(2,1)} %bitcast.31), custom_call_target="tpu_custom_call" | custom-call | tf_op jit(solution)/shard_map/pallas_call | solution.py:29
  3.1 8.4 %all-to-all-start = ((bf16[8,80,128]{2,1,0:T(8,128)(2,1)}), bf16[8,80,128]{2,1,0:T(8,128)(2,1)S(1)}, u32[]{:S(2)}, u32[]{:S(2)}) async-start(bf16[8,80,128]{2,1,0:T(8,128)(2,1)} %get-tuple-element.18), calls=%async_computation | async-start | bytes 327680 | tf_op jit(solution)/shard_map/all_to_all | solution.py:322
  12.1 0.0 copy-start.13
  12.1 3.9 %shard_map.131 = (f32[128,64]{1,0:T(8,128)}, f32[128,64]{1,0:T(8,128)}, bf16[160,128]{1,0:T(8,128)(2,1)}) custom-call(s32[1]{0:T(128)S(6)} %copy.14.level_ref.refs_0_, s32[1]{0:T(128)} %get-tuple-element.16._, bf16[128,3072]{1,0:T(8,128)(2,1)} %hidden_ref.3, bf16[64,3072]{1,0:T(8,128)(2,1)} %bitcast.24, bf16[64,128]{1,0:T(8,128)(2,1)} %bitcast.33, ...), custom_call_target="tpu_custom_call" | custom-call | tf_op jit(solution)/shard_map/pallas_call | solution.py:29
  16.0 2.0 %all-to-all-done.recv_ref = bf16[8,80,128]{2,1,0:T(8,128)(2,1)S(1)} async-done(((bf16[8,80,128]{2,1,0:T(8,128)(2,1)}), bf16[8,80,128]{2,1,0:T(8,128)(2,1)S(1)}, u32[]{:S(2)}, u32[]{:S(2)}) %all-to-all-start) | async-done | bytes 163872 | tf_op jit(solution)/shard_map/all_to_all | solution.py:322
  18.1 0.8 copy-done.8
  18.9 27.8 %all_to_all.40.recv_ref = bf16[4,192,128]{2,1,0:T(8,128)(2,1)S(1)} all-to-all(bf16[4,192,128]{2,1,0:T(8,128)(2,1)S(1)} %shard_map.132), channel_id=1, replica_groups=mesh['role'=2,'z_far'=4,'z_near'=4,'y_hi'=2,'mp'=8] {'z_far'}, dimensions={0} | all-to-all | bytes 393216 | tf_op jit(solution)/shard_map/all_to_all | solution.py:322
  46.7 0.1 shard_map.133
  46.8 0.0 copy-start.6
  46.8 0.9 copy-done.6
  47.7 15.2 %all_to_all.41.recv_ref = bf16[8,144,128]{2,1,0:T(8,128)(2,1)S(1)} all-to-all(bf16[8,144,128]{2,1,0:T(8,128)(2,1)S(1)} %get-tuple-element.19), channel_id=1, replica_groups=mesh['role'=2,'z_far'=4,'z_near'=4,'y_hi'=2,'mp'=8] {'z_near','y_hi'}, dimensions={0} | all-to-all | bytes 589824 | tf_op jit(solution)/shard_map/all_to_all | solution.py:322
  62.9 5.9 %all-to-all-start.3 = ((bf16[8,384,128]{2,1,0:T(8,128)(2,1)}), bf16[8,384,128]{2,1,0:T(8,128)(2,1)S(1)}, u32[]{:S(2)}, u32[]{:S(2)}) async-start(bf16[8,384,128]{2,1,0:T(8,128)(2,1)} %copy-done.6), calls=%async_computation.3 | async-start | bytes 1572864 | tf_op jit(solution)/shard_map/all_to_all | solution.py:322
  68.8 1.9 %collective-permute-start.2 = (bf16[8,64,128]{2,1,0:T(8,128)(2,1)S(1)}, bf16[8,64,128]{2,1,0:T(8,128)(2,1)S(1)}, u32[]{:S(2)}, u32[]{:S(2)}) collective-permute-start(bf16[8,64,128]{2,1,0:T(8,128)(2,1)S(1)} %slice.4), channel_id=1, source_target_pairs={{0,3},{1,2},{2,1},{3,0},{4,7},{5,6},{6,5},{7,4},{8,11},{9,10},{10,... | collective-permute-start | bytes 393224 | tf_op jit(solution)/shard_map/ppermute | solution.py:365
  70.7 3.4 %collective-permute-start.1 = (bf16[8,64,128]{2,1,0:T(8,128)(2,1)S(1)}, bf16[8,64,128]{2,1,0:T(8,128)(2,1)S(1)}, u32[]{:S(2)}, u32[]{:S(2)}) collective-permute-start(bf16[8,64,128]{2,1,0:T(8,128)(2,1)S(1)} %slice.4), channel_id=1, source_target_pairs={{0,2},{1,3},{2,0},{3,1},{4,6},{5,7},{6,4},{7,5},{8,10},{9,11},{10,... | collective-permute-start | bytes 393224 | tf_op jit(solution)/shard_map/ppermute | solution.py:365
  74.1 2.3 %collective-permute-start = (bf16[8,64,128]{2,1,0:T(8,128)(2,1)S(1)}, bf16[8,64,128]{2,1,0:T(8,128)(2,1)S(1)}, u32[]{:S(2)}, u32[]{:S(2)}) collective-permute-start(bf16[8,64,128]{2,1,0:T(8,128)(2,1)S(1)} %slice.4), channel_id=1, source_target_pairs={{0,1},{1,0},{2,3},{3,2},{4,5},{5,4},{6,7},{7,6},{8,9},{9,8},{10,11... | collective-permute-start | bytes 393224 | tf_op jit(solution)/shard_map/ppermute | solution.py:365
  76.4 0.0 collective-permute-done.2.other3_ref
  76.4 2.5 %collective-permute-done.1.other2_ref = bf16[8,64,128]{2,1,0:T(8,128)(2,1)S(1)} collective-permute-done((bf16[8,64,128]{2,1,0:T(8,128)(2,1)S(1)}, bf16[8,64,128]{2,1,0:T(8,128)(2,1)S(1)}, u32[]{:S(2)}, u32[]{:S(2)}) %collective-permute-start.1) | collective-permute-done | bytes 131104 | tf_op jit(solution)/shard_map/ppermute | solution.py:365
  78.9 0.0 collective-permute-done.other1_ref
  78.9 0.0 copy-done.13
  78.9 0.0 copy-done.9
  78.9 6.3 %shard_map.134.image_ref = f32[7,128,128]{2,1,0:T(8,128)S(1)} custom-call(bf16[160,128]{1,0:T(8,128)(2,1)S(1)} %copy-done.9, bf16[8,144,128]{2,1,0:T(8,128)(2,1)S(1)} %all_to_all.41.recv_ref, bf16[8,64,128]{2,1,0:T(8,128)(2,1)S(1)} %collective-permute-done.other1_ref, bf16[8,64,128]{2,1,0:T(8,128)(2,1)S(1)} %collective-permute-done.1.other2_ref, ...), custom_call_target="tpu_custom_call" | custom-call | tf_op jit(solution)/shard_map/pallas_call | solution.py:29
  85.2 0.0 copy-start.3
  85.2 0.8 copy-done.3
  86.0 0.0 all-to-all-done.3
  86.0 1.0 copy-done.4
  87.0 1.3 shard_map.135
  88.3 0.0 copy-done
  88.3 0.0 copy-start.1
  88.3 0.0 copy-start.7
  88.3 0.0 copy-start.10
  88.3 0.0 copy-start.12
  88.4 0.6 convolution_convert_fusion
  88.9 0.0 copy-start.2
  89.0 0.0 copy-start.5
  89.0 0.0 copy-start.11
  89.0 17.4 %all_to_all.42.parts_ref = bf16[8,16,3072]{2,1,0:T(8,128)(2,1)S(1)} all-to-all(bf16[8,16,3072]{2,1,0:T(8,128)(2,1)S(1)} %bitcast.30), channel_id=1, replica_groups=mesh['role'=2,'z_far'=4,'z_near'=4,'y_hi'=2,'mp'=8] {'mp'}, dimensions={0} | all-to-all | bytes 1572864 | tf_op jit(solution)/shard_map/all_to_all | solution.py:322
  106.3 0.0 copy-done.1
  106.3 0.0 copy-done.7
  106.3 0.0 copy-done.10
  106.4 0.0 copy-done.12
  106.4 0.6 shard_map.136
  107.0 8.7 %all_to_all.43.both_ref = f32[16,8,128]{2,1,0:T(8,128)S(1)} all-to-all(f32[16,8,128]{2,1,0:T(8,128)S(1)} %shard_map.136), channel_id=1, replica_groups=mesh['role'=2,'z_far'=4,'z_near'=4,'y_hi'=2,'mp'=8] {'role','mp'}, dimensions={0} | all-to-all | bytes 131072 | tf_op jit(solution)/shard_map/all_to_all | solution.py:322
  115.7 0.0 copy-done.2
  115.7 0.4 shard_map.137
  116.1 15.6 %all_to_all.44.recv_ref = bf16[8,104,128]{2,1,0:T(8,128)(2,1)S(1)} all-to-all(bf16[8,104,128]{2,1,0:T(8,128)(2,1)S(1)} %get-tuple-element.23), channel_id=1, replica_groups=mesh['role'=2,'z_far'=4,'z_near'=4,'y_hi'=2,'mp'=8] {'z_near','y_hi'}, dimensions={0} | all-to-all | bytes 425984 | tf_op jit(solution)/shard_map/all_to_all | solution.py:322
  131.8 18.1 %all_to_all.45.refs_1_ = bf16[4,104,128]{2,1,0:T(8,128)(2,1)S(1)} all-to-all(bf16[4,104,128]{2,1,0:T(8,128)(2,1)S(1)} %shard_map.138), channel_id=1, replica_groups=mesh['role'=2,'z_far'=4,'z_near'=4,'y_hi'=2,'mp'=8] {'z_far'}, dimensions={0} | all-to-all | bytes 212992 | tf_op jit(solution)/shard_map/all_to_all | solution.py:322
  149.9 0.9 shard_map.139
  (8 shorter events, 0.1 us)
Async XLA Ops:
  0.6 87.7 %copy-start = (bf16[1,384,3072]{2,1,0:T(8,128)(2,1)S(1)}, bf16[1,384,3072]{2,1,0:T(8,128)(2,1)}, u32[]{:S(2)}) copy-start(bf16[1,384,3072]{2,1,0:T(8,128)(2,1)} %param.20) | copy-start | bytes 7077892
  3.1 15.0 %all-to-all-start = ((bf16[8,80,128]{2,1,0:T(8,128)(2,1)}), bf16[8,80,128]{2,1,0:T(8,128)(2,1)S(1)}, u32[]{:S(2)}, u32[]{:S(2)}) async-start(bf16[8,80,128]{2,1,0:T(8,128)(2,1)} %get-tuple-element.18), calls=%async_computation | async-start | bytes 327680 | tf_op jit(solution)/shard_map/all_to_all | solution.py:322
  12.1 66.8 %copy-start.13 = (f32[1,2,128]{2,1,0:T(2,128)S(1)}, f32[1,2,128]{2,1,0:T(2,128)}, u32[]{:S(2)}) copy-start(f32[1,2,128]{2,1,0:T(2,128)} %param.18) | copy-start | bytes 3076
  18.1 0.8 copy-start.8
  18.9 60.1 %copy-start.9 = (bf16[160,128]{1,0:T(8,128)(2,1)S(1)}, bf16[160,128]{1,0:T(8,128)(2,1)}, u32[]{:S(2)}) copy-start(bf16[160,128]{1,0:T(8,128)(2,1)} %get-tuple-element.17.send_ref) | copy-start | bytes 122884
  46.8 0.9 copy-start.6
  62.9 23.1 %all-to-all-start.3 = ((bf16[8,384,128]{2,1,0:T(8,128)(2,1)}), bf16[8,384,128]{2,1,0:T(8,128)(2,1)S(1)}, u32[]{:S(2)}, u32[]{:S(2)}) async-start(bf16[8,384,128]{2,1,0:T(8,128)(2,1)} %copy-done.6), calls=%async_computation.3 | async-start | bytes 1572864 | tf_op jit(solution)/shard_map/all_to_all | solution.py:322
  68.8 7.6 %collective-permute-start.2 = (bf16[8,64,128]{2,1,0:T(8,128)(2,1)S(1)}, bf16[8,64,128]{2,1,0:T(8,128)(2,1)S(1)}, u32[]{:S(2)}, u32[]{:S(2)}) collective-permute-start(bf16[8,64,128]{2,1,0:T(8,128)(2,1)S(1)} %slice.4), channel_id=1, source_target_pairs={{0,3},{1,2},{2,1},{3,0},{4,7},{5,6},{6,5},{7,4},{8,11},{9,10},{10,... | collective-permute-start | bytes 393224 | tf_op jit(solution)/shard_map/ppermute | solution.py:365
  70.7 8.2 %collective-permute-start.1 = (bf16[8,64,128]{2,1,0:T(8,128)(2,1)S(1)}, bf16[8,64,128]{2,1,0:T(8,128)(2,1)S(1)}, u32[]{:S(2)}, u32[]{:S(2)}) collective-permute-start(bf16[8,64,128]{2,1,0:T(8,128)(2,1)S(1)} %slice.4), channel_id=1, source_target_pairs={{0,2},{1,3},{2,0},{3,1},{4,6},{5,7},{6,4},{7,5},{8,10},{9,11},{10,... | collective-permute-start | bytes 393224 | tf_op jit(solution)/shard_map/ppermute | solution.py:365
  74.1 4.8 %collective-permute-start = (bf16[8,64,128]{2,1,0:T(8,128)(2,1)S(1)}, bf16[8,64,128]{2,1,0:T(8,128)(2,1)S(1)}, u32[]{:S(2)}, u32[]{:S(2)}) collective-permute-start(bf16[8,64,128]{2,1,0:T(8,128)(2,1)S(1)} %slice.4), channel_id=1, source_target_pairs={{0,1},{1,0},{2,3},{3,2},{4,5},{5,4},{6,7},{7,6},{8,9},{9,8},{10,11... | collective-permute-start | bytes 393224 | tf_op jit(solution)/shard_map/ppermute | solution.py:365
  85.2 0.8 copy-start.3
  86.0 1.0 copy-start.4
  88.3 18.0 %copy-start.1 = (bf16[1,64,3072]{2,1,0:T(8,128)(2,1)S(1)}, bf16[1,64,3072]{2,1,0:T(8,128)(2,1)}, u32[]{:S(2)}) copy-start(bf16[1,64,3072]{2,1,0:T(8,128)(2,1)} %param.15) | copy-start | bytes 1179652
  88.3 18.0 %copy-start.7 = (bf16[1,3072,64]{1,2,0:T(8,128)(2,1)S(1)}, bf16[1,3072,64]{1,2,0:T(8,128)(2,1)}, u32[]{:S(2)}) copy-start(bf16[1,3072,64]{1,2,0:T(8,128)(2,1)} %param.21) | copy-start | bytes 1179652
  88.3 18.0 %copy-start.10 = (f32[1,3,3072]{2,0,1:T(1,128)S(1)}, f32[1,3,3072]{2,0,1:T(1,128)}, u32[]{:S(2)}) copy-start(f32[1,3,3072]{2,0,1:T(1,128)} %param.16) | copy-start | bytes 110596
  88.3 18.0 %copy-start.12 = (f32[128,64]{1,0:T(8,128)S(1)}, f32[128,64]{1,0:T(8,128)}, u32[]{:S(2)}) copy-start(f32[128,64]{1,0:T(8,128)} %get-tuple-element.21.noised_ref) | copy-start | bytes 98308
  88.9 26.8 %copy-start.2 = (bf16[128,3072]{1,0:T(8,128)(2,1)S(1)}, bf16[128,3072]{1,0:T(8,128)(2,1)}, u32[]{:S(2)}) copy-start(bf16[128,3072]{1,0:T(8,128)(2,1)} %hidden_ref.3) | copy-start | bytes 2359300
  89.0 26.7 %copy-start.5 = (bf16[3072,64]{0,1:T(8,128)(2,1)S(1)}, bf16[3072,64]{0,1:T(8,128)(2,1)}, u32[]{:S(2)}) copy-start(bf16[3072,64]{0,1:T(8,128)(2,1)} %param.12) | copy-start | bytes 1179652
  89.0 26.7 %copy-start.11 = (f32[128,64]{1,0:T(8,128)S(1)}, f32[128,64]{1,0:T(8,128)}, u32[]{:S(2)}) copy-start(f32[128,64]{1,0:T(8,128)} %get-tuple-element.22.gap_ref) | copy-start | bytes 98308

commit v7 on v6

--- a/solution.py
+++ b/solution.py
@@ -140,7 +140,7 @@
     send_ref, recv_ref, other1_ref, other2_ref, other3_ref, gain_ref, out_ref, lat_ref, s_ref, v_ref, m_ref, own_ref, sum_ref
 ):
     tokens = lat_ref.shape[1]
-    chunk = 1024
+    chunk = 2048
     n_chunks = tokens // chunk
     ones = jnp.where(lax.broadcasted_iota(jnp.int32, (MROWS - CHANS, HD), 0) == 0, 1.0, 0.0).astype(BF16)
     other_refs = (other1_ref, other2_ref, other3_ref)
@@ -223,7 +223,7 @@
     out_ref[6] = numbers
 
 
-def text_body(image_ref, text_ref, att_ref):
+def text_body(image_ref, text_ref, own_ref, other_ref, att_ref):
     def block(first):
         return text_ref[:, first : first + 16, :].reshape(text_ref.shape[0] * 16, HD)
 
@@ -235,7 +235,11 @@
         p = jnp.exp2(s - top)
         acc = image_ref[head] * keep + dot(p.astype(BF16), block(48 + head * 16))
         total = image_ref[6][:, 3 + head : 4 + head] * keep + jnp.sum(p, axis=1, keepdims=True)
-        att_ref[:, head * HD : (head + 1) * HD] = (acc / total).astype(BF16)
+        att_ref[:, :, head * HD : (head + 1) * HD] = (acc / total).reshape(att_ref.shape[0], -1, HD)
+    core = lax.axis_index("mp") & 1
+    for i in range(own_ref.shape[0]):
+        own_ref[i] = att_ref[2 * i + core].astype(BF16)
+        other_ref[i] = att_ref[2 * i + 1 - core].astype(BF16)
 
 
 def velocity_body(parts_ref, noised_ref, embed_ref, mod_ref, final_t_ref, v_ref):
@@ -318,8 +322,8 @@
         gen_ref[:, g * HD : (g + 1) * HD] = total[g * half : (g + 1) * half, :] * factor
 
 
-def exchange(array, axis):
-    return lax.all_to_all(array, axis, 0, 0, tiled=True)
+def exchange(array, axis, groups=None):
+    return lax.all_to_all(array, axis, 0, 0, axis_index_groups=groups, tiled=True)
 
 
 def on_device(
@@ -378,9 +382,15 @@
         ),
     )
     own_rows = rows_here // n_mp
-    attended = call(text_body, sds((rows_here, 3 * HD), BF16), (image, text))
-    y = dot(attended, w_out[0]).astype(BF16).reshape(n_mp, own_rows, width)
-    parts = exchange(y, "mp")
+    share = sds((n_mp // 2, own_rows, 3 * HD), BF16)
+    att_own, att_other = call(
+        text_body, (share, share), (image, text), scratch=(pltpu.VMEM((n_mp, own_rows, 3 * HD), F32),)
+    )
+    y_other = dot(att_other.reshape(-1, 3 * HD), w_out[0]).astype(BF16)
+    y_other = lax.ppermute(y_other, "mp", [(i, i ^ 1) for i in range(n_mp)])
+    y = (dot(att_own.reshape(-1, 3 * HD), w_out[0]) + y_other.astype(F32)).astype(BF16)
+    same_core = [[2 * x + core for x in range(n_mp // 2)] for core in range(2)]
+    parts = exchange(y.reshape(n_mp // 2, own_rows, width), "mp", same_core)
     velocity = call(
         velocity_body,
         sds((2 * n_mp, 8, 2 * chans), F32),

time: 152 us -> 150 us (0.987)
  blocking collectives: 103 us -> 98.7 us
  starting transfers between devices: 21.8 us -> 24.3 us
    all_to_all x6, blocking collectives: 103 us -> 98.7 us  [exchange(): lax.all_to_all(array, axis, 0, 0, axis_index_groups=groups, tiled=True)]
    ppermute x0 -> x1, starting transfers between devices: none -> 2.52 us  [on_device(): y_other = lax.ppermute(y_other, 'mp', [(i, i ^ 1) for i in range(n_mp)])]
  transfers between devices with their start and end apart: 5 -> 6, of which waited for: 2 -> 3; matrix products, arithmetic and copies ran while one was open for 0% -> 0% of each run, Pallas kernels for 7% -> 6%
where the time goes in v7:
time: 150 us
  blocking collectives  98.7 us (66%)
  starting transfers between devices  24.3 us (16%)
  Pallas kernels  14.6 us (10%)
  waiting for transfers between devices  5.89 us (4%)
  local copies, waits for them, and re-layouts  3.51 us (2%)
    all_to_all x6, blocking collectives, exchange(): lax.all_to_all(array, axis, 0, 0, axis_index_groups=groups, tiled=True)  98.7 us
    pallas_call x10, Pallas kernels, call(): pl.pallas_call(body, out_shape=out_shape, in_specs=[scalars if i < smem e...  14.6 us
    all_to_all x2, starting transfers between devices, exchange(): lax.all_to_all(array, axis, 0, 0, axis_index_groups=groups, tiled=True)  14.2 us
    ppermute x3, starting transfers between devices, on_device(): lax.ppermute(channels, 'mp', [(i, i ^ k) for i in range(n_mp)])  7.59 us
    unnamed x28, local copies, waits for them, and re-layouts  3.5 us
  transfers between devices with their start and end apart: 6, of which 3 were waited for; matrix products, arithmetic and copies ran while one was open for 0% of the time, Pallas kernels for 6%

profile of v7, /device:TPU:64, one launch (start us, length us, event | category | flops | bytes accessed | tf_op | source)
XLA Modules:
  0.0 149.6 jit_solution(14659162022198424696)
XLA Ops:
  0.6 0.0 copy-start
  0.6 2.4 %shard_map.130 = (bf16[8,80,128]{2,1,0:T(8,128)(2,1)}, s32[1]{0:T(128)}) custom-call(bf16[64,3072]{1,0:T(8,128)(2,1)} %bitcast.25, f32[3,1,3072]{2,1,0:T(1,128)} %bitcast.32, bf16[3,96,384]{2,1,0:T(8,128)(2,1)} %bitcast.38), custom_call_target="tpu_custom_call" | custom-call | tf_op jit(solution)/shard_map/pallas_call | solution.py:29
  3.1 8.4 %all-to-all-start = ((bf16[8,80,128]{2,1,0:T(8,128)(2,1)}), bf16[8,80,128]{2,1,0:T(8,128)(2,1)S(1)}, u32[]{:S(2)}, u32[]{:S(2)}) async-start(bf16[8,80,128]{2,1,0:T(8,128)(2,1)} %get-tuple-element.20), calls=%async_computation | async-start | bytes 327680 | tf_op jit(solution)/shard_map/all_to_all | solution.py:326
  12.1 0.0 copy-start.13
  12.1 3.9 %shard_map.131 = (f32[128,64]{1,0:T(8,128)}, f32[128,64]{1,0:T(8,128)}, bf16[160,128]{1,0:T(8,128)(2,1)}) custom-call(s32[1]{0:T(128)S(6)} %copy.14.level_ref.refs_0_, s32[1]{0:T(128)} %get-tuple-element.18._, bf16[128,3072]{1,0:T(8,128)(2,1)} %hidden_ref.3, bf16[64,3072]{1,0:T(8,128)(2,1)} %bitcast.29, bf16[64,128]{1,0:T(8,128)(2,1)} %bitcast.40, ...), custom_call_target="tpu_custom_call" | custom-call | tf_op jit(solution)/shard_map/pallas_call | solution.py:29
  16.0 2.0 %all-to-all-done.recv_ref = bf16[8,80,128]{2,1,0:T(8,128)(2,1)S(1)} async-done(((bf16[8,80,128]{2,1,0:T(8,128)(2,1)}), bf16[8,80,128]{2,1,0:T(8,128)(2,1)S(1)}, u32[]{:S(2)}, u32[]{:S(2)}) %all-to-all-start) | async-done | bytes 163872 | tf_op jit(solution)/shard_map/all_to_all | solution.py:326
  18.1 0.8 copy-done.8
  18.9 27.8 %all_to_all.40.recv_ref = bf16[4,192,128]{2,1,0:T(8,128)(2,1)S(1)} all-to-all(bf16[4,192,128]{2,1,0:T(8,128)(2,1)S(1)} %shard_map.132), channel_id=1, replica_groups=mesh['role'=2,'z_far'=4,'z_near'=4,'y_hi'=2,'mp'=8] {'z_far'}, dimensions={0} | all-to-all | bytes 393216 | tf_op jit(solution)/shard_map/all_to_all | solution.py:326
  46.7 0.1 shard_map.133
  46.8 0.0 copy-start.6
  46.8 0.9 copy-done.6
  47.7 15.2 %all_to_all.41.recv_ref = bf16[8,144,128]{2,1,0:T(8,128)(2,1)S(1)} all-to-all(bf16[8,144,128]{2,1,0:T(8,128)(2,1)S(1)} %get-tuple-element.21), channel_id=1, replica_groups=mesh['role'=2,'z_far'=4,'z_near'=4,'y_hi'=2,'mp'=8] {'z_near','y_hi'}, dimensions={0} | all-to-all | bytes 589824 | tf_op jit(solution)/shard_map/all_to_all | solution.py:326
  62.9 5.9 %all-to-all-start.3 = ((bf16[8,384,128]{2,1,0:T(8,128)(2,1)}), bf16[8,384,128]{2,1,0:T(8,128)(2,1)S(1)}, u32[]{:S(2)}, u32[]{:S(2)}) async-start(bf16[8,384,128]{2,1,0:T(8,128)(2,1)} %copy-done.6), calls=%async_computation.3 | async-start | bytes 1572864 | tf_op jit(solution)/shard_map/all_to_all | solution.py:326
  68.8 1.9 %collective-permute-start.2 = (bf16[8,64,128]{2,1,0:T(8,128)(2,1)S(1)}, bf16[8,64,128]{2,1,0:T(8,128)(2,1)S(1)}, u32[]{:S(2)}, u32[]{:S(2)}) collective-permute-start(bf16[8,64,128]{2,1,0:T(8,128)(2,1)S(1)} %slice.4), channel_id=1, source_target_pairs={{0,3},{1,2},{2,1},{3,0},{4,7},{5,6},{6,5},{7,4},{8,11},{9,10},{10,... | collective-permute-start | bytes 393224 | tf_op jit(solution)/shard_map/ppermute | solution.py:369
  70.7 3.4 %collective-permute-start.1 = (bf16[8,64,128]{2,1,0:T(8,128)(2,1)S(1)}, bf16[8,64,128]{2,1,0:T(8,128)(2,1)S(1)}, u32[]{:S(2)}, u32[]{:S(2)}) collective-permute-start(bf16[8,64,128]{2,1,0:T(8,128)(2,1)S(1)} %slice.4), channel_id=1, source_target_pairs={{0,2},{1,3},{2,0},{3,1},{4,6},{5,7},{6,4},{7,5},{8,10},{9,11},{10,... | collective-permute-start | bytes 393224 | tf_op jit(solution)/shard_map/ppermute | solution.py:369
  74.1 2.3 %collective-permute-start = (bf16[8,64,128]{2,1,0:T(8,128)(2,1)S(1)}, bf16[8,64,128]{2,1,0:T(8,128)(2,1)S(1)}, u32[]{:S(2)}, u32[]{:S(2)}) collective-permute-start(bf16[8,64,128]{2,1,0:T(8,128)(2,1)S(1)} %slice.4), channel_id=1, source_target_pairs={{0,1},{1,0},{2,3},{3,2},{4,5},{5,4},{6,7},{7,6},{8,9},{9,8},{10,11... | collective-permute-start | bytes 393224 | tf_op jit(solution)/shard_map/ppermute | solution.py:369
  76.4 0.0 collective-permute-done.2.other3_ref
  76.5 2.5 %collective-permute-done.1.other2_ref = bf16[8,64,128]{2,1,0:T(8,128)(2,1)S(1)} collective-permute-done((bf16[8,64,128]{2,1,0:T(8,128)(2,1)S(1)}, bf16[8,64,128]{2,1,0:T(8,128)(2,1)S(1)}, u32[]{:S(2)}, u32[]{:S(2)}) %collective-permute-start.1) | collective-permute-done | bytes 131104 | tf_op jit(solution)/shard_map/ppermute | solution.py:369
  78.9 0.0 collective-permute-done.other1_ref
  78.9 0.0 copy-done.13
  78.9 0.0 copy-done.9
  78.9 4.8 %shard_map.134.image_ref = f32[7,128,128]{2,1,0:T(8,128)S(1)} custom-call(bf16[160,128]{1,0:T(8,128)(2,1)S(1)} %copy-done.9, bf16[8,144,128]{2,1,0:T(8,128)(2,1)S(1)} %all_to_all.41.recv_ref, bf16[8,64,128]{2,1,0:T(8,128)(2,1)S(1)} %collective-permute-done.other1_ref, bf16[8,64,128]{2,1,0:T(8,128)(2,1)S(1)} %collective-permute-done.1.other2_ref, ...), custom_call_target="tpu_custom_call" | custom-call | tf_op jit(solution)/shard_map/pallas_call | solution.py:29
  83.7 0.0 copy-start.3
  83.7 0.8 copy-done.3
  84.5 0.0 all-to-all-done.3
  84.5 1.0 copy-done.4
  85.5 1.3 shard_map.135
  86.9 0.0 copy-done
  86.9 0.5 convolution_convert_fusion
  87.4 0.0 copy-start.1
  87.4 0.0 copy-start.7
  87.4 0.0 copy-start.10
  87.5 0.0 copy-start.12
  87.5 2.5 %collective-permute-start.3 = (bf16[64,3072]{1,0:T(8,128)(2,1)S(1)}, bf16[64,3072]{1,0:T(8,128)(2,1)S(1)}, u32[]{:S(2)}, u32[]{:S(2)}) collective-permute-start(bf16[64,3072]{1,0:T(8,128)(2,1)S(1)} %convolution_convert_fusion), channel_id=1, source_target_pairs={{0,1},{1,0},{2,3},{3,2},{4,5},{5,4},{6,7},{7,6},{8,9},{9,8},{10,11... | collective-permute-start | bytes 1179656 | tf_op jit(solution)/shard_map/ppermute | solution.py:390
  90.0 1.3 collective-permute-done.3
  91.3 0.6 fusion
  91.9 12.5 %all_to_all.42.parts_ref = bf16[4,16,3072]{2,1,0:T(8,128)(2,1)S(1)} all-to-all(bf16[4,16,3072]{2,1,0:T(8,128)(2,1)S(1)} %bitcast.37), channel_id=1, replica_groups={{0,2,4,6},{1,3,5,7},{8,10,12,14},{9,11,13,15},{16,18,20,22},{17,19,21,2..., dimensions={0} | all-to-all | bytes 786432 | tf_op jit(solution)/shard_map/all_to_all | solution.py:326
  104.4 0.0 copy-done.1
  104.4 0.0 copy-done.7
  104.4 0.0 copy-done.10
  104.4 0.0 copy-done.12
  104.4 0.6 shard_map.136
  105.0 8.7 %all_to_all.43.both_ref = f32[16,8,128]{2,1,0:T(8,128)S(1)} all-to-all(f32[16,8,128]{2,1,0:T(8,128)S(1)} %shard_map.136), channel_id=1, replica_groups=mesh['role'=2,'z_far'=4,'z_near'=4,'y_hi'=2,'mp'=8] {'role','mp'}, dimensions={0} | all-to-all | bytes 131072 | tf_op jit(solution)/shard_map/all_to_all | solution.py:326
  113.7 0.0 copy-done.2
  113.7 0.4 shard_map.137
  114.1 15.4 %all_to_all.44.recv_ref = bf16[8,104,128]{2,1,0:T(8,128)(2,1)S(1)} all-to-all(bf16[8,104,128]{2,1,0:T(8,128)(2,1)S(1)} %get-tuple-element.27), channel_id=1, replica_groups=mesh['role'=2,'z_far'=4,'z_near'=4,'y_hi'=2,'mp'=8] {'z_near','y_hi'}, dimensions={0} | all-to-all | bytes 425984 | tf_op jit(solution)/shard_map/all_to_all | solution.py:326
  129.6 19.1 %all_to_all.45.refs_1_ = bf16[4,104,128]{2,1,0:T(8,128)(2,1)S(1)} all-to-all(bf16[4,104,128]{2,1,0:T(8,128)(2,1)S(1)} %shard_map.138), channel_id=1, replica_groups=mesh['role'=2,'z_far'=4,'z_near'=4,'y_hi'=2,'mp'=8] {'z_far'}, dimensions={0} | all-to-all | bytes 212992 | tf_op jit(solution)/shard_map/all_to_all | solution.py:326
  148.7 0.9 shard_map.139
  (11 shorter events, 0.1 us)
Async XLA Ops:
  0.6 86.2 %copy-start = (bf16[1,384,3072]{2,1,0:T(8,128)(2,1)S(1)}, bf16[1,384,3072]{2,1,0:T(8,128)(2,1)}, u32[]{:S(2)}) copy-start(bf16[1,384,3072]{2,1,0:T(8,128)(2,1)} %param.20) | copy-start | bytes 7077892
  3.1 15.0 %all-to-all-start = ((bf16[8,80,128]{2,1,0:T(8,128)(2,1)}), bf16[8,80,128]{2,1,0:T(8,128)(2,1)S(1)}, u32[]{:S(2)}, u32[]{:S(2)}) async-start(bf16[8,80,128]{2,1,0:T(8,128)(2,1)} %get-tuple-element.20), calls=%async_computation | async-start | bytes 327680 | tf_op jit(solution)/shard_map/all_to_all | solution.py:326
  12.1 66.9 %copy-start.13 = (f32[1,2,128]{2,1,0:T(2,128)S(1)}, f32[1,2,128]{2,1,0:T(2,128)}, u32[]{:S(2)}) copy-start(f32[1,2,128]{2,1,0:T(2,128)} %param.18) | copy-start | bytes 3076
  18.1 0.8 copy-start.8
  18.9 60.1 %copy-start.9 = (bf16[160,128]{1,0:T(8,128)(2,1)S(1)}, bf16[160,128]{1,0:T(8,128)(2,1)}, u32[]{:S(2)}) copy-start(bf16[160,128]{1,0:T(8,128)(2,1)} %get-tuple-element.19.send_ref) | copy-start | bytes 122884
  46.8 0.9 copy-start.6
  62.9 21.6 %all-to-all-start.3 = ((bf16[8,384,128]{2,1,0:T(8,128)(2,1)}), bf16[8,384,128]{2,1,0:T(8,128)(2,1)S(1)}, u32[]{:S(2)}, u32[]{:S(2)}) async-start(bf16[8,384,128]{2,1,0:T(8,128)(2,1)} %copy-done.6), calls=%async_computation.3 | async-start | bytes 1572864 | tf_op jit(solution)/shard_map/all_to_all | solution.py:326
  68.8 7.6 %collective-permute-start.2 = (bf16[8,64,128]{2,1,0:T(8,128)(2,1)S(1)}, bf16[8,64,128]{2,1,0:T(8,128)(2,1)S(1)}, u32[]{:S(2)}, u32[]{:S(2)}) collective-permute-start(bf16[8,64,128]{2,1,0:T(8,128)(2,1)S(1)} %slice.4), channel_id=1, source_target_pairs={{0,3},{1,2},{2,1},{3,0},{4,7},{5,6},{6,5},{7,4},{8,11},{9,10},{10,... | collective-permute-start | bytes 393224 | tf_op jit(solution)/shard_map/ppermute | solution.py:369
  70.7 8.2 %collective-permute-start.1 = (bf16[8,64,128]{2,1,0:T(8,128)(2,1)S(1)}, bf16[8,64,128]{2,1,0:T(8,128)(2,1)S(1)}, u32[]{:S(2)}, u32[]{:S(2)}) collective-permute-start(bf16[8,64,128]{2,1,0:T(8,128)(2,1)S(1)} %slice.4), channel_id=1, source_target_pairs={{0,2},{1,3},{2,0},{3,1},{4,6},{5,7},{6,4},{7,5},{8,10},{9,11},{10,... | collective-permute-start | bytes 393224 | tf_op jit(solution)/shard_map/ppermute | solution.py:369
  74.1 4.8 %collective-permute-start = (bf16[8,64,128]{2,1,0:T(8,128)(2,1)S(1)}, bf16[8,64,128]{2,1,0:T(8,128)(2,1)S(1)}, u32[]{:S(2)}, u32[]{:S(2)}) collective-permute-start(bf16[8,64,128]{2,1,0:T(8,128)(2,1)S(1)} %slice.4), channel_id=1, source_target_pairs={{0,1},{1,0},{2,3},{3,2},{4,5},{5,4},{6,7},{7,6},{8,9},{9,8},{10,11... | collective-permute-start | bytes 393224 | tf_op jit(solution)/shard_map/ppermute | solution.py:369
  83.7 0.8 copy-start.3
  84.5 1.0 copy-start.4
  87.4 16.9 %copy-start.1 = (bf16[1,64,3072]{2,1,0:T(8,128)(2,1)S(1)}, bf16[1,64,3072]{2,1,0:T(8,128)(2,1)}, u32[]{:S(2)}) copy-start(bf16[1,64,3072]{2,1,0:T(8,128)(2,1)} %param.15) | copy-start | bytes 1179652
  87.4 16.9 %copy-start.7 = (bf16[1,3072,64]{1,2,0:T(8,128)(2,1)S(1)}, bf16[1,3072,64]{1,2,0:T(8,128)(2,1)}, u32[]{:S(2)}) copy-start(bf16[1,3072,64]{1,2,0:T(8,128)(2,1)} %param.21) | copy-start | bytes 1179652
  87.4 16.9 %copy-start.10 = (f32[1,3,3072]{2,0,1:T(1,128)S(1)}, f32[1,3,3072]{2,0,1:T(1,128)}, u32[]{:S(2)}) copy-start(f32[1,3,3072]{2,0,1:T(1,128)} %param.16) | copy-start | bytes 110596
  87.5 16.9 %copy-start.12 = (f32[128,64]{1,0:T(8,128)S(1)}, f32[128,64]{1,0:T(8,128)}, u32[]{:S(2)}) copy-start(f32[128,64]{1,0:T(8,128)} %get-tuple-element.25.noised_ref) | copy-start | bytes 98308
  87.5 3.9 %collective-permute-start.3 = (bf16[64,3072]{1,0:T(8,128)(2,1)S(1)}, bf16[64,3072]{1,0:T(8,128)(2,1)S(1)}, u32[]{:S(2)}, u32[]{:S(2)}) collective-permute-start(bf16[64,3072]{1,0:T(8,128)(2,1)S(1)} %convolution_convert_fusion), channel_id=1, source_target_pairs={{0,1},{1,0},{2,3},{3,2},{4,5},{5,4},{6,7},{7,6},{8,9},{9,8},{10,11... | collective-permute-start | bytes 1179656 | tf_op jit(solution)/shard_map/ppermute | solution.py:390
  91.3 22.4 %copy-start.2 = (bf16[128,3072]{1,0:T(8,128)(2,1)S(1)}, bf16[128,3072]{1,0:T(8,128)(2,1)}, u32[]{:S(2)}) copy-start(bf16[128,3072]{1,0:T(8,128)(2,1)} %hidden_ref.3) | copy-start | bytes 2359300
  91.3 22.4 %copy-start.5 = (bf16[3072,64]{0,1:T(8,128)(2,1)S(1)}, bf16[3072,64]{0,1:T(8,128)(2,1)}, u32[]{:S(2)}) copy-start(bf16[3072,64]{0,1:T(8,128)(2,1)} %param.12) | copy-start | bytes 1179652
  91.3 22.4 %copy-start.11 = (f32[128,64]{1,0:T(8,128)S(1)}, f32[128,64]{1,0:T(8,128)}, u32[]{:S(2)}) copy-start(f32[128,64]{1,0:T(8,128)} %get-tuple-element.26.gap_ref) | copy-start | bytes 98308

commit v8 on v7

--- a/solution.py
+++ b/solution.py
@@ -242,6 +242,17 @@
         other_ref[i] = att_ref[2 * i + 1 - core].astype(BF16)
 
 
+def project_body(own_ref, other_ref, out_w_ref, y_own_ref, y_other_ref):
+    own = own_ref[...].reshape(-1, own_ref.shape[2])
+    other = other_ref[...].reshape(-1, own_ref.shape[2])
+    step = 512
+    for j in range(out_w_ref.shape[1] // step):
+        at = slice(j * step, (j + 1) * step)
+        out_w = out_w_ref[:, at]
+        y_other_ref[:, at] = dot(other, out_w).astype(BF16)
+        y_own_ref[:, at] = dot(own, out_w)
+
+
 def velocity_body(parts_ref, noised_ref, embed_ref, mod_ref, final_t_ref, v_ref):
     total = parts_ref[0].astype(F32)
     for i in range(1, parts_ref.shape[0]):
@@ -386,9 +397,13 @@
     att_own, att_other = call(
         text_body, (share, share), (image, text), scratch=(pltpu.VMEM((n_mp, own_rows, 3 * HD), F32),)
     )
-    y_other = dot(att_other.reshape(-1, 3 * HD), w_out[0]).astype(BF16)
+    y_own, y_other = call(
+        project_body,
+        (sds((rows_here // 2, width), F32), sds((rows_here // 2, width), BF16)),
+        (att_own, att_other, w_out[0]),
+    )
     y_other = lax.ppermute(y_other, "mp", [(i, i ^ 1) for i in range(n_mp)])
-    y = (dot(att_own.reshape(-1, 3 * HD), w_out[0]) + y_other.astype(F32)).astype(BF16)
+    y = (y_own + y_other.astype(F32)).astype(BF16)
     same_core = [[2 * x + core for x in range(n_mp // 2)] for core in range(2)]
     parts = exchange(y.reshape(n_mp // 2, own_rows, width), "mp", same_core)
     velocity = call(

time: 150 us -> 150 us (level)
    pallas_call x10 -> x11, Pallas kernels: 14.6 us -> 15.4 us  [call(): pl.pallas_call(body, out_shape=out_shape, in_specs=[scalars if i < smem e...]
where the time goes in v8:
time: 150 us
  blocking collectives  98.8 us (66%)
  starting transfers between devices  24.3 us (16%)
  Pallas kernels  15.4 us (10%)
  waiting for transfers between devices  5.9 us (4%)
  local copies, waits for them, and re-layouts  3.52 us (2%)
    all_to_all x6, blocking collectives, exchange(): lax.all_to_all(array, axis, 0, 0, axis_index_groups=groups, tiled=True)  98.8 us
    pallas_call x11, Pallas kernels, call(): pl.pallas_call(body, out_shape=out_shape, in_specs=[scalars if i < smem e...  15.4 us
    all_to_all x2, starting transfers between devices, exchange(): lax.all_to_all(array, axis, 0, 0, axis_index_groups=groups, tiled=True)  14.2 us
    ppermute x3, starting transfers between devices, on_device(): lax.ppermute(channels, 'mp', [(i, i ^ k) for i in range(n_mp)])  7.59 us
    unnamed x28, local copies, waits for them, and re-layouts  3.51 us
  transfers between devices with their start and end apart: 6, of which 3 were waited for; matrix products, arithmetic and copies ran while one was open for 0% of the time, Pallas kernels for 6%

profile of v8, /device:TPU:64, one launch (start us, length us, event | category | flops | bytes accessed | tf_op | source)
XLA Modules:
  0.0 149.5 jit_solution(9224157518736070158)
XLA Ops:
  0.6 2.3 %shard_map.130 = (bf16[8,80,128]{2,1,0:T(8,128)(2,1)}, s32[1]{0:T(128)}) custom-call(bf16[64,3072]{1,0:T(8,128)(2,1)} %bitcast.17, f32[3,1,3072]{2,1,0:T(1,128)} %bitcast.25, bf16[3,96,384]{2,1,0:T(8,128)(2,1)} %bitcast.29), custom_call_target="tpu_custom_call" | custom-call | tf_op jit(solution)/shard_map/pallas_call | solution.py:29
  2.9 8.3 %all-to-all-start = ((bf16[8,80,128]{2,1,0:T(8,128)(2,1)}), bf16[8,80,128]{2,1,0:T(8,128)(2,1)S(1)}, u32[]{:S(2)}, u32[]{:S(2)}) async-start(bf16[8,80,128]{2,1,0:T(8,128)(2,1)} %get-tuple-element.22), calls=%async_computation | async-start | bytes 327680 | tf_op jit(solution)/shard_map/all_to_all | solution.py:337
  11.9 0.0 copy-start.13
  11.9 3.9 %shard_map.131 = (f32[128,64]{1,0:T(8,128)}, f32[128,64]{1,0:T(8,128)}, bf16[160,128]{1,0:T(8,128)(2,1)}) custom-call(s32[1]{0:T(128)S(6)} %copy.14.level_ref.refs_0_, s32[1]{0:T(128)} %get-tuple-element.20._, bf16[128,3072]{1,0:T(8,128)(2,1)} %hidden_ref.3, bf16[64,3072]{1,0:T(8,128)(2,1)} %bitcast.22, bf16[64,128]{1,0:T(8,128)(2,1)} %bitcast.31, ...), custom_call_target="tpu_custom_call" | custom-call | tf_op jit(solution)/shard_map/pallas_call | solution.py:29
  15.9 2.1 %all-to-all-done.recv_ref = bf16[8,80,128]{2,1,0:T(8,128)(2,1)S(1)} async-done(((bf16[8,80,128]{2,1,0:T(8,128)(2,1)}), bf16[8,80,128]{2,1,0:T(8,128)(2,1)S(1)}, u32[]{:S(2)}, u32[]{:S(2)}) %all-to-all-start) | async-done | bytes 163872 | tf_op jit(solution)/shard_map/all_to_all | solution.py:337
  17.9 0.8 copy-done.8
  18.7 27.8 %all_to_all.40.recv_ref = bf16[4,192,128]{2,1,0:T(8,128)(2,1)S(1)} all-to-all(bf16[4,192,128]{2,1,0:T(8,128)(2,1)S(1)} %shard_map.132), channel_id=1, replica_groups=mesh['role'=2,'z_far'=4,'z_near'=4,'y_hi'=2,'mp'=8] {'z_far'}, dimensions={0} | all-to-all | bytes 393216 | tf_op jit(solution)/shard_map/all_to_all | solution.py:337
  46.5 0.1 shard_map.133
  46.7 0.0 copy-start.6
  46.7 0.9 copy-done.6
  47.6 15.3 %all_to_all.41.recv_ref = bf16[8,144,128]{2,1,0:T(8,128)(2,1)S(1)} all-to-all(bf16[8,144,128]{2,1,0:T(8,128)(2,1)S(1)} %get-tuple-element.23), channel_id=1, replica_groups=mesh['role'=2,'z_far'=4,'z_near'=4,'y_hi'=2,'mp'=8] {'z_near','y_hi'}, dimensions={0} | all-to-all | bytes 589824 | tf_op jit(solution)/shard_map/all_to_all | solution.py:337
  62.9 5.9 %all-to-all-start.3 = ((bf16[8,384,128]{2,1,0:T(8,128)(2,1)}), bf16[8,384,128]{2,1,0:T(8,128)(2,1)S(1)}, u32[]{:S(2)}, u32[]{:S(2)}) async-start(bf16[8,384,128]{2,1,0:T(8,128)(2,1)} %copy-done.6), calls=%async_computation.3 | async-start | bytes 1572864 | tf_op jit(solution)/shard_map/all_to_all | solution.py:337
  68.8 1.9 %collective-permute-start.2 = (bf16[8,64,128]{2,1,0:T(8,128)(2,1)S(1)}, bf16[8,64,128]{2,1,0:T(8,128)(2,1)S(1)}, u32[]{:S(2)}, u32[]{:S(2)}) collective-permute-start(bf16[8,64,128]{2,1,0:T(8,128)(2,1)S(1)} %slice.4), channel_id=1, source_target_pairs={{0,3},{1,2},{2,1},{3,0},{4,7},{5,6},{6,5},{7,4},{8,11},{9,10},{10,... | collective-permute-start | bytes 393224 | tf_op jit(solution)/shard_map/ppermute | solution.py:380
  70.7 3.4 %collective-permute-start.1 = (bf16[8,64,128]{2,1,0:T(8,128)(2,1)S(1)}, bf16[8,64,128]{2,1,0:T(8,128)(2,1)S(1)}, u32[]{:S(2)}, u32[]{:S(2)}) collective-permute-start(bf16[8,64,128]{2,1,0:T(8,128)(2,1)S(1)} %slice.4), channel_id=1, source_target_pairs={{0,2},{1,3},{2,0},{3,1},{4,6},{5,7},{6,4},{7,5},{8,10},{9,11},{10,... | collective-permute-start | bytes 393224 | tf_op jit(solution)/shard_map/ppermute | solution.py:380
  74.1 2.3 %collective-permute-start = (bf16[8,64,128]{2,1,0:T(8,128)(2,1)S(1)}, bf16[8,64,128]{2,1,0:T(8,128)(2,1)S(1)}, u32[]{:S(2)}, u32[]{:S(2)}) collective-permute-start(bf16[8,64,128]{2,1,0:T(8,128)(2,1)S(1)} %slice.4), channel_id=1, source_target_pairs={{0,1},{1,0},{2,3},{3,2},{4,5},{5,4},{6,7},{7,6},{8,9},{9,8},{10,11... | collective-permute-start | bytes 393224 | tf_op jit(solution)/shard_map/ppermute | solution.py:380
  76.4 0.0 collective-permute-done.2.other3_ref
  76.4 2.5 %collective-permute-done.1.other2_ref = bf16[8,64,128]{2,1,0:T(8,128)(2,1)S(1)} collective-permute-done((bf16[8,64,128]{2,1,0:T(8,128)(2,1)S(1)}, bf16[8,64,128]{2,1,0:T(8,128)(2,1)S(1)}, u32[]{:S(2)}, u32[]{:S(2)}) %collective-permute-start.1) | collective-permute-done | bytes 131104 | tf_op jit(solution)/shard_map/ppermute | solution.py:380
  78.9 0.0 collective-permute-done.other1_ref
  78.9 0.0 copy-done.13
  78.9 0.0 copy-done.9
  78.9 4.8 %shard_map.134.image_ref = f32[7,128,128]{2,1,0:T(8,128)S(1)} custom-call(bf16[160,128]{1,0:T(8,128)(2,1)S(1)} %copy-done.9, bf16[8,144,128]{2,1,0:T(8,128)(2,1)S(1)} %all_to_all.41.recv_ref, bf16[8,64,128]{2,1,0:T(8,128)(2,1)S(1)} %collective-permute-done.other1_ref, bf16[8,64,128]{2,1,0:T(8,128)(2,1)S(1)} %collective-permute-done.1.other2_ref, ...), custom_call_target="tpu_custom_call" | custom-call | tf_op jit(solution)/shard_map/pallas_call | solution.py:29
  83.7 0.0 copy-start.3
  83.7 0.8 copy-done.3
  84.5 0.0 all-to-all-done.3
  84.5 1.0 copy-done.4
  85.5 1.3 shard_map.135
  86.8 0.0 copy-done.2
  86.8 0.0 copy-start
  86.9 0.0 copy-start.7
  86.9 0.0 copy-start.10
  86.9 0.0 copy-start.12
  86.9 1.0 shard_map.136
  87.9 0.0 copy-start.1
  87.9 0.0 copy-start.5
  87.9 0.0 copy-start.11
  87.9 2.5 %collective-permute-start.3 = (bf16[64,3072]{1,0:T(8,128)(2,1)S(1)}, bf16[64,3072]{1,0:T(8,128)(2,1)S(1)}, u32[]{:S(2)}, u32[]{:S(2)}) collective-permute-start(bf16[64,3072]{1,0:T(8,128)(2,1)S(1)} %get-tuple-element.28), channel_id=1, source_target_pairs={{0,1},{1,0},{2,3},{3,2},{4,5},{5,4},{6,7},{7,6},{8,9},{9,8},{10,11... | collective-permute-start | bytes 1179656 | tf_op jit(solution)/shard_map/ppermute | solution.py:405
  90.4 1.3 collective-permute-done.3
  91.8 0.1 add_convert_fusion
  91.9 12.5 %all_to_all.42.parts_ref = bf16[4,16,3072]{2,1,0:T(8,128)(2,1)S(1)} all-to-all(bf16[4,16,3072]{2,1,0:T(8,128)(2,1)S(1)} %bitcast.28), channel_id=1, replica_groups={{0,2,4,6},{1,3,5,7},{8,10,12,14},{9,11,13,15},{16,18,20,22},{17,19,21,2..., dimensions={0} | all-to-all | bytes 786432 | tf_op jit(solution)/shard_map/all_to_all | solution.py:337
  104.3 0.0 copy-done
  104.3 0.0 copy-done.7
  104.3 0.0 copy-done.10
  104.3 0.6 shard_map.137
  105.0 8.7 %all_to_all.43.both_ref = f32[16,8,128]{2,1,0:T(8,128)S(1)} all-to-all(f32[16,8,128]{2,1,0:T(8,128)S(1)} %shard_map.137), channel_id=1, replica_groups=mesh['role'=2,'z_far'=4,'z_near'=4,'y_hi'=2,'mp'=8] {'role','mp'}, dimensions={0} | all-to-all | bytes 131072 | tf_op jit(solution)/shard_map/all_to_all | solution.py:337
  113.7 0.4 shard_map.138
  114.1 15.4 %all_to_all.44.recv_ref = bf16[8,104,128]{2,1,0:T(8,128)(2,1)S(1)} all-to-all(bf16[8,104,128]{2,1,0:T(8,128)(2,1)S(1)} %get-tuple-element.31), channel_id=1, replica_groups=mesh['role'=2,'z_far'=4,'z_near'=4,'y_hi'=2,'mp'=8] {'z_near','y_hi'}, dimensions={0} | all-to-all | bytes 425984 | tf_op jit(solution)/shard_map/all_to_all | solution.py:337
  129.5 19.1 %all_to_all.45.refs_1_ = bf16[4,104,128]{2,1,0:T(8,128)(2,1)S(1)} all-to-all(bf16[4,104,128]{2,1,0:T(8,128)(2,1)S(1)} %shard_map.139), channel_id=1, replica_groups=mesh['role'=2,'z_far'=4,'z_near'=4,'y_hi'=2,'mp'=8] {'z_far'}, dimensions={0} | all-to-all | bytes 212992 | tf_op jit(solution)/shard_map/all_to_all | solution.py:337
  148.6 0.9 shard_map.140
  (11 shorter events, 0.1 us)
Async XLA Ops:
  2.9 15.0 %all-to-all-start = ((bf16[8,80,128]{2,1,0:T(8,128)(2,1)}), bf16[8,80,128]{2,1,0:T(8,128)(2,1)S(1)}, u32[]{:S(2)}, u32[]{:S(2)}) async-start(bf16[8,80,128]{2,1,0:T(8,128)(2,1)} %get-tuple-element.22), calls=%async_computation | async-start | bytes 327680 | tf_op jit(solution)/shard_map/all_to_all | solution.py:337
  11.9 67.0 %copy-start.13 = (f32[1,2,128]{2,1,0:T(2,128)S(1)}, f32[1,2,128]{2,1,0:T(2,128)}, u32[]{:S(2)}) copy-start(f32[1,2,128]{2,1,0:T(2,128)} %param.18) | copy-start | bytes 3076
  17.9 0.8 copy-start.8
  18.7 60.2 %copy-start.9 = (bf16[160,128]{1,0:T(8,128)(2,1)S(1)}, bf16[160,128]{1,0:T(8,128)(2,1)}, u32[]{:S(2)}) copy-start(bf16[160,128]{1,0:T(8,128)(2,1)} %get-tuple-element.21.send_ref) | copy-start | bytes 122884
  46.7 0.9 copy-start.6
  47.6 39.3 %copy-start.2 = (bf16[1,384,3072]{2,1,0:T(8,128)(2,1)S(1)}, bf16[1,384,3072]{2,1,0:T(8,128)(2,1)}, u32[]{:S(2)}) copy-start(bf16[1,384,3072]{2,1,0:T(8,128)(2,1)} %param.20) | copy-start | bytes 7077892
  62.9 21.6 %all-to-all-start.3 = ((bf16[8,384,128]{2,1,0:T(8,128)(2,1)}), bf16[8,384,128]{2,1,0:T(8,128)(2,1)S(1)}, u32[]{:S(2)}, u32[]{:S(2)}) async-start(bf16[8,384,128]{2,1,0:T(8,128)(2,1)} %copy-done.6), calls=%async_computation.3 | async-start | bytes 1572864 | tf_op jit(solution)/shard_map/all_to_all | solution.py:337
  68.8 7.6 %collective-permute-start.2 = (bf16[8,64,128]{2,1,0:T(8,128)(2,1)S(1)}, bf16[8,64,128]{2,1,0:T(8,128)(2,1)S(1)}, u32[]{:S(2)}, u32[]{:S(2)}) collective-permute-start(bf16[8,64,128]{2,1,0:T(8,128)(2,1)S(1)} %slice.4), channel_id=1, source_target_pairs={{0,3},{1,2},{2,1},{3,0},{4,7},{5,6},{6,5},{7,4},{8,11},{9,10},{10,... | collective-permute-start | bytes 393224 | tf_op jit(solution)/shard_map/ppermute | solution.py:380
  70.7 8.2 %collective-permute-start.1 = (bf16[8,64,128]{2,1,0:T(8,128)(2,1)S(1)}, bf16[8,64,128]{2,1,0:T(8,128)(2,1)S(1)}, u32[]{:S(2)}, u32[]{:S(2)}) collective-permute-start(bf16[8,64,128]{2,1,0:T(8,128)(2,1)S(1)} %slice.4), channel_id=1, source_target_pairs={{0,2},{1,3},{2,0},{3,1},{4,6},{5,7},{6,4},{7,5},{8,10},{9,11},{10,... | collective-permute-start | bytes 393224 | tf_op jit(solution)/shard_map/ppermute | solution.py:380
  74.1 4.8 %collective-permute-start = (bf16[8,64,128]{2,1,0:T(8,128)(2,1)S(1)}, bf16[8,64,128]{2,1,0:T(8,128)(2,1)S(1)}, u32[]{:S(2)}, u32[]{:S(2)}) collective-permute-start(bf16[8,64,128]{2,1,0:T(8,128)(2,1)S(1)} %slice.4), channel_id=1, source_target_pairs={{0,1},{1,0},{2,3},{3,2},{4,5},{5,4},{6,7},{7,6},{8,9},{9,8},{10,11... | collective-permute-start | bytes 393224 | tf_op jit(solution)/shard_map/ppermute | solution.py:380
  83.7 0.8 copy-start.3
  84.5 1.0 copy-start.4
  86.8 17.5 %copy-start = (bf16[1,64,3072]{2,1,0:T(8,128)(2,1)S(1)}, bf16[1,64,3072]{2,1,0:T(8,128)(2,1)}, u32[]{:S(2)}) copy-start(bf16[1,64,3072]{2,1,0:T(8,128)(2,1)} %param.15) | copy-start | bytes 1179652
  86.9 17.5 %copy-start.7 = (bf16[1,3072,64]{1,2,0:T(8,128)(2,1)S(1)}, bf16[1,3072,64]{1,2,0:T(8,128)(2,1)}, u32[]{:S(2)}) copy-start(bf16[1,3072,64]{1,2,0:T(8,128)(2,1)} %param.21) | copy-start | bytes 1179652
  86.9 17.5 %copy-start.10 = (f32[1,3,3072]{2,0,1:T(1,128)S(1)}, f32[1,3,3072]{2,0,1:T(1,128)}, u32[]{:S(2)}) copy-start(f32[1,3,3072]{2,0,1:T(1,128)} %param.16) | copy-start | bytes 110596
  86.9 17.5 %copy-start.12 = (f32[128,64]{1,0:T(8,128)S(1)}, f32[128,64]{1,0:T(8,128)}, u32[]{:S(2)}) copy-start(f32[128,64]{1,0:T(8,128)} %get-tuple-element.29.noised_ref) | copy-start | bytes 98308
  87.9 25.8 %copy-start.1 = (bf16[128,3072]{1,0:T(8,128)(2,1)S(1)}, bf16[128,3072]{1,0:T(8,128)(2,1)}, u32[]{:S(2)}) copy-start(bf16[128,3072]{1,0:T(8,128)(2,1)} %hidden_ref.3) | copy-start | bytes 2359300
  87.9 25.8 %copy-start.5 = (bf16[3072,64]{0,1:T(8,128)(2,1)S(1)}, bf16[3072,64]{0,1:T(8,128)(2,1)}, u32[]{:S(2)}) copy-start(bf16[3072,64]{0,1:T(8,128)(2,1)} %param.12) | copy-start | bytes 1179652
  87.9 25.8 %copy-start.11 = (f32[128,64]{1,0:T(8,128)S(1)}, f32[128,64]{1,0:T(8,128)}, u32[]{:S(2)}) copy-start(f32[128,64]{1,0:T(8,128)} %get-tuple-element.30.gap_ref) | copy-start | bytes 98308
  87.9 3.9 %collective-permute-start.3 = (bf16[64,3072]{1,0:T(8,128)(2,1)S(1)}, bf16[64,3072]{1,0:T(8,128)(2,1)S(1)}, u32[]{:S(2)}, u32[]{:S(2)}) collective-permute-start(bf16[64,3072]{1,0:T(8,128)(2,1)S(1)} %get-tuple-element.28), channel_id=1, source_target_pairs={{0,1},{1,0},{2,3},{3,2},{4,5},{5,4},{6,7},{7,6},{8,9},{9,8},{10,11... | collective-permute-start | bytes 1179656 | tf_op jit(solution)/shard_map/ppermute | solution.py:405

commit v9 on v8

--- a/solution.py
+++ b/solution.py
@@ -140,7 +140,7 @@
     send_ref, recv_ref, other1_ref, other2_ref, other3_ref, gain_ref, out_ref, lat_ref, s_ref, v_ref, m_ref, own_ref, sum_ref
 ):
     tokens = lat_ref.shape[1]
-    chunk = 2048
+    chunk = 4096
     n_chunks = tokens // chunk
     ones = jnp.where(lax.broadcasted_iota(jnp.int32, (MROWS - CHANS, HD), 0) == 0, 1.0, 0.0).astype(BF16)
     other_refs = (other1_ref, other2_ref, other3_ref)

time: 150 us -> 150 us (level)
  transfers between devices with their start and end apart: 6 -> 6, of which waited for: 3 -> 4; matrix products, arithmetic and copies ran while one was open for 0% -> 0% of each run, Pallas kernels for 6% -> 5%
where the time goes in v9:
time: 150 us
  blocking collectives  99.6 us (66%)
  starting transfers between devices  24.1 us (16%)
  Pallas kernels  14.5 us (10%)
  waiting for transfers between devices  6.28 us (4%)
  local copies, waits for them, and re-layouts  3.52 us (2%)
    all_to_all x6, blocking collectives, exchange(): lax.all_to_all(array, axis, 0, 0, axis_index_groups=groups, tiled=True)  99.6 us
    pallas_call x11, Pallas kernels, call(): pl.pallas_call(body, out_shape=out_shape, in_specs=[scalars if i < smem e...  14.5 us
    all_to_all x2, starting transfers between devices, exchange(): lax.all_to_all(array, axis, 0, 0, axis_index_groups=groups, tiled=True)  14.2 us
    ppermute x3, starting transfers between devices, on_device(): lax.ppermute(channels, 'mp', [(i, i ^ k) for i in range(n_mp)])  7.59 us
    unnamed x28, local copies, waits for them, and re-layouts  3.51 us
  transfers between devices with their start and end apart: 6, of which 4 were waited for; matrix products, arithmetic and copies ran while one was open for 0% of the time, Pallas kernels for 5%

profile of v9, /device:TPU:64, one launch (start us, length us, event | category | flops | bytes accessed | tf_op | source)
XLA Modules:
  0.0 149.5 jit_solution(13437156378426814701)
XLA Ops:
  0.6 2.3 %shard_map.130 = (bf16[8,80,128]{2,1,0:T(8,128)(2,1)}, s32[1]{0:T(128)}) custom-call(bf16[64,3072]{1,0:T(8,128)(2,1)} %bitcast.17, f32[3,1,3072]{2,1,0:T(1,128)} %bitcast.25, bf16[3,96,384]{2,1,0:T(8,128)(2,1)} %bitcast.29), custom_call_target="tpu_custom_call" | custom-call | tf_op jit(solution)/shard_map/pallas_call | solution.py:29
  2.9 8.3 %all-to-all-start = ((bf16[8,80,128]{2,1,0:T(8,128)(2,1)}), bf16[8,80,128]{2,1,0:T(8,128)(2,1)S(1)}, u32[]{:S(2)}, u32[]{:S(2)}) async-start(bf16[8,80,128]{2,1,0:T(8,128)(2,1)} %get-tuple-element.22), calls=%async_computation | async-start | bytes 327680 | tf_op jit(solution)/shard_map/all_to_all | solution.py:337
  11.9 0.0 copy-start.13
  11.9 3.9 %shard_map.131 = (f32[128,64]{1,0:T(8,128)}, f32[128,64]{1,0:T(8,128)}, bf16[160,128]{1,0:T(8,128)(2,1)}) custom-call(s32[1]{0:T(128)S(6)} %copy.14.level_ref.refs_0_, s32[1]{0:T(128)} %get-tuple-element.20._, bf16[128,3072]{1,0:T(8,128)(2,1)} %hidden_ref.3, bf16[64,3072]{1,0:T(8,128)(2,1)} %bitcast.22, bf16[64,128]{1,0:T(8,128)(2,1)} %bitcast.31, ...), custom_call_target="tpu_custom_call" | custom-call | tf_op jit(solution)/shard_map/pallas_call | solution.py:29
  15.9 2.1 %all-to-all-done.recv_ref = bf16[8,80,128]{2,1,0:T(8,128)(2,1)S(1)} async-done(((bf16[8,80,128]{2,1,0:T(8,128)(2,1)}), bf16[8,80,128]{2,1,0:T(8,128)(2,1)S(1)}, u32[]{:S(2)}, u32[]{:S(2)}) %all-to-all-start) | async-done | bytes 163872 | tf_op jit(solution)/shard_map/all_to_all | solution.py:337
  17.9 0.8 copy-done.8
  18.7 27.8 %all_to_all.40.recv_ref = bf16[4,192,128]{2,1,0:T(8,128)(2,1)S(1)} all-to-all(bf16[4,192,128]{2,1,0:T(8,128)(2,1)S(1)} %shard_map.132), channel_id=1, replica_groups=mesh['role'=2,'z_far'=4,'z_near'=4,'y_hi'=2,'mp'=8] {'z_far'}, dimensions={0} | all-to-all | bytes 393216 | tf_op jit(solution)/shard_map/all_to_all | solution.py:337
  46.5 0.1 shard_map.133
  46.7 0.0 copy-start.6
  46.7 0.9 copy-done.6
  47.6 15.3 %all_to_all.41.recv_ref = bf16[8,144,128]{2,1,0:T(8,128)(2,1)S(1)} all-to-all(bf16[8,144,128]{2,1,0:T(8,128)(2,1)S(1)} %get-tuple-element.23), channel_id=1, replica_groups=mesh['role'=2,'z_far'=4,'z_near'=4,'y_hi'=2,'mp'=8] {'z_near','y_hi'}, dimensions={0} | all-to-all | bytes 589824 | tf_op jit(solution)/shard_map/all_to_all | solution.py:337
  62.9 5.9 %all-to-all-start.3 = ((bf16[8,384,128]{2,1,0:T(8,128)(2,1)}), bf16[8,384,128]{2,1,0:T(8,128)(2,1)S(1)}, u32[]{:S(2)}, u32[]{:S(2)}) async-start(bf16[8,384,128]{2,1,0:T(8,128)(2,1)} %copy-done.6), calls=%async_computation.3 | async-start | bytes 1572864 | tf_op jit(solution)/shard_map/all_to_all | solution.py:337
  68.8 1.9 %collective-permute-start.2 = (bf16[8,64,128]{2,1,0:T(8,128)(2,1)S(1)}, bf16[8,64,128]{2,1,0:T(8,128)(2,1)S(1)}, u32[]{:S(2)}, u32[]{:S(2)}) collective-permute-start(bf16[8,64,128]{2,1,0:T(8,128)(2,1)S(1)} %slice.4), channel_id=1, source_target_pairs={{0,3},{1,2},{2,1},{3,0},{4,7},{5,6},{6,5},{7,4},{8,11},{9,10},{10,... | collective-permute-start | bytes 393224 | tf_op jit(solution)/shard_map/ppermute | solution.py:380
  70.7 3.4 %collective-permute-start.1 = (bf16[8,64,128]{2,1,0:T(8,128)(2,1)S(1)}, bf16[8,64,128]{2,1,0:T(8,128)(2,1)S(1)}, u32[]{:S(2)}, u32[]{:S(2)}) collective-permute-start(bf16[8,64,128]{2,1,0:T(8,128)(2,1)S(1)} %slice.4), channel_id=1, source_target_pairs={{0,2},{1,3},{2,0},{3,1},{4,6},{5,7},{6,4},{7,5},{8,10},{9,11},{10,... | collective-permute-start | bytes 393224 | tf_op jit(solution)/shard_map/ppermute | solution.py:380
  74.1 2.3 %collective-permute-start = (bf16[8,64,128]{2,1,0:T(8,128)(2,1)S(1)}, bf16[8,64,128]{2,1,0:T(8,128)(2,1)S(1)}, u32[]{:S(2)}, u32[]{:S(2)}) collective-permute-start(bf16[8,64,128]{2,1,0:T(8,128)(2,1)S(1)} %slice.4), channel_id=1, source_target_pairs={{0,1},{1,0},{2,3},{3,2},{4,5},{5,4},{6,7},{7,6},{8,9},{9,8},{10,11... | collective-permute-start | bytes 393224 | tf_op jit(solution)/shard_map/ppermute | solution.py:380
  76.4 0.0 collective-permute-done.2.other3_ref
  76.4 2.5 %collective-permute-done.1.other2_ref = bf16[8,64,128]{2,1,0:T(8,128)(2,1)S(1)} collective-permute-done((bf16[8,64,128]{2,1,0:T(8,128)(2,1)S(1)}, bf16[8,64,128]{2,1,0:T(8,128)(2,1)S(1)}, u32[]{:S(2)}, u32[]{:S(2)}) %collective-permute-start.1) | collective-permute-done | bytes 131104 | tf_op jit(solution)/shard_map/ppermute | solution.py:380
  78.9 0.0 collective-permute-done.other1_ref
  78.9 0.0 copy-done.13
  78.9 0.0 copy-done.9
  78.9 3.9 %shard_map.134.image_ref = f32[7,128,128]{2,1,0:T(8,128)S(1)} custom-call(bf16[160,128]{1,0:T(8,128)(2,1)S(1)} %copy-done.9, bf16[8,144,128]{2,1,0:T(8,128)(2,1)S(1)} %all_to_all.41.recv_ref, bf16[8,64,128]{2,1,0:T(8,128)(2,1)S(1)} %collective-permute-done.other1_ref, bf16[8,64,128]{2,1,0:T(8,128)(2,1)S(1)} %collective-permute-done.1.other2_ref, ...), custom_call_target="tpu_custom_call" | custom-call | tf_op jit(solution)/shard_map/pallas_call | solution.py:29
  82.8 0.0 copy-start.3
  82.8 0.8 copy-done.3
  83.6 0.3 all-to-all-done.3
  83.8 1.0 copy-done.4
  84.9 1.3 shard_map.135
  86.2 0.0 copy-done.2
  86.2 0.0 copy-start
  86.2 0.0 copy-start.7
  86.2 0.0 copy-start.10
  86.2 0.0 copy-start.12
  86.2 1.0 shard_map.136
  87.2 0.0 copy-start.1
  87.2 0.0 copy-start.5
  87.2 0.0 copy-start.11
  87.2 2.3 %collective-permute-start.3 = (bf16[64,3072]{1,0:T(8,128)(2,1)S(1)}, bf16[64,3072]{1,0:T(8,128)(2,1)S(1)}, u32[]{:S(2)}, u32[]{:S(2)}) collective-permute-start(bf16[64,3072]{1,0:T(8,128)(2,1)S(1)} %get-tuple-element.28), channel_id=1, source_target_pairs={{0,1},{1,0},{2,3},{3,2},{4,5},{5,4},{6,7},{7,6},{8,9},{9,8},{10,11... | collective-permute-start | bytes 1179656 | tf_op jit(solution)/shard_map/ppermute | solution.py:405
  89.5 1.5 collective-permute-done.3
  91.0 0.1 add_convert_fusion
  91.1 12.5 %all_to_all.42.parts_ref = bf16[4,16,3072]{2,1,0:T(8,128)(2,1)S(1)} all-to-all(bf16[4,16,3072]{2,1,0:T(8,128)(2,1)S(1)} %bitcast.28), channel_id=1, replica_groups={{0,2,4,6},{1,3,5,7},{8,10,12,14},{9,11,13,15},{16,18,20,22},{17,19,21,2..., dimensions={0} | all-to-all | bytes 786432 | tf_op jit(solution)/shard_map/all_to_all | solution.py:337
  103.5 0.0 copy-done
  103.5 0.0 copy-done.12
  103.6 0.6 shard_map.137
  104.2 8.7 %all_to_all.43.both_ref = f32[16,8,128]{2,1,0:T(8,128)S(1)} all-to-all(f32[16,8,128]{2,1,0:T(8,128)S(1)} %shard_map.137), channel_id=1, replica_groups=mesh['role'=2,'z_far'=4,'z_near'=4,'y_hi'=2,'mp'=8] {'role','mp'}, dimensions={0} | all-to-all | bytes 131072 | tf_op jit(solution)/shard_map/all_to_all | solution.py:337
  112.9 0.0 copy-done.11
  112.9 0.4 shard_map.138
  113.3 15.3 %all_to_all.44.recv_ref = bf16[8,104,128]{2,1,0:T(8,128)(2,1)S(1)} all-to-all(bf16[8,104,128]{2,1,0:T(8,128)(2,1)S(1)} %get-tuple-element.31), channel_id=1, replica_groups=mesh['role'=2,'z_far'=4,'z_near'=4,'y_hi'=2,'mp'=8] {'z_near','y_hi'}, dimensions={0} | all-to-all | bytes 425984 | tf_op jit(solution)/shard_map/all_to_all | solution.py:337
  128.6 20.0 %all_to_all.45.refs_1_ = bf16[4,104,128]{2,1,0:T(8,128)(2,1)S(1)} all-to-all(bf16[4,104,128]{2,1,0:T(8,128)(2,1)S(1)} %shard_map.139), channel_id=1, replica_groups=mesh['role'=2,'z_far'=4,'z_near'=4,'y_hi'=2,'mp'=8] {'z_far'}, dimensions={0} | all-to-all | bytes 212992 | tf_op jit(solution)/shard_map/all_to_all | solution.py:337
  148.6 0.9 shard_map.140
  (11 shorter events, 0.1 us)
Async XLA Ops:
  2.9 15.0 %all-to-all-start = ((bf16[8,80,128]{2,1,0:T(8,128)(2,1)}), bf16[8,80,128]{2,1,0:T(8,128)(2,1)S(1)}, u32[]{:S(2)}, u32[]{:S(2)}) async-start(bf16[8,80,128]{2,1,0:T(8,128)(2,1)} %get-tuple-element.22), calls=%async_computation | async-start | bytes 327680 | tf_op jit(solution)/shard_map/all_to_all | solution.py:337
  11.9 67.0 %copy-start.13 = (f32[1,2,128]{2,1,0:T(2,128)S(1)}, f32[1,2,128]{2,1,0:T(2,128)}, u32[]{:S(2)}) copy-start(f32[1,2,128]{2,1,0:T(2,128)} %param.18) | copy-start | bytes 3076
  17.9 0.8 copy-start.8
  18.7 60.2 %copy-start.9 = (bf16[160,128]{1,0:T(8,128)(2,1)S(1)}, bf16[160,128]{1,0:T(8,128)(2,1)}, u32[]{:S(2)}) copy-start(bf16[160,128]{1,0:T(8,128)(2,1)} %get-tuple-element.21.send_ref) | copy-start | bytes 122884
  46.7 0.9 copy-start.6
  47.6 38.6 %copy-start.2 = (bf16[1,384,3072]{2,1,0:T(8,128)(2,1)S(1)}, bf16[1,384,3072]{2,1,0:T(8,128)(2,1)}, u32[]{:S(2)}) copy-start(bf16[1,384,3072]{2,1,0:T(8,128)(2,1)} %param.20) | copy-start | bytes 7077892
  62.9 20.9 %all-to-all-start.3 = ((bf16[8,384,128]{2,1,0:T(8,128)(2,1)}), bf16[8,384,128]{2,1,0:T(8,128)(2,1)S(1)}, u32[]{:S(2)}, u32[]{:S(2)}) async-start(bf16[8,384,128]{2,1,0:T(8,128)(2,1)} %copy-done.6), calls=%async_computation.3 | async-start | bytes 1572864 | tf_op jit(solution)/shard_map/all_to_all | solution.py:337
  68.8 7.6 %collective-permute-start.2 = (bf16[8,64,128]{2,1,0:T(8,128)(2,1)S(1)}, bf16[8,64,128]{2,1,0:T(8,128)(2,1)S(1)}, u32[]{:S(2)}, u32[]{:S(2)}) collective-permute-start(bf16[8,64,128]{2,1,0:T(8,128)(2,1)S(1)} %slice.4), channel_id=1, source_target_pairs={{0,3},{1,2},{2,1},{3,0},{4,7},{5,6},{6,5},{7,4},{8,11},{9,10},{10,... | collective-permute-start | bytes 393224 | tf_op jit(solution)/shard_map/ppermute | solution.py:380
  70.7 8.2 %collective-permute-start.1 = (bf16[8,64,128]{2,1,0:T(8,128)(2,1)S(1)}, bf16[8,64,128]{2,1,0:T(8,128)(2,1)S(1)}, u32[]{:S(2)}, u32[]{:S(2)}) collective-permute-start(bf16[8,64,128]{2,1,0:T(8,128)(2,1)S(1)} %slice.4), channel_id=1, source_target_pairs={{0,2},{1,3},{2,0},{3,1},{4,6},{5,7},{6,4},{7,5},{8,10},{9,11},{10,... | collective-permute-start | bytes 393224 | tf_op jit(solution)/shard_map/ppermute | solution.py:380
  74.1 4.8 %collective-permute-start = (bf16[8,64,128]{2,1,0:T(8,128)(2,1)S(1)}, bf16[8,64,128]{2,1,0:T(8,128)(2,1)S(1)}, u32[]{:S(2)}, u32[]{:S(2)}) collective-permute-start(bf16[8,64,128]{2,1,0:T(8,128)(2,1)S(1)} %slice.4), channel_id=1, source_target_pairs={{0,1},{1,0},{2,3},{3,2},{4,5},{5,4},{6,7},{7,6},{8,9},{9,8},{10,11... | collective-permute-start | bytes 393224 | tf_op jit(solution)/shard_map/ppermute | solution.py:380
  82.8 0.8 copy-start.3
  83.8 1.0 copy-start.4
  86.2 17.3 %copy-start = (bf16[1,64,3072]{2,1,0:T(8,128)(2,1)S(1)}, bf16[1,64,3072]{2,1,0:T(8,128)(2,1)}, u32[]{:S(2)}) copy-start(bf16[1,64,3072]{2,1,0:T(8,128)(2,1)} %param.15) | copy-start | bytes 1179652
  86.2 17.3 %copy-start.7 = (bf16[1,3072,64]{1,2,0:T(8,128)(2,1)S(1)}, bf16[1,3072,64]{1,2,0:T(8,128)(2,1)}, u32[]{:S(2)}) copy-start(bf16[1,3072,64]{1,2,0:T(8,128)(2,1)} %param.21) | copy-start | bytes 1179652
  86.2 17.3 %copy-start.10 = (f32[1,3,3072]{2,0,1:T(1,128)S(1)}, f32[1,3,3072]{2,0,1:T(1,128)}, u32[]{:S(2)}) copy-start(f32[1,3,3072]{2,0,1:T(1,128)} %param.16) | copy-start | bytes 110596
  86.2 17.3 %copy-start.12 = (f32[128,64]{1,0:T(8,128)S(1)}, f32[128,64]{1,0:T(8,128)}, u32[]{:S(2)}) copy-start(f32[128,64]{1,0:T(8,128)} %get-tuple-element.29.noised_ref) | copy-start | bytes 98308
  87.2 25.7 %copy-start.1 = (bf16[128,3072]{1,0:T(8,128)(2,1)S(1)}, bf16[128,3072]{1,0:T(8,128)(2,1)}, u32[]{:S(2)}) copy-start(bf16[128,3072]{1,0:T(8,128)(2,1)} %hidden_ref.3) | copy-start | bytes 2359300
  87.2 25.7 %copy-start.5 = (bf16[3072,64]{0,1:T(8,128)(2,1)S(1)}, bf16[3072,64]{0,1:T(8,128)(2,1)}, u32[]{:S(2)}) copy-start(bf16[3072,64]{0,1:T(8,128)(2,1)} %param.12) | copy-start | bytes 1179652
  87.2 25.7 %copy-start.11 = (f32[128,64]{1,0:T(8,128)S(1)}, f32[128,64]{1,0:T(8,128)}, u32[]{:S(2)}) copy-start(f32[128,64]{1,0:T(8,128)} %get-tuple-element.30.gap_ref) | copy-start | bytes 98308
  87.2 3.7 %collective-permute-start.3 = (bf16[64,3072]{1,0:T(8,128)(2,1)S(1)}, bf16[64,3072]{1,0:T(8,128)(2,1)S(1)}, u32[]{:S(2)}, u32[]{:S(2)}) collective-permute-start(bf16[64,3072]{1,0:T(8,128)(2,1)S(1)} %get-tuple-element.28), channel_id=1, source_target_pairs={{0,1},{1,0},{2,3},{3,2},{4,5},{5,4},{6,7},{7,6},{8,9},{9,8},{10,11... | collective-permute-start | bytes 1179656 | tf_op jit(solution)/shard_map/ppermute | solution.py:405

commit v10 on v9

--- a/solution.py
+++ b/solution.py
@@ -316,7 +316,7 @@
     return total[0:last, :], number
 
 
-def near_body(recv_ref, out_ref):
+def sum_body(recv_ref, out_ref):
     total, number = whole_total(recv_ref)
     out = in_parts(jnp.concatenate([total, jnp.broadcast_to(number, (8, HD))], axis=0))
     for i in range(out_ref.shape[0]):
@@ -415,14 +415,14 @@
     half = chans // 2
     grad_piece, share, raw = call(
         grad_body,
-        (sds((8, 3 * half + 8, HD), BF16), sds((half, rows_here), F32), sds((rows_here, width // 2), F32)),
+        (sds((n_far, 3 * half + 8, HD), BF16), sds((half, rows_here), F32), sds((rows_here, width // 2), F32)),
         (level_index, both, gap, gen_hidden, gen_t),
         scratch=(pltpu.VMEM((chans, rows_here), F32), pltpu.VMEM((half, 3 * HD), F32)),
         smem=1,
     )
-    near = exchange(grad_piece, NEAR)
-    near = call(near_body, sds((n_far, 3 * half + 8, HD), BF16), (near,))
-    everything = exchange(near, "z_far")
+    far = exchange(grad_piece, "z_far")
+    far = call(sum_body, sds((n_seq // n_far, 3 * half + 8, HD), BF16), (far,))
+    everything = exchange(far, NEAR)
 
     def last(*refs):
         last_body(*refs, entries=tokens * chans)

time: 150 us -> 150 us (level)
  the two profiles are of different devices: /device:TPU:64 before, /device:TPU:2 now
where the time goes in v10:
time: 150 us; the launch traced here: 149 us
  blocking collectives  98 us (65%)
  starting transfers between devices  21.7 us (14%)
  Pallas kernels  14.5 us (10%)
  waiting for transfers between devices  9.94 us (7%)
  local copies, waits for them, and re-layouts  3.52 us (2%)
    all_to_all x6, blocking collectives, exchange(): lax.all_to_all(array, axis, 0, 0, axis_index_groups=groups, tiled=True)  98 us
    pallas_call x11, Pallas kernels, call(): pl.pallas_call(body, out_shape=out_shape, in_specs=[scalars if i < smem e...  14.5 us
    all_to_all x2, starting transfers between devices, exchange(): lax.all_to_all(array, axis, 0, 0, axis_index_groups=groups, tiled=True)  12.1 us
    ppermute x3, starting transfers between devices, on_device(): lax.ppermute(channels, 'mp', [(i, i ^ k) for i in range(n_mp)])  7.59 us
    all_to_all x2, waiting for transfers between devices, exchange(): lax.all_to_all(array, axis, 0, 0, axis_index_groups=groups, tiled=True)  6 us
    unnamed x28, local copies, waits for them, and re-layouts  3.51 us
  transfers between devices with their start and end apart: 6, of which 4 were waited for; matrix products, arithmetic and copies ran while one was open for 0% of the time, Pallas kernels for 5%

profile of v10, /device:TPU:2, one launch (start us, length us, event | category | flops | bytes accessed | tf_op | source)
XLA Modules:
  0.0 149.2 jit_solution(3892410746518880790)
XLA Ops:
  0.6 2.3 %shard_map.130 = (bf16[8,80,128]{2,1,0:T(8,128)(2,1)}, s32[1]{0:T(128)}) custom-call(bf16[64,3072]{1,0:T(8,128)(2,1)} %bitcast.17, f32[3,1,3072]{2,1,0:T(1,128)} %bitcast.25, bf16[3,96,384]{2,1,0:T(8,128)(2,1)} %bitcast.29), custom_call_target="tpu_custom_call" | custom-call | tf_op jit(solution)/shard_map/pallas_call | solution.py:29
  2.9 8.5 %all-to-all-start = ((bf16[8,80,128]{2,1,0:T(8,128)(2,1)}), bf16[8,80,128]{2,1,0:T(8,128)(2,1)S(1)}, u32[]{:S(2)}, u32[]{:S(2)}) async-start(bf16[8,80,128]{2,1,0:T(8,128)(2,1)} %get-tuple-element.22), calls=%async_computation | async-start | bytes 327680 | tf_op jit(solution)/shard_map/all_to_all | solution.py:337
  12.1 0.0 copy-start.13
  12.1 3.9 %shard_map.131 = (f32[128,64]{1,0:T(8,128)}, f32[128,64]{1,0:T(8,128)}, bf16[160,128]{1,0:T(8,128)(2,1)}) custom-call(s32[1]{0:T(128)S(6)} %copy.14.level_ref.refs_0_, s32[1]{0:T(128)} %get-tuple-element.20._, bf16[128,3072]{1,0:T(8,128)(2,1)} %hidden_ref.3, bf16[64,3072]{1,0:T(8,128)(2,1)} %bitcast.22, bf16[64,128]{1,0:T(8,128)(2,1)} %bitcast.31, ...), custom_call_target="tpu_custom_call" | custom-call | tf_op jit(solution)/shard_map/pallas_call | solution.py:29
  16.1 4.5 %all-to-all-done.recv_ref = bf16[8,80,128]{2,1,0:T(8,128)(2,1)S(1)} async-done(((bf16[8,80,128]{2,1,0:T(8,128)(2,1)}), bf16[8,80,128]{2,1,0:T(8,128)(2,1)S(1)}, u32[]{:S(2)}, u32[]{:S(2)}) %all-to-all-start) | async-done | bytes 163872 | tf_op jit(solution)/shard_map/all_to_all | solution.py:337
  20.5 0.8 copy-done.8
  21.3 27.4 %all_to_all.40.recv_ref = bf16[4,192,128]{2,1,0:T(8,128)(2,1)S(1)} all-to-all(bf16[4,192,128]{2,1,0:T(8,128)(2,1)S(1)} %shard_map.132), channel_id=1, replica_groups=mesh['role'=2,'z_far'=4,'z_near'=4,'y_hi'=2,'mp'=8] {'z_far'}, dimensions={0} | all-to-all | bytes 393216 | tf_op jit(solution)/shard_map/all_to_all | solution.py:337
  48.8 0.1 shard_map.133
  48.9 0.0 copy-start.6
  48.9 0.9 copy-done.6
  49.8 15.8 %all_to_all.41.recv_ref = bf16[8,144,128]{2,1,0:T(8,128)(2,1)S(1)} all-to-all(bf16[8,144,128]{2,1,0:T(8,128)(2,1)S(1)} %get-tuple-element.23), channel_id=1, replica_groups=mesh['role'=2,'z_far'=4,'z_near'=4,'y_hi'=2,'mp'=8] {'z_near','y_hi'}, dimensions={0} | all-to-all | bytes 589824 | tf_op jit(solution)/shard_map/all_to_all | solution.py:337
  65.7 3.5 %all-to-all-start.3 = ((bf16[8,384,128]{2,1,0:T(8,128)(2,1)}), bf16[8,384,128]{2,1,0:T(8,128)(2,1)S(1)}, u32[]{:S(2)}, u32[]{:S(2)}) async-start(bf16[8,384,128]{2,1,0:T(8,128)(2,1)} %copy-done.6), calls=%async_computation.3 | async-start | bytes 1572864 | tf_op jit(solution)/shard_map/all_to_all | solution.py:337
  69.2 1.9 %collective-permute-start.2 = (bf16[8,64,128]{2,1,0:T(8,128)(2,1)S(1)}, bf16[8,64,128]{2,1,0:T(8,128)(2,1)S(1)}, u32[]{:S(2)}, u32[]{:S(2)}) collective-permute-start(bf16[8,64,128]{2,1,0:T(8,128)(2,1)S(1)} %slice.4), channel_id=1, source_target_pairs={{0,3},{1,2},{2,1},{3,0},{4,7},{5,6},{6,5},{7,4},{8,11},{9,10},{10,... | collective-permute-start | bytes 393224 | tf_op jit(solution)/shard_map/ppermute | solution.py:380
  71.2 2.4 %collective-permute-start.1 = (bf16[8,64,128]{2,1,0:T(8,128)(2,1)S(1)}, bf16[8,64,128]{2,1,0:T(8,128)(2,1)S(1)}, u32[]{:S(2)}, u32[]{:S(2)}) collective-permute-start(bf16[8,64,128]{2,1,0:T(8,128)(2,1)S(1)} %slice.4), channel_id=1, source_target_pairs={{0,2},{1,3},{2,0},{3,1},{4,6},{5,7},{6,4},{7,5},{8,10},{9,11},{10,... | collective-permute-start | bytes 393224 | tf_op jit(solution)/shard_map/ppermute | solution.py:380
  73.6 3.2 %collective-permute-start = (bf16[8,64,128]{2,1,0:T(8,128)(2,1)S(1)}, bf16[8,64,128]{2,1,0:T(8,128)(2,1)S(1)}, u32[]{:S(2)}, u32[]{:S(2)}) collective-permute-start(bf16[8,64,128]{2,1,0:T(8,128)(2,1)S(1)} %slice.4), channel_id=1, source_target_pairs={{0,1},{1,0},{2,3},{3,2},{4,5},{5,4},{6,7},{7,6},{8,9},{9,8},{10,11... | collective-permute-start | bytes 393224 | tf_op jit(solution)/shard_map/ppermute | solution.py:380
  76.8 0.0 collective-permute-done.2.other3_ref
  76.8 2.2 %collective-permute-done.1.other2_ref = bf16[8,64,128]{2,1,0:T(8,128)(2,1)S(1)} collective-permute-done((bf16[8,64,128]{2,1,0:T(8,128)(2,1)S(1)}, bf16[8,64,128]{2,1,0:T(8,128)(2,1)S(1)}, u32[]{:S(2)}, u32[]{:S(2)}) %collective-permute-start.1) | collective-permute-done | bytes 131104 | tf_op jit(solution)/shard_map/ppermute | solution.py:380
  79.1 0.0 collective-permute-done.other1_ref
  79.1 0.0 copy-done.13
  79.1 0.0 copy-done.9
  79.1 3.9 %shard_map.134.image_ref = f32[7,128,128]{2,1,0:T(8,128)S(1)} custom-call(bf16[160,128]{1,0:T(8,128)(2,1)S(1)} %copy-done.9, bf16[8,144,128]{2,1,0:T(8,128)(2,1)S(1)} %all_to_all.41.recv_ref, bf16[8,64,128]{2,1,0:T(8,128)(2,1)S(1)} %collective-permute-done.other1_ref, bf16[8,64,128]{2,1,0:T(8,128)(2,1)S(1)} %collective-permute-done.1.other2_ref, ...), custom_call_target="tpu_custom_call" | custom-call | tf_op jit(solution)/shard_map/pallas_call | solution.py:29
  83.0 0.0 copy-start.3
  83.0 0.8 copy-done.3
  83.8 1.5 %all-to-all-done.3 = bf16[8,384,128]{2,1,0:T(8,128)(2,1)S(1)} async-done(((bf16[8,384,128]{2,1,0:T(8,128)(2,1)}), bf16[8,384,128]{2,1,0:T(8,128)(2,1)S(1)}, u32[]{:S(2)}, u32[]{:S(2)}) %all-to-all-start.3) | async-done | bytes 786464 | tf_op jit(solution)/shard_map/all_to_all | solution.py:337
  85.3 1.0 copy-done.4
  86.3 1.3 shard_map.135
  87.6 0.0 copy-done.2
  87.7 0.0 copy-start
  87.7 0.0 copy-start.7
  87.7 0.0 copy-start.10
  87.7 0.0 copy-start.12
  87.7 1.0 shard_map.136
  88.7 0.0 copy-start.1
  88.7 0.0 copy-start.5
  88.7 0.0 copy-start.11
  88.7 2.1 %collective-permute-start.3 = (bf16[64,3072]{1,0:T(8,128)(2,1)S(1)}, bf16[64,3072]{1,0:T(8,128)(2,1)S(1)}, u32[]{:S(2)}, u32[]{:S(2)}) collective-permute-start(bf16[64,3072]{1,0:T(8,128)(2,1)S(1)} %get-tuple-element.28), channel_id=1, source_target_pairs={{0,1},{1,0},{2,3},{3,2},{4,5},{5,4},{6,7},{7,6},{8,9},{9,8},{10,11... | collective-permute-start | bytes 1179656 | tf_op jit(solution)/shard_map/ppermute | solution.py:405
  90.8 1.7 %collective-permute-done.3 = bf16[64,3072]{1,0:T(8,128)(2,1)S(1)} collective-permute-done((bf16[64,3072]{1,0:T(8,128)(2,1)S(1)}, bf16[64,3072]{1,0:T(8,128)(2,1)S(1)}, u32[]{:S(2)}, u32[]{:S(2)}) %collective-permute-start.3) | collective-permute-done | bytes 393248 | tf_op jit(solution)/shard_map/ppermute | solution.py:405
  92.4 0.1 add_convert_fusion
  92.5 11.5 %all_to_all.42.parts_ref = bf16[4,16,3072]{2,1,0:T(8,128)(2,1)S(1)} all-to-all(bf16[4,16,3072]{2,1,0:T(8,128)(2,1)S(1)} %bitcast.28), channel_id=1, replica_groups={{0,2,4,6},{1,3,5,7},{8,10,12,14},{9,11,13,15},{16,18,20,22},{17,19,21,2..., dimensions={0} | all-to-all | bytes 786432 | tf_op jit(solution)/shard_map/all_to_all | solution.py:337
  104.1 0.0 copy-done
  104.1 0.0 copy-done.7
  104.1 0.0 copy-done.10
  104.1 0.6 shard_map.137
  104.7 8.7 %all_to_all.43.both_ref = f32[16,8,128]{2,1,0:T(8,128)S(1)} all-to-all(f32[16,8,128]{2,1,0:T(8,128)S(1)} %shard_map.137), channel_id=1, replica_groups=mesh['role'=2,'z_far'=4,'z_near'=4,'y_hi'=2,'mp'=8] {'role','mp'}, dimensions={0} | all-to-all | bytes 131072 | tf_op jit(solution)/shard_map/all_to_all | solution.py:337
  113.5 0.4 shard_map.138
  113.9 20.6 %all_to_all.44.recv_ref = bf16[4,104,128]{2,1,0:T(8,128)(2,1)S(1)} all-to-all(bf16[4,104,128]{2,1,0:T(8,128)(2,1)S(1)} %get-tuple-element.31), channel_id=1, replica_groups=mesh['role'=2,'z_far'=4,'z_near'=4,'y_hi'=2,'mp'=8] {'z_far'}, dimensions={0} | all-to-all | bytes 212992 | tf_op jit(solution)/shard_map/all_to_all | solution.py:337
  134.5 13.8 %all_to_all.45.refs_1_ = bf16[8,104,128]{2,1,0:T(8,128)(2,1)S(1)} all-to-all(bf16[8,104,128]{2,1,0:T(8,128)(2,1)S(1)} %shard_map.139), channel_id=1, replica_groups=mesh['role'=2,'z_far'=4,'z_near'=4,'y_hi'=2,'mp'=8] {'z_near','y_hi'}, dimensions={0} | all-to-all | bytes 425984 | tf_op jit(solution)/shard_map/all_to_all | solution.py:337
  148.3 0.9 shard_map.140
  (11 shorter events, 0.1 us)
Async XLA Ops:
  2.9 17.6 %all-to-all-start = ((bf16[8,80,128]{2,1,0:T(8,128)(2,1)}), bf16[8,80,128]{2,1,0:T(8,128)(2,1)S(1)}, u32[]{:S(2)}, u32[]{:S(2)}) async-start(bf16[8,80,128]{2,1,0:T(8,128)(2,1)} %get-tuple-element.22), calls=%async_computation | async-start | bytes 327680 | tf_op jit(solution)/shard_map/all_to_all | solution.py:337
  12.1 67.0 %copy-start.13 = (f32[1,2,128]{2,1,0:T(2,128)S(1)}, f32[1,2,128]{2,1,0:T(2,128)}, u32[]{:S(2)}) copy-start(f32[1,2,128]{2,1,0:T(2,128)} %param.18) | copy-start | bytes 3076
  20.5 0.8 copy-start.8
  21.3 57.8 %copy-start.9 = (bf16[160,128]{1,0:T(8,128)(2,1)S(1)}, bf16[160,128]{1,0:T(8,128)(2,1)}, u32[]{:S(2)}) copy-start(bf16[160,128]{1,0:T(8,128)(2,1)} %get-tuple-element.21.send_ref) | copy-start | bytes 122884
  48.9 0.9 copy-start.6
  49.8 37.8 %copy-start.2 = (bf16[1,384,3072]{2,1,0:T(8,128)(2,1)S(1)}, bf16[1,384,3072]{2,1,0:T(8,128)(2,1)}, u32[]{:S(2)}) copy-start(bf16[1,384,3072]{2,1,0:T(8,128)(2,1)} %param.20) | copy-start | bytes 7077892
  65.7 19.6 %all-to-all-start.3 = ((bf16[8,384,128]{2,1,0:T(8,128)(2,1)}), bf16[8,384,128]{2,1,0:T(8,128)(2,1)S(1)}, u32[]{:S(2)}, u32[]{:S(2)}) async-start(bf16[8,384,128]{2,1,0:T(8,128)(2,1)} %copy-done.6), calls=%async_computation.3 | async-start | bytes 1572864 | tf_op jit(solution)/shard_map/all_to_all | solution.py:337
  69.2 7.6 %collective-permute-start.2 = (bf16[8,64,128]{2,1,0:T(8,128)(2,1)S(1)}, bf16[8,64,128]{2,1,0:T(8,128)(2,1)S(1)}, u32[]{:S(2)}, u32[]{:S(2)}) collective-permute-start(bf16[8,64,128]{2,1,0:T(8,128)(2,1)S(1)} %slice.4), channel_id=1, source_target_pairs={{0,3},{1,2},{2,1},{3,0},{4,7},{5,6},{6,5},{7,4},{8,11},{9,10},{10,... | collective-permute-start | bytes 393224 | tf_op jit(solution)/shard_map/ppermute | solution.py:380
  71.2 7.9 %collective-permute-start.1 = (bf16[8,64,128]{2,1,0:T(8,128)(2,1)S(1)}, bf16[8,64,128]{2,1,0:T(8,128)(2,1)S(1)}, u32[]{:S(2)}, u32[]{:S(2)}) collective-permute-start(bf16[8,64,128]{2,1,0:T(8,128)(2,1)S(1)} %slice.4), channel_id=1, source_target_pairs={{0,2},{1,3},{2,0},{3,1},{4,6},{5,7},{6,4},{7,5},{8,10},{9,11},{10,... | collective-permute-start | bytes 393224 | tf_op jit(solution)/shard_map/ppermute | solution.py:380
  73.6 5.5 %collective-permute-start = (bf16[8,64,128]{2,1,0:T(8,128)(2,1)S(1)}, bf16[8,64,128]{2,1,0:T(8,128)(2,1)S(1)}, u32[]{:S(2)}, u32[]{:S(2)}) collective-permute-start(bf16[8,64,128]{2,1,0:T(8,128)(2,1)S(1)} %slice.4), channel_id=1, source_target_pairs={{0,1},{1,0},{2,3},{3,2},{4,5},{5,4},{6,7},{7,6},{8,9},{9,8},{10,11... | collective-permute-start | bytes 393224 | tf_op jit(solution)/shard_map/ppermute | solution.py:380
  83.0 0.8 copy-start.3
  85.3 1.0 copy-start.4
  87.7 16.4 %copy-start = (bf16[1,64,3072]{2,1,0:T(8,128)(2,1)S(1)}, bf16[1,64,3072]{2,1,0:T(8,128)(2,1)}, u32[]{:S(2)}) copy-start(bf16[1,64,3072]{2,1,0:T(8,128)(2,1)} %param.15) | copy-start | bytes 1179652
  87.7 16.4 %copy-start.7 = (bf16[1,3072,64]{1,2,0:T(8,128)(2,1)S(1)}, bf16[1,3072,64]{1,2,0:T(8,128)(2,1)}, u32[]{:S(2)}) copy-start(bf16[1,3072,64]{1,2,0:T(8,128)(2,1)} %param.21) | copy-start | bytes 1179652
  87.7 16.4 %copy-start.10 = (f32[1,3,3072]{2,0,1:T(1,128)S(1)}, f32[1,3,3072]{2,0,1:T(1,128)}, u32[]{:S(2)}) copy-start(f32[1,3,3072]{2,0,1:T(1,128)} %param.16) | copy-start | bytes 110596
  87.7 16.4 %copy-start.12 = (f32[128,64]{1,0:T(8,128)S(1)}, f32[128,64]{1,0:T(8,128)}, u32[]{:S(2)}) copy-start(f32[128,64]{1,0:T(8,128)} %get-tuple-element.29.noised_ref) | copy-start | bytes 98308
  88.7 24.8 %copy-start.1 = (bf16[128,3072]{1,0:T(8,128)(2,1)S(1)}, bf16[128,3072]{1,0:T(8,128)(2,1)}, u32[]{:S(2)}) copy-start(bf16[128,3072]{1,0:T(8,128)(2,1)} %hidden_ref.3) | copy-start | bytes 2359300
  88.7 24.8 %copy-start.5 = (bf16[3072,64]{0,1:T(8,128)(2,1)S(1)}, bf16[3072,64]{0,1:T(8,128)(2,1)}, u32[]{:S(2)}) copy-start(bf16[3072,64]{0,1:T(8,128)(2,1)} %param.12) | copy-start | bytes 1179652
  88.7 24.8 %copy-start.11 = (f32[128,64]{1,0:T(8,128)S(1)}, f32[128,64]{1,0:T(8,128)}, u32[]{:S(2)}) copy-start(f32[128,64]{1,0:T(8,128)} %get-tuple-element.30.gap_ref) | copy-start | bytes 98308
  88.7 3.7 %collective-permute-start.3 = (bf16[64,3072]{1,0:T(8,128)(2,1)S(1)}, bf16[64,3072]{1,0:T(8,128)(2,1)S(1)}, u32[]{:S(2)}, u32[]{:S(2)}) collective-permute-start(bf16[64,3072]{1,0:T(8,128)(2,1)S(1)} %get-tuple-element.28), channel_id=1, source_target_pairs={{0,1},{1,0},{2,3},{3,2},{4,5},{5,4},{6,7},{7,6},{8,9},{9,8},{10,11... | collective-permute-start | bytes 1179656 | tf_op jit(solution)/shard_map/ppermute | solution.py:405
